TPU v7x, 256 devices: a whole 4x4x8 slice. The times are simulated.
256 devices in a mesh: dom: 32 (over z, x), coarse: 8 (over y, core).
Axes of the slice: x: 4, y: 4, z: 8, core: 2. Of those that a mesh axis runs over, the one named last changes fastest.
Arguments:
- pressure_residual: float32 [8, 8, 8, 32, 8, 128], P(None, None, None, 'dom', 'coarse'), may hold values from -6 to 6
- margin_weight: float32 [8, 8, 8, 32, 8, 128], P(None, None, None, 'dom', 'coarse'), may hold values from 0.1 to 1.9
- stiffness_diag: float32 [8, 8, 8, 32, 8, 128], P(None, None, None, 'dom', 'coarse'), may hold values from 0.5 to 4
- fdm_basis: float32 [3, 10, 10, 32, 8, 128], P(None, None, None, 'dom', 'coarse'), may hold values from -2 to 2
- fdm_eigen: float32 [3, 10, 32, 8, 128], P(None, None, 'dom', 'coarse'), may hold values from 0.3 to 30
- coarse_map: int32 [32, 8, 128], P('dom', 'coarse'), may hold values from 0 to 127
- factor_own: float32 [32, 8, 128, 128], P('dom', 'coarse'), may hold values from -0.5 to 0.5
- factor_group: float32 [32, 8, 128, 256], P('dom', 'coarse'), may hold values from -0.125 to 0.125
- factor_top: float32 [32, 8, 128, 512], P('dom', 'coarse'), may hold values from -0.0625 to 0.0625
Outputs:
- preconditioned: float32 [8, 8, 8, 32, 8, 128], P(None, None, None, 'dom', 'coarse')
All inputs are finite; a program needn't handle non-finite values.
Results may differ from a plain program's by a relative error of at most 0.000059.
Values sent between devices are 32-bit elements; how exact they have to be, the bound alone decides.
No kernel may reach another device: no remote copies, remote signals or barrier semaphores. Data moves between devices by JAX's collectives and lax.ppermute only.
A program may use at most 64 MiB of HBM per device.

v0:
```python
import jax
import jax.numpy as jnp
from jax import lax
from jax.sharding import PartitionSpec as P

sum_scale = 0.015625


def with_halo(array, sides, width, wrap):
    for axis, dim in sides:
        size, length = (lax.axis_size(axis), array.shape[dim])
        up = [(i, (i + 1) % size) for i in range(size if wrap else size - 1)]
        down = [(j, i) for i, j in up]
        last = lax.slice_in_dim(array, length - width, length, axis=dim)
        leading = lax.slice_in_dim(array, 0, width, axis=dim)
        before = lax.ppermute(last, axis, up)
        after = lax.ppermute(leading, axis, down)
        array = jnp.concatenate([before, array, after], axis=dim)
    return array


def assemble(weighted, z_low, z_high, x_low, x_high, y_low, y_high):
    points = weighted.shape[0] + 2
    extended = jnp.zeros((points, points, points) + weighted.shape[3:], jnp.float32)
    extended = extended.at[1:-1, 1:-1, 1:-1].set(weighted)
    extended = extended.at[0, 1:-1, 1:-1].set(z_low).at[-1, 1:-1, 1:-1].set(z_high)
    extended = extended.at[1:-1, 0, 1:-1].set(x_low).at[1:-1, -1, 1:-1].set(x_high)
    extended = extended.at[1:-1, 1:-1, 0].set(y_low).at[1:-1, 1:-1, -1].set(y_high)
    return extended


def contract(basis_one, source, axis, forward):
    total = None
    others = tuple((dim for dim in range(3) if dim != axis))
    for index in range(source.shape[axis]):
        if forward:
            coef = basis_one[index]
        else:
            coef = basis_one[:, index]
        coef = jnp.expand_dims(coef, others)
        piece = lax.slice_in_dim(source, index, index + 1, axis=axis)
        term = coef * piece
        total = term if total is None else total + term
    return total


def fdm_solve(extended, basis, eigen):
    temp = contract(basis[0], extended, 0, True)
    temp = contract(basis[1], temp, 1, True)
    temp = contract(basis[2], temp, 2, True)
    denom = eigen[0][:, None, None] + eigen[1][None, :, None] + eigen[2][None, None, :]
    temp = temp / denom
    temp = contract(basis[0], temp, 0, False)
    temp = contract(basis[1], temp, 1, False)
    return contract(basis[2], temp, 2, False)


def schwarz_pass(field, margin_weight, fdm_basis, fdm_eigen):
    weighted = margin_weight * field
    z_faces = jnp.stack([weighted[0, :, :, 0], weighted[-1, :, :, -1]])
    z_halo = with_halo(z_faces, (("dom", 0),), 1, True)
    x_faces = jnp.stack([weighted[:, 0, :, :, 0], weighted[:, -1, :, :, -1]])
    x_halo = with_halo(x_faces, (("coarse", 0),), 1, False)
    z_low_rest = weighted[-1, :, :, :-1]
    z_high_rest = weighted[0, :, :, 1:]
    x_low_rest = weighted[:, -1, :, :, :-1]
    x_high_rest = weighted[:, 0, :, :, 1:]
    y_low = jnp.roll(weighted[:, :, -1], 1, axis=4)
    y_high = jnp.roll(weighted[:, :, 0], -1, axis=4)
    z_low_recv = z_halo[0][:, :, None]
    z_high_recv = z_halo[3][:, :, None]
    x_low_recv = x_halo[0][:, :, :, None]
    x_high_recv = x_halo[3][:, :, :, None]
    extended = assemble(
        weighted,
        jnp.concatenate([z_low_recv, z_low_rest], axis=2),
        jnp.concatenate([z_high_rest, z_high_recv], axis=2),
        jnp.concatenate([x_low_recv, x_low_rest], axis=3),
        jnp.concatenate([x_high_rest, x_high_recv], axis=3),
        y_low,
        y_high,
    )
    solved = fdm_solve(extended, fdm_basis, fdm_eigen)
    result = solved[1:-1, 1:-1, 1:-1]
    z_back = jnp.stack([solved[0, 1:-1, 1:-1, 0], solved[-1, 1:-1, 1:-1, -1]])
    z_recv = with_halo(z_back, (("dom", 0),), 1, True)
    result = result.at[-1].add(
        jnp.concatenate([solved[0, 1:-1, 1:-1, 1:], z_recv[3][:, :, None]], axis=2)
    )
    result = result.at[0].add(
        jnp.concatenate([z_recv[0][:, :, None], solved[-1, 1:-1, 1:-1, :-1]], axis=2)
    )
    x_back = jnp.stack([solved[1:-1, 0, 1:-1, :, 0], solved[1:-1, -1, 1:-1, :, -1]])
    x_recv = with_halo(x_back, (("coarse", 0),), 1, False)
    result = result.at[:, -1].add(
        jnp.concatenate([solved[1:-1, 0, 1:-1, :, 1:], x_recv[3][:, :, :, None]], axis=3)
    )
    result = result.at[:, 0].add(
        jnp.concatenate([x_recv[0][:, :, :, None], solved[1:-1, -1, 1:-1, :, :-1]], axis=3)
    )
    result = result.at[:, :, -1].add(jnp.roll(solved[1:-1, 1:-1, 0], -1, axis=4))
    result = result.at[:, :, 0].add(jnp.roll(solved[1:-1, 1:-1, -1], 1, axis=4))
    return result


def coarse_solve(weighted, coarse_map, factor_own, factor_group, factor_top):
    best = lax.Precision.HIGHEST
    unknowns = factor_own.shape[2]
    element_sum = jnp.sum(weighted, axis=(0, 1, 2)) * sum_scale
    one_hot = (
        coarse_map.reshape(-1)[:, None] == jnp.arange(unknowns, dtype=jnp.int32)[None, :]
    ).astype(jnp.float32)
    coarse_rhs = jnp.dot(element_sum.reshape(1, -1), one_hot, precision=best)[0]
    own_block = factor_own[0, 0]
    group_block = factor_group[0, 0]
    top_block = factor_top[0, 0]
    own_part = jnp.dot(coarse_rhs, own_block, precision=best)
    group_term = jnp.dot(coarse_rhs, group_block, precision=best)
    top_term = jnp.dot(coarse_rhs, top_block, precision=best)
    group_part = lax.psum(group_term, "coarse")
    top_part = lax.psum(top_term, ("dom", "coarse"))
    coarse_sol = jnp.dot(own_block, own_part, precision=best)
    coarse_sol = coarse_sol + jnp.dot(group_block, group_part, precision=best)
    coarse_sol = coarse_sol + jnp.dot(top_block, top_part, precision=best)
    correction = jnp.dot(one_hot, coarse_sol, precision=best)
    return correction.reshape(coarse_map.shape)


def body(
    pressure_residual,
    margin_weight,
    stiffness_diag,
    fdm_basis,
    fdm_eigen,
    coarse_map,
    factor_own,
    factor_group,
    factor_top,
):
    first = schwarz_pass(pressure_residual, margin_weight, fdm_basis, fdm_eigen)
    second = schwarz_pass(
        pressure_residual - stiffness_diag * first, margin_weight, fdm_basis, fdm_eigen
    )
    correction = coarse_solve(
        margin_weight * pressure_residual, coarse_map, factor_own, factor_group, factor_top
    )
    return first + second + correction[None, None, None]


def solution(mesh):
    in_specs = (
        P(None, None, None, "dom", "coarse", None),
        P(None, None, None, "dom", "coarse", None),
        P(None, None, None, "dom", "coarse", None),
        P(None, None, None, "dom", "coarse", None),
        P(None, None, "dom", "coarse", None),
        P("dom", "coarse", None),
        P("dom", "coarse", None, None),
        P("dom", "coarse", None, None),
        P("dom", "coarse", None, None),
    )
    out_specs = P(None, None, None, "dom", "coarse", None)
    return jax.shard_map(body, mesh=mesh, in_specs=in_specs, out_specs=out_specs, check_vma=False)
```

profile of v0, /device:TPU:1, one launch (start us, length us, event | category | flops | bytes accessed | tf_op | source)
XLA Modules:
  0.0 159.3 jit_solution(11652427258223497783)
XLA Ops:
  0.0 1.6 %fusion.25 = (f32[128]{0:T(128)S(1)}, f32[8,8,8,1,1,128]{5,4,3,2,1,0:T(1,128)S(1)}) fusion(f32[8,8,8,1,1,128]{5,4,3,2,1,0:T(1,128)} %param.62, f32[8,8,8,1,1,128]{5,4,3,2,1,0:T(1,128)} %param.61), kind=kLoop, calls=%fused_computation.273 | loop fusion | flops 130944 | bytes 786944 | tf_op jit(solution)/shard_map/reduce_sum | solution.py:109
  1.7 2.1 %collective-permute-start = (f32[1,8,8,1,128]{4,2,1,3,0:T(8,128)S(1)}, f32[1,8,8,1,128]{4,2,1,3,0:T(8,128)S(1)}, u32[]{:S(2)}, u32[]{:S(2)}) collective-permute-start(f32[1,8,8,1,128]{4,2,1,3,0:T(8,128)S(1)} %bitcast.583), channel_id=1, source_target_pairs={{0,8},{8,16},{16,24},{24,32},{32,40},{40,48},{48,56},{56,64},{64,7... | collective-permute-start | bytes 98312 | tf_op jit(solution)/shard_map/ppermute | solution.py:16
  3.8 6.6 %collective-permute-start.1 = (f32[1,8,8,1,128]{4,2,1,3,0:T(8,128)S(1)}, f32[1,8,8,1,128]{4,2,1,3,0:T(8,128)S(1)}, u32[]{:S(2)}, u32[]{:S(2)}) collective-permute-start(f32[1,8,8,1,128]{4,2,1,3,0:T(8,128)S(1)} %bitcast.581), channel_id=1, source_target_pairs={{8,0},{16,8},{24,16},{32,24},{40,32},{48,40},{56,48},{64,56},{72,6... | collective-permute-start | bytes 98312 | tf_op jit(solution)/shard_map/ppermute | solution.py:17
  10.4 4.0 %collective-permute-start.2 = (f32[1,8,8,1,128]{4,2,1,3,0:T(8,128)S(1)}, f32[1,8,8,1,128]{4,2,1,3,0:T(8,128)S(1)}, u32[]{:S(2)}, u32[]{:S(2)}) collective-permute-start(f32[1,8,8,1,128]{4,2,1,3,0:T(8,128)S(1)} %bitcast.582), channel_id=1, source_target_pairs={{0,1},{1,2},{2,3},{3,4},{4,5},{5,6},{6,7},{8,9},{9,10},{10,11},{11... | collective-permute-start | bytes 98312 | tf_op jit(solution)/shard_map/ppermute | solution.py:16
  14.5 1.9 %collective-permute-start.3 = (f32[1,8,8,1,128]{4,2,1,3,0:T(8,128)S(1)}, f32[1,8,8,1,128]{4,2,1,3,0:T(8,128)S(1)}, u32[]{:S(2)}, u32[]{:S(2)}) collective-permute-start(f32[1,8,8,1,128]{4,2,1,3,0:T(8,128)S(1)} %bitcast.580), channel_id=1, source_target_pairs={{1,0},{2,1},{3,2},{4,3},{5,4},{6,5},{7,6},{9,8},{10,9},{11,10},{12... | collective-permute-start | bytes 98312 | tf_op jit(solution)/shard_map/ppermute | solution.py:17
  16.5 0.7 copy-done.7
  17.4 0.5 copy-done.8
  17.9 0.2 convolution_bitcast_fusion.5
  18.1 0.2 convolution_bitcast_fusion.4
  18.3 0.2 convolution_bitcast_fusion.3
  18.5 0.2 fusion.8
  18.7 12.5 %psum.14 = f32[256]{0:T(256)S(1)} all-reduce(f32[256]{0:T(256)S(1)} %bitcast.593), channel_id=1, replica_groups=mesh['dom'=32,'coarse'=8] {'coarse'}, use_global_device_ids=true, to_apply=%region_1.2 | all-reduce | flops 256 | bytes 2048 | tf_op jit(solution)/shard_map/psum | solution.py:120
  31.2 0.2 fusion.4
  31.4 73.1 %psum.15 = f32[512]{0:T(512)S(1)} all-reduce(f32[512]{0:T(512)S(1)} %bitcast.590), channel_id=1, replica_groups=mesh['dom'=32,'coarse'=8] {'dom','coarse'}, use_global_device_ids=true, to_apply=%region_2.3 | all-reduce | flops 512 | bytes 4096 | tf_op jit(solution)/shard_map/psum | solution.py:121
  104.6 0.3 convolution_bitcast_fusion
  104.8 0.2 fusion.2
  105.1 0.2 convolution_bitcast_fusion.1
  105.3 0.1 slice.2126
  105.4 0.1 slice.2129
  106.0 0.3 scatter.46
  106.7 0.5 multiply_add_fusion.9
  107.3 0.5 multiply_add_fusion.8
  107.9 0.6 add_divide_fusion.1
  108.6 0.6 multiply_add_fusion.7
  109.2 0.5 multiply_add_fusion.6
  109.8 0.6 multiply_add_fusion.5
  110.5 4.1 %collective-permute-start.4 = (f32[1,8,8,1,128]{4,1,2,3,0:T(8,128)S(1)}, f32[1,8,8,1,128]{4,1,2,3,0:T(8,128)S(1)}, u32[]{:S(2)}, u32[]{:S(2)}) collective-permute-start(f32[1,8,8,1,128]{4,1,2,3,0:T(8,128)S(1)} %get-tuple-element.390), channel_id=1, source_target_pairs={{8,0},{16,8},{24,16},{32,24},{40,32},{48,40},{56,48},{64,56},{72,6... | collective-permute-start | bytes 98312 | tf_op jit(solution)/shard_map/ppermute | solution.py:17
  114.6 2.9 %collective-permute-start.6 = (f32[1,8,8,1,128]{4,1,2,3,0:T(8,128)S(1)}, f32[1,8,8,1,128]{4,1,2,3,0:T(8,128)S(1)}, u32[]{:S(2)}, u32[]{:S(2)}) collective-permute-start(f32[1,8,8,1,128]{4,1,2,3,0:T(8,128)S(1)} %bitcast.589), channel_id=1, source_target_pairs={{1,0},{2,1},{3,2},{4,3},{5,4},{6,5},{7,6},{9,8},{10,9},{11,10},{12... | collective-permute-start | bytes 98312 | tf_op jit(solution)/shard_map/ppermute | solution.py:17
  117.5 2.7 %collective-permute-start.7 = (f32[1,8,8,1,128]{4,1,2,3,0:T(8,128)S(1)}, f32[1,8,8,1,128]{4,1,2,3,0:T(8,128)S(1)}, u32[]{:S(2)}, u32[]{:S(2)}) collective-permute-start(f32[1,8,8,1,128]{4,1,2,3,0:T(8,128)S(1)} %bitcast.586), channel_id=1, source_target_pairs={{0,1},{1,2},{2,3},{3,4},{4,5},{5,6},{6,7},{8,9},{9,10},{10,11},{11... | collective-permute-start | bytes 98312 | tf_op jit(solution)/shard_map/ppermute | solution.py:16
  120.4 6.5 %collective-permute-done.5 = f32[1,8,8,1,128]{4,1,2,3,0:T(8,128)S(1)} collective-permute-done((f32[1,8,8,1,128]{4,1,2,3,0:T(8,128)S(1)}, f32[1,8,8,1,128]{4,1,2,3,0:T(8,128)S(1)}, u32[]{:S(2)}, u32[]{:S(2)}) %collective-permute-start.5) | collective-permute-done | bytes 32800 | tf_op jit(solution)/shard_map/ppermute | solution.py:16
  127.0 0.1 scatter-add.44
  127.2 0.1 scatter-add.45
  127.3 0.1 fusion.16
  127.5 0.4 copy-done.2
  127.9 0.1 copy-done.1
  128.0 0.1 copy_multiply_fusion
  128.2 2.6 %collective-permute-start.10 = (f32[1,8,8,1,128]{4,1,2,3,0:T(8,128)S(1)}, f32[1,8,8,1,128]{4,1,2,3,0:T(8,128)S(1)}, u32[]{:S(2)}, u32[]{:S(2)}) collective-permute-start(f32[1,8,8,1,128]{4,1,2,3,0:T(8,128)S(1)} %bitcast.587), channel_id=1, source_target_pairs={{0,1},{1,2},{2,3},{3,4},{4,5},{5,6},{6,7},{8,9},{9,10},{10,11},{11... | collective-permute-start | bytes 98312 | tf_op jit(solution)/shard_map/ppermute | solution.py:16
  130.8 1.9 %collective-permute-start.11 = (f32[1,8,8,1,128]{4,1,2,3,0:T(8,128)S(1)}, f32[1,8,8,1,128]{4,1,2,3,0:T(8,128)S(1)}, u32[]{:S(2)}, u32[]{:S(2)}) collective-permute-start(f32[1,8,8,1,128]{4,1,2,3,0:T(8,128)S(1)} %bitcast.584), channel_id=1, source_target_pairs={{1,0},{2,1},{3,2},{4,3},{5,4},{6,5},{7,6},{9,8},{10,9},{11,10},{12... | collective-permute-start | bytes 98312 | tf_op jit(solution)/shard_map/ppermute | solution.py:17
  132.7 0.3 collective-permute-start.9
  133.0 1.5 collective-permute-start.8
  134.6 0.1 maximum_bitcast_fusion.3
  134.7 0.1 maximum_bitcast_fusion.2
  134.8 4.3 %collective-permute-done.8 = f32[1,8,8,1,128]{4,1,2,3,0:T(8,128)S(1)} collective-permute-done((f32[1,8,8,1,128]{4,1,2,3,0:T(8,128)S(1)}, f32[1,8,8,1,128]{4,1,2,3,0:T(8,128)S(1)}, u32[]{:S(2)}, u32[]{:S(2)}) %collective-permute-start.8) | collective-permute-done | bytes 32800 | tf_op jit(solution)/shard_map/ppermute | solution.py:16
  139.2 0.1 scatter.60
  139.3 0.1 scatter.61
  139.5 0.2 scatter.64
  139.6 0.2 scatter.65
  139.8 0.1 scatter.66
  139.9 0.1 scatter.69
  140.4 0.5 multiply_add_fusion.4
  141.0 0.5 multiply_add_fusion.3
  141.6 0.6 add_divide_fusion
  142.3 0.5 multiply_add_fusion.2
  143.0 0.5 multiply_add_fusion.1
  143.6 0.6 multiply_add_fusion
  144.5 2.2 %collective-permute-start.14 = (f32[1,8,8,1,128]{4,1,2,3,0:T(8,128)S(1)}, f32[1,8,8,1,128]{4,1,2,3,0:T(8,128)S(1)}, u32[]{:S(2)}, u32[]{:S(2)}) collective-permute-start(f32[1,8,8,1,128]{4,1,2,3,0:T(8,128)S(1)} %bitcast.588), channel_id=1, source_target_pairs={{1,0},{2,1},{3,2},{4,3},{5,4},{6,5},{7,6},{9,8},{10,9},{11,10},{12... | collective-permute-start | bytes 98312 | tf_op jit(solution)/shard_map/ppermute | solution.py:17
  146.7 4.5 %collective-permute-start.15 = (f32[1,8,8,1,128]{4,1,2,3,0:T(8,128)S(1)}, f32[1,8,8,1,128]{4,1,2,3,0:T(8,128)S(1)}, u32[]{:S(2)}, u32[]{:S(2)}) collective-permute-start(f32[1,8,8,1,128]{4,1,2,3,0:T(8,128)S(1)} %bitcast.585), channel_id=1, source_target_pairs={{0,1},{1,2},{2,3},{3,4},{4,5},{5,6},{6,7},{8,9},{9,10},{10,11},{11... | collective-permute-start | bytes 98312 | tf_op jit(solution)/shard_map/ppermute | solution.py:16
  151.3 1.8 %collective-permute-start.13 = (f32[1,8,8,1,128]{4,1,2,3,0:T(8,128)S(1)}, f32[1,8,8,1,128]{4,1,2,3,0:T(8,128)S(1)}, u32[]{:S(2)}, u32[]{:S(2)}) collective-permute-start(f32[1,8,8,1,128]{4,1,2,3,0:T(8,128)S(1)} %get-tuple-element.323), channel_id=1, source_target_pairs={{0,8},{8,16},{16,24},{24,32},{32,40},{40,48},{48,56},{56,64},{64,7... | collective-permute-start | bytes 98312 | tf_op jit(solution)/shard_map/ppermute | solution.py:16
  153.0 4.3 %collective-permute-done.13 = f32[1,8,8,1,128]{4,1,2,3,0:T(8,128)S(1)} collective-permute-done((f32[1,8,8,1,128]{4,1,2,3,0:T(8,128)S(1)}, f32[1,8,8,1,128]{4,1,2,3,0:T(8,128)S(1)}, u32[]{:S(2)}, u32[]{:S(2)}) %collective-permute-start.13) | collective-permute-done | bytes 32800 | tf_op jit(solution)/shard_map/ppermute | solution.py:16
  157.4 0.1 scatter-add.54
  157.6 0.1 scatter-add.55
  157.8 0.1 fusion.12
  157.9 0.3 copy.42
  158.2 1.1 fusion.6
  (138 shorter events, 3.0 us)
Async XLA Ops:
  0.0 31.2 %copy-start = (f32[1,1,128,512]{3,2,1,0:T(8,128)S(1)}, f32[1,1,128,512]{3,2,1,0:T(8,128)}, u32[]{:S(2)}) copy-start(f32[1,1,128,512]{3,2,1,0:T(8,128)} %param.69) | copy-start | bytes 786436
  1.6 14.8 %copy-start.3 = (f32[3,10,10,1,1,128]{5,4,3,2,1,0:T(1,128)S(1)}, f32[3,10,10,1,1,128]{5,4,3,2,1,0:T(1,128)}, u32[]{:S(2)}) copy-start(f32[3,10,10,1,1,128]{5,4,3,2,1,0:T(1,128)} %param.64) | copy-start | bytes 460804
  1.7 104.7 %collective-permute-start = (f32[1,8,8,1,128]{4,2,1,3,0:T(8,128)S(1)}, f32[1,8,8,1,128]{4,2,1,3,0:T(8,128)S(1)}, u32[]{:S(2)}, u32[]{:S(2)}) collective-permute-start(f32[1,8,8,1,128]{4,2,1,3,0:T(8,128)S(1)} %bitcast.583), channel_id=1, source_target_pairs={{0,8},{8,16},{16,24},{24,32},{32,40},{40,48},{48,56},{56,64},{64,7... | collective-permute-start | bytes 98312 | tf_op jit(solution)/shard_map/ppermute | solution.py:16
  3.8 102.6 %collective-permute-start.1 = (f32[1,8,8,1,128]{4,2,1,3,0:T(8,128)S(1)}, f32[1,8,8,1,128]{4,2,1,3,0:T(8,128)S(1)}, u32[]{:S(2)}, u32[]{:S(2)}) collective-permute-start(f32[1,8,8,1,128]{4,2,1,3,0:T(8,128)S(1)} %bitcast.581), channel_id=1, source_target_pairs={{8,0},{16,8},{24,16},{32,24},{40,32},{48,40},{56,48},{64,56},{72,6... | collective-permute-start | bytes 98312 | tf_op jit(solution)/shard_map/ppermute | solution.py:17
  10.4 96.0 %collective-permute-start.2 = (f32[1,8,8,1,128]{4,2,1,3,0:T(8,128)S(1)}, f32[1,8,8,1,128]{4,2,1,3,0:T(8,128)S(1)}, u32[]{:S(2)}, u32[]{:S(2)}) collective-permute-start(f32[1,8,8,1,128]{4,2,1,3,0:T(8,128)S(1)} %bitcast.582), channel_id=1, source_target_pairs={{0,1},{1,2},{2,3},{3,4},{4,5},{5,6},{6,7},{8,9},{9,10},{10,11},{11... | collective-permute-start | bytes 98312 | tf_op jit(solution)/shard_map/ppermute | solution.py:16
  14.5 92.0 %collective-permute-start.3 = (f32[1,8,8,1,128]{4,2,1,3,0:T(8,128)S(1)}, f32[1,8,8,1,128]{4,2,1,3,0:T(8,128)S(1)}, u32[]{:S(2)}, u32[]{:S(2)}) collective-permute-start(f32[1,8,8,1,128]{4,2,1,3,0:T(8,128)S(1)} %bitcast.580), channel_id=1, source_target_pairs={{1,0},{2,1},{3,2},{4,3},{5,4},{6,5},{7,6},{9,8},{10,9},{11,10},{12... | collective-permute-start | bytes 98312 | tf_op jit(solution)/shard_map/ppermute | solution.py:17
  16.5 0.7 copy-start.7
  17.2 0.7 copy-start.8
  17.3 0.8 copy-start.6
  17.3 1.2 copy-start.4
  110.5 9.9 %collective-permute-start.4 = (f32[1,8,8,1,128]{4,1,2,3,0:T(8,128)S(1)}, f32[1,8,8,1,128]{4,1,2,3,0:T(8,128)S(1)}, u32[]{:S(2)}, u32[]{:S(2)}) collective-permute-start(f32[1,8,8,1,128]{4,1,2,3,0:T(8,128)S(1)} %get-tuple-element.390), channel_id=1, source_target_pairs={{8,0},{16,8},{24,16},{32,24},{40,32},{48,40},{56,48},{64,56},{72,6... | collective-permute-start | bytes 98312 | tf_op jit(solution)/shard_map/ppermute | solution.py:17
  114.6 12.3 %collective-permute-start.6 = (f32[1,8,8,1,128]{4,1,2,3,0:T(8,128)S(1)}, f32[1,8,8,1,128]{4,1,2,3,0:T(8,128)S(1)}, u32[]{:S(2)}, u32[]{:S(2)}) collective-permute-start(f32[1,8,8,1,128]{4,1,2,3,0:T(8,128)S(1)} %bitcast.589), channel_id=1, source_target_pairs={{1,0},{2,1},{3,2},{4,3},{5,4},{6,5},{7,6},{9,8},{10,9},{11,10},{12... | collective-permute-start | bytes 98312 | tf_op jit(solution)/shard_map/ppermute | solution.py:17
  117.5 9.7 %collective-permute-start.7 = (f32[1,8,8,1,128]{4,1,2,3,0:T(8,128)S(1)}, f32[1,8,8,1,128]{4,1,2,3,0:T(8,128)S(1)}, u32[]{:S(2)}, u32[]{:S(2)}) collective-permute-start(f32[1,8,8,1,128]{4,1,2,3,0:T(8,128)S(1)} %bitcast.586), channel_id=1, source_target_pairs={{0,1},{1,2},{2,3},{3,4},{4,5},{5,6},{6,7},{8,9},{9,10},{10,11},{11... | collective-permute-start | bytes 98312 | tf_op jit(solution)/shard_map/ppermute | solution.py:16
  120.3 6.6 %collective-permute-start.5 = (f32[1,8,8,1,128]{4,1,2,3,0:T(8,128)S(1)}, f32[1,8,8,1,128]{4,1,2,3,0:T(8,128)S(1)}, u32[]{:S(2)}, u32[]{:S(2)}) collective-permute-start(f32[1,8,8,1,128]{4,1,2,3,0:T(8,128)S(1)} %get-tuple-element.389), channel_id=1, source_target_pairs={{0,8},{8,16},{16,24},{24,32},{32,40},{40,48},{48,56},{56,64},{64,7... | collective-permute-start | bytes 98312 | tf_op jit(solution)/shard_map/ppermute | solution.py:16
  120.4 7.1 %copy-start.5 = (f32[8,8,8,1,1,128]{5,4,3,2,1,0:T(1,128)S(1)}, f32[8,8,8,1,1,128]{5,4,3,2,1,0:T(1,128)}, u32[]{:S(2)}) copy-start(f32[8,8,8,1,1,128]{5,4,3,2,1,0:T(1,128)} %param.63) | copy-start | bytes 786436
  126.9 1.0 copy-start.2
  127.0 1.0 copy-start.1
  128.2 11.3 %collective-permute-start.10 = (f32[1,8,8,1,128]{4,1,2,3,0:T(8,128)S(1)}, f32[1,8,8,1,128]{4,1,2,3,0:T(8,128)S(1)}, u32[]{:S(2)}, u32[]{:S(2)}) collective-permute-start(f32[1,8,8,1,128]{4,1,2,3,0:T(8,128)S(1)} %bitcast.587), channel_id=1, source_target_pairs={{0,1},{1,2},{2,3},{3,4},{4,5},{5,6},{6,7},{8,9},{9,10},{10,11},{11... | collective-permute-start | bytes 98312 | tf_op jit(solution)/shard_map/ppermute | solution.py:16
  130.8 8.8 %collective-permute-start.11 = (f32[1,8,8,1,128]{4,1,2,3,0:T(8,128)S(1)}, f32[1,8,8,1,128]{4,1,2,3,0:T(8,128)S(1)}, u32[]{:S(2)}, u32[]{:S(2)}) collective-permute-start(f32[1,8,8,1,128]{4,1,2,3,0:T(8,128)S(1)} %bitcast.584), channel_id=1, source_target_pairs={{1,0},{2,1},{3,2},{4,3},{5,4},{6,5},{7,6},{9,8},{10,9},{11,10},{12... | collective-permute-start | bytes 98312 | tf_op jit(solution)/shard_map/ppermute | solution.py:17
  132.7 6.6 %collective-permute-start.9 = (f32[1,8,8,1,128]{4,1,2,3,0:T(8,128)S(1)}, f32[1,8,8,1,128]{4,1,2,3,0:T(8,128)S(1)}, u32[]{:S(2)}, u32[]{:S(2)}) collective-permute-start(f32[1,8,8,1,128]{4,1,2,3,0:T(8,128)S(1)} %get-tuple-element.455), channel_id=1, source_target_pairs={{8,0},{16,8},{24,16},{32,24},{40,32},{48,40},{56,48},{64,56},{72,6... | collective-permute-start | bytes 98312 | tf_op jit(solution)/shard_map/ppermute | solution.py:17
  133.0 6.2 %collective-permute-start.8 = (f32[1,8,8,1,128]{4,1,2,3,0:T(8,128)S(1)}, f32[1,8,8,1,128]{4,1,2,3,0:T(8,128)S(1)}, u32[]{:S(2)}, u32[]{:S(2)}) collective-permute-start(f32[1,8,8,1,128]{4,1,2,3,0:T(8,128)S(1)} %get-tuple-element.456), channel_id=1, source_target_pairs={{0,8},{8,16},{16,24},{24,32},{32,40},{40,48},{48,56},{56,64},{64,7... | collective-permute-start | bytes 98312 | tf_op jit(solution)/shard_map/ppermute | solution.py:16
  144.3 8.7 %collective-permute-start.12 = (f32[1,8,8,1,128]{4,1,2,3,0:T(8,128)S(1)}, f32[1,8,8,1,128]{4,1,2,3,0:T(8,128)S(1)}, u32[]{:S(2)}, u32[]{:S(2)}) collective-permute-start(f32[1,8,8,1,128]{4,1,2,3,0:T(8,128)S(1)} %get-tuple-element.324), channel_id=1, source_target_pairs={{8,0},{16,8},{24,16},{32,24},{40,32},{48,40},{56,48},{64,56},{72,6... | collective-permute-start | bytes 98312 | tf_op jit(solution)/shard_map/ppermute | solution.py:17
  144.5 12.9 %collective-permute-start.14 = (f32[1,8,8,1,128]{4,1,2,3,0:T(8,128)S(1)}, f32[1,8,8,1,128]{4,1,2,3,0:T(8,128)S(1)}, u32[]{:S(2)}, u32[]{:S(2)}) collective-permute-start(f32[1,8,8,1,128]{4,1,2,3,0:T(8,128)S(1)} %bitcast.588), channel_id=1, source_target_pairs={{1,0},{2,1},{3,2},{4,3},{5,4},{6,5},{7,6},{9,8},{10,9},{11,10},{12... | collective-permute-start | bytes 98312 | tf_op jit(solution)/shard_map/ppermute | solution.py:17
  146.7 10.9 %collective-permute-start.15 = (f32[1,8,8,1,128]{4,1,2,3,0:T(8,128)S(1)}, f32[1,8,8,1,128]{4,1,2,3,0:T(8,128)S(1)}, u32[]{:S(2)}, u32[]{:S(2)}) collective-permute-start(f32[1,8,8,1,128]{4,1,2,3,0:T(8,128)S(1)} %bitcast.585), channel_id=1, source_target_pairs={{0,1},{1,2},{2,3},{3,4},{4,5},{5,6},{6,7},{8,9},{9,10},{10,11},{11... | collective-permute-start | bytes 98312 | tf_op jit(solution)/shard_map/ppermute | solution.py:16
  151.3 6.1 %collective-permute-start.13 = (f32[1,8,8,1,128]{4,1,2,3,0:T(8,128)S(1)}, f32[1,8,8,1,128]{4,1,2,3,0:T(8,128)S(1)}, u32[]{:S(2)}, u32[]{:S(2)}) collective-permute-start(f32[1,8,8,1,128]{4,1,2,3,0:T(8,128)S(1)} %get-tuple-element.323), channel_id=1, source_target_pairs={{0,8},{8,16},{16,24},{24,32},{32,40},{40,48},{48,56},{56,64},{64,7... | collective-permute-start | bytes 98312 | tf_op jit(solution)/shard_map/ppermute | solution.py:16
where the time goes:
time: 160 us; the launch traced here: 159 us
  blocking collectives  85.6 us (54%)
  starting transfers between devices  39.1 us (24%)
  waiting for transfers between devices  15.2 us (10%)
  other arithmetic  10.4 us (6%)
  local copies, waits for them, and re-layouts  6.14 us (4%)
  matrix products  1.71 us (1%)
    psum x1, blocking collectives, coarse_solve(): top_part = lax.psum(top_term, ('dom', 'coarse'))  73.1 us
    ppermute x8, starting transfers between devices, with_halo(): after = lax.ppermute(leading, axis, down)  20 us
    ppermute x8, starting transfers between devices, with_halo(): before = lax.ppermute(last, axis, up)  19.2 us
    ppermute x8, waiting for transfers between devices, with_halo(): before = lax.ppermute(last, axis, up)  15.2 us
    psum x1, blocking collectives, coarse_solve(): group_part = lax.psum(group_term, 'coarse')  12.5 us
    add x10, other arithmetic, contract(): total = term if total is None else total + term  5.45 us
  transfers between devices with their start and end apart: 16, of which 3 were waited for; matrix products, arithmetic and copies ran while one was open for 3% of the time, Pallas kernels for 0%

commit v1 on v0

--- a/solution.py
+++ b/solution.py
@@ -6,15 +6,56 @@
 sum_scale = 0.015625
 
 
+def swap(length, stride, odd):
+    ring = length // stride
+    pairs = []
+    for low in range(odd, ring, 2):
+        high = (low + 1) % ring
+        pairs += [(low, high), (high, low)]
+    return [(a * stride + r, b * stride + r) for a, b in pairs for r in range(stride)]
+
+
+def within(length, group, odd):
+    pairs = swap(group, 1, odd)
+    return [(base + a, base + b) for base in range(0, length, group) for a, b in pairs]
+
+
+def add_over(value, axis, pairs):
+    return value + lax.ppermute(value, axis, pairs)
+
+
+def sum_coarse(value):
+    size = lax.axis_size("coarse")
+    value = add_over(value, "coarse", within(size, 2, 0))
+    value = add_over(value, "coarse", swap(size, 2, 0))
+    return add_over(value, "coarse", swap(size, 2, 1))
+
+
+def sum_dom(value):
+    size = lax.axis_size("dom")
+    value = add_over(value, "dom", within(size, 4, 0))
+    value = add_over(value, "dom", within(size, 4, 1))
+    even, odd = swap(size, 4, 0), swap(size, 4, 1)
+    value = add_over(value, "dom", even)
+    beside = lax.ppermute(value, "dom", odd)
+    across = lax.ppermute(beside, "dom", even)
+    far = lax.ppermute(across, "dom", odd)
+    return value + beside + across + far
+
+
 def with_halo(array, sides, width, wrap):
     for axis, dim in sides:
         size, length = (lax.axis_size(axis), array.shape[dim])
-        up = [(i, (i + 1) % size) for i in range(size if wrap else size - 1)]
+        up = [(i, (i + 1) % size) for i in range(size)]
         down = [(j, i) for i, j in up]
         last = lax.slice_in_dim(array, length - width, length, axis=dim)
         leading = lax.slice_in_dim(array, 0, width, axis=dim)
         before = lax.ppermute(last, axis, up)
         after = lax.ppermute(leading, axis, down)
+        if not wrap:
+            place = lax.axis_index(axis)
+            before = jnp.where(place == 0, 0.0, before)
+            after = jnp.where(place == size - 1, 0.0, after)
         array = jnp.concatenate([before, array, after], axis=dim)
     return array
 
@@ -117,8 +158,9 @@
     own_part = jnp.dot(coarse_rhs, own_block, precision=best)
     group_term = jnp.dot(coarse_rhs, group_block, precision=best)
     top_term = jnp.dot(coarse_rhs, top_block, precision=best)
-    group_part = lax.psum(group_term, "coarse")
-    top_part = lax.psum(top_term, ("dom", "coarse"))
+    both = sum_coarse(jnp.concatenate([group_term, top_term]).reshape(-1, 128))
+    group_part = both[: group_term.shape[0] // 128].reshape(-1)
+    top_part = sum_dom(both[group_term.shape[0] // 128 :]).reshape(-1)
     coarse_sol = jnp.dot(own_block, own_part, precision=best)
     coarse_sol = coarse_sol + jnp.dot(group_block, group_part, precision=best)
     coarse_sol = coarse_sol + jnp.dot(top_block, top_part, precision=best)

time: 160 us -> 98.7 us (0.62)
  blocking collectives: 85.6 us -> 0 us
  waiting for transfers between devices: 15.2 us -> 29.9 us
  starting transfers between devices: 39.1 us -> 45.7 us
  local copies, waits for them, and re-layouts: 6.14 us -> 9.01 us
    psum x2 -> x0, blocking collectives: 85.6 us -> none  [the longest x1 73.1 us: coarse_solve(): top_part = lax.psum(top_term, ('dom', 'coarse'))]
    ppermute x0 -> x9, waiting for transfers between devices: none -> 17.3 us  [the longest x6 10.6 us: add_over(): return value + lax.ppermute(value, axis, pairs)]
    ppermute x0 -> x9, starting transfers between devices: none -> 11.1 us  [the longest x6 8.54 us: add_over(): return value + lax.ppermute(value, axis, pairs)]
    ppermute x8, starting transfers between devices: 19.2 us -> 9.81 us  [with_halo(): before = lax.ppermute(last, axis, up)]
    ppermute x8, starting transfers between devices: 20 us -> 24.8 us  [with_halo(): after = lax.ppermute(leading, axis, down)]
    ppermute x8, waiting for transfers between devices: 15.2 us -> 12.6 us  [with_halo(): before = lax.ppermute(last, axis, up)]
    add x10 -> x11, other arithmetic: 5.45 us -> 5.81 us  [contract(): total = term if total is None else total + term]
  transfers between devices with their start and end apart: 16 -> 25, of which waited for: 3 -> 11; matrix products, arithmetic and copies ran while one was open for 3% -> 5% of each run, Pallas kernels for 0% -> 0%
where the time goes in v1:
time: 98.7 us; the launch traced here: 98.5 us
  starting transfers between devices  45.7 us (46%)
  waiting for transfers between devices  29.9 us (30%)
  other arithmetic  11.1 us (11%)
  local copies, waits for them, and re-layouts  9.01 us (9%)
  matrix products  1.64 us (2%)
  between operations  1.13 us (1%)
    ppermute x8, starting transfers between devices, with_halo(): after = lax.ppermute(leading, axis, down)  24.8 us
    ppermute x8, waiting for transfers between devices, with_halo(): before = lax.ppermute(last, axis, up)  12.6 us
    ppermute x6, waiting for transfers between devices, add_over(): return value + lax.ppermute(value, axis, pairs)  10.6 us
    ppermute x8, starting transfers between devices, with_halo(): before = lax.ppermute(last, axis, up)  9.81 us
    ppermute x6, starting transfers between devices, add_over(): return value + lax.ppermute(value, axis, pairs)  8.54 us
    add x11, other arithmetic, contract(): total = term if total is None else total + term  5.81 us
    unnamed x74, local copies, waits for them, and re-layouts  3.17 us
    ppermute x1, waiting for transfers between devices, sum_dom(): across = lax.ppermute(beside, 'dom', even)  2.25 us
  transfers between devices with their start and end apart: 25, of which 11 were waited for; matrix products, arithmetic and copies ran while one was open for 5% of the time, Pallas kernels for 0%

profile of v1, /device:TPU:1, one launch (start us, length us, event | category | flops | bytes accessed | tf_op | source)
XLA Modules:
  0.0 98.5 jit_solution(14249377459627184795)
XLA Ops:
  0.0 1.4 %fusion.29 = (f32[128]{0:T(128)S(1)}, f32[8,8,8,1,1,128]{5,0,2,4,3,1:T(8,128)S(1)}) fusion(f32[8,8,8,1,1,128]{5,4,3,2,1,0:T(1,128)} %param.61, f32[8,8,8,1,1,128]{5,4,3,2,1,0:T(1,128)} %param.62), kind=kLoop, calls=%fused_computation.285 | loop fusion | flops 130944 | bytes 786944 | tf_op jit(solution)/shard_map/reduce_sum | solution.py:150
  1.4 0.7 copy-done.9
  2.0 0.2 convolution_bitcast_fusion.5
  2.2 0.2 fusion.10
  2.4 0.3 fusion.4
  2.7 3.3 %collective-permute-start.16 = (f32[6,128]{1,0:T(8,128)S(1)}, f32[6,128]{1,0:T(8,128)S(1)}, u32[]{:S(2)}, u32[]{:S(2)}) collective-permute-start(f32[6,128]{1,0:T(8,128)S(1)} %maximum_bitcast_fusion.7), channel_id=1, source_target_pairs={{0,1},{1,0},{2,3},{3,2},{4,5},{5,4},{6,7},{7,6},{8,9},{9,8},{10,11... | collective-permute-start | bytes 9224 | tf_op jit(solution)/shard_map/ppermute | solution.py:24
  6.2 6.1 %collective-permute-start.1 = (f32[1,8,8,1,128]{4,2,1,3,0:T(8,128)S(1)}, f32[1,8,8,1,128]{4,2,1,3,0:T(8,128)S(1)}, u32[]{:S(2)}, u32[]{:S(2)}) collective-permute-start(f32[1,8,8,1,128]{4,2,1,3,0:T(8,128)S(1)} %bitcast.623), channel_id=1, source_target_pairs={{8,0},{16,8},{24,16},{32,24},{40,32},{48,40},{56,48},{64,56},{72,6... | collective-permute-start | bytes 98312 | tf_op jit(solution)/shard_map/ppermute | solution.py:54
  12.3 0.3 collective-permute-start.3
  12.6 1.4 %collective-permute-start.2 = (f32[1,8,8,1,128]{4,1,2,3,0:T(8,128)S(1)}, f32[1,8,8,1,128]{4,1,2,3,0:T(8,128)S(1)}, u32[]{:S(2)}, u32[]{:S(2)}) collective-permute-start(f32[1,8,8,1,128]{4,1,2,3,0:T(8,128)S(1)} %get-tuple-element.462), channel_id=1, source_target_pairs={{0,1},{1,2},{2,3},{3,4},{4,5},{5,6},{6,7},{7,0},{8,9},{9,10},{10,1... | collective-permute-start | bytes 98312 | tf_op jit(solution)/shard_map/ppermute | solution.py:53
  14.1 0.7 copy-done.8
  15.0 0.8 copy-done.6
  15.8 0.2 convolution_bitcast_fusion.4
  16.2 1.4 %collective-permute-start.17 = (f32[6,128]{1,0:T(8,128)S(1)}, f32[6,128]{1,0:T(8,128)S(1)}, u32[]{:S(2)}, u32[]{:S(2)}) collective-permute-start(f32[6,128]{1,0:T(8,128)S(1)} %fusion.28), channel_id=1, source_target_pairs={{0,2},{1,3},{2,0},{3,1},{4,6},{5,7},{6,4},{7,5},{8,10},{9,11},{10,... | collective-permute-start | bytes 9224 | tf_op jit(solution)/shard_map/ppermute | solution.py:24
  17.6 1.5 %collective-permute-done.17 = f32[6,128]{1,0:T(8,128)S(1)} collective-permute-done((f32[6,128]{1,0:T(8,128)S(1)}, f32[6,128]{1,0:T(8,128)S(1)}, u32[]{:S(2)}, u32[]{:S(2)}) %collective-permute-start.17) | collective-permute-done | bytes 3104 | tf_op jit(solution)/shard_map/ppermute | solution.py:24
  19.1 3.7 %collective-permute-start.18 = (f32[6,128]{1,0:T(8,128)S(1)}, f32[6,128]{1,0:T(8,128)S(1)}, u32[]{:S(2)}, u32[]{:S(2)}) collective-permute-start(f32[6,128]{1,0:T(8,128)S(1)} %fusion.50), channel_id=1, source_target_pairs={{2,4},{3,5},{4,2},{5,3},{6,0},{7,1},{0,6},{1,7},{10,12},{11,13},{1... | collective-permute-start | bytes 9224 | tf_op jit(solution)/shard_map/ppermute | solution.py:24
  22.8 1.0 %collective-permute-done.18 = f32[6,128]{1,0:T(8,128)S(1)} collective-permute-done((f32[6,128]{1,0:T(8,128)S(1)}, f32[6,128]{1,0:T(8,128)S(1)}, u32[]{:S(2)}, u32[]{:S(2)}) %collective-permute-start.18) | collective-permute-done | bytes 3104 | tf_op jit(solution)/shard_map/ppermute | solution.py:24
  24.0 2.4 %collective-permute-done.19 = f32[4,128]{1,0:T(4,128)S(1)} collective-permute-done((f32[4,128]{1,0:T(4,128)S(1)}, f32[4,128]{1,0:T(4,128)S(1)}, u32[]{:S(2)}, u32[]{:S(2)}) %collective-permute-start.19) | collective-permute-done | bytes 2080 | tf_op jit(solution)/shard_map/ppermute | solution.py:24
  26.4 3.6 %collective-permute-done.20 = f32[4,128]{1,0:T(4,128)S(1)} collective-permute-done((f32[4,128]{1,0:T(4,128)S(1)}, f32[4,128]{1,0:T(4,128)S(1)}, u32[]{:S(2)}, u32[]{:S(2)}) %collective-permute-start.20) | collective-permute-done | bytes 2080 | tf_op jit(solution)/shard_map/ppermute | solution.py:24
  30.0 0.2 convolution_bitcast_fusion.3
  30.3 2.1 %collective-permute-done.21 = f32[4,128]{1,0:T(4,128)S(1)} collective-permute-done((f32[4,128]{1,0:T(4,128)S(1)}, f32[4,128]{1,0:T(4,128)S(1)}, u32[]{:S(2)}, u32[]{:S(2)}) %collective-permute-start.21) | collective-permute-done | bytes 2080 | tf_op jit(solution)/shard_map/ppermute | solution.py:24
  32.5 1.3 %collective-permute-start.22 = (f32[4,128]{1,0:T(4,128)S(1)}, f32[4,128]{1,0:T(4,128)S(1)}, u32[]{:S(2)}, u32[]{:S(2)}) collective-permute-start(f32[4,128]{1,0:T(4,128)S(1)} %add.1547), channel_id=1, source_target_pairs={{32,64},{40,72},{48,80},{56,88},{64,32},{72,40},{80,48},{88,56},{9... | collective-permute-start | bytes 6152 | tf_op jit(solution)/shard_map/ppermute | solution.py:40
  33.9 2.2 %collective-permute-done.22 = f32[4,128]{1,0:T(4,128)S(1)} collective-permute-done((f32[4,128]{1,0:T(4,128)S(1)}, f32[4,128]{1,0:T(4,128)S(1)}, u32[]{:S(2)}, u32[]{:S(2)}) %collective-permute-start.22) | collective-permute-done | bytes 2080 | tf_op jit(solution)/shard_map/ppermute | solution.py:40
  36.3 2.2 %collective-permute-done.23 = f32[4,128]{1,0:T(4,128)S(1)} collective-permute-done((f32[4,128]{1,0:T(4,128)S(1)}, f32[4,128]{1,0:T(4,128)S(1)}, u32[]{:S(2)}, u32[]{:S(2)}) %collective-permute-start.23) | collective-permute-done | bytes 2080 | tf_op jit(solution)/shard_map/ppermute | solution.py:41
  38.5 1.3 %collective-permute-start.24 = (f32[4,128]{1,0:T(4,128)S(1)}, f32[4,128]{1,0:T(4,128)S(1)}, u32[]{:S(2)}, u32[]{:S(2)}) collective-permute-start(f32[4,128]{1,0:T(4,128)S(1)} %collective-permute-done.23), channel_id=1, source_target_pairs={{32,64},{40,72},{48,80},{56,88},{64,32},{72,40},{80,48},{88,56},{9... | collective-permute-start | bytes 6152 | tf_op jit(solution)/shard_map/ppermute | solution.py:42
  39.8 0.2 fusion
  40.0 2.2 %collective-permute-done.24 = f32[4,128]{1,0:T(4,128)S(1)} collective-permute-done((f32[4,128]{1,0:T(4,128)S(1)}, f32[4,128]{1,0:T(4,128)S(1)}, u32[]{:S(2)}, u32[]{:S(2)}) %collective-permute-start.24) | collective-permute-done | bytes 2080 | tf_op jit(solution)/shard_map/ppermute | solution.py:42
  42.2 0.2 fusion.2
  42.4 0.3 convolution_bitcast_fusion.1
  42.8 0.2 scatter.49
  43.0 0.3 scatter.50
  43.9 0.3 fusion.34
  44.4 0.5 multiply_add_fusion.9
  45.0 0.5 multiply_add_fusion.8
  45.6 0.6 add_divide_fusion.1
  46.3 0.6 multiply_add_fusion.7
  46.9 0.6 multiply_add_fusion.6
  47.5 0.6 multiply_add_fusion.5
  48.2 1.5 %collective-permute-start.4 = (f32[1,8,8,1,128]{4,2,1,3,0:T(8,128)S(1)}, f32[1,8,8,1,128]{4,2,1,3,0:T(8,128)S(1)}, u32[]{:S(2)}, u32[]{:S(2)}) collective-permute-start(f32[1,8,8,1,128]{4,2,1,3,0:T(8,128)S(1)} %bitcast.619), channel_id=1, source_target_pairs={{8,0},{16,8},{24,16},{32,24},{40,32},{48,40},{56,48},{64,56},{72,6... | collective-permute-start | bytes 98312 | tf_op jit(solution)/shard_map/ppermute | solution.py:54
  49.9 8.0 %collective-permute-start.7 = (f32[1,8,8,1,128]{4,1,2,3,0:T(8,128)S(1)}, f32[1,8,8,1,128]{4,1,2,3,0:T(8,128)S(1)}, u32[]{:S(2)}, u32[]{:S(2)}) collective-permute-start(f32[1,8,8,1,128]{4,1,2,3,0:T(8,128)S(1)} %get-tuple-element.388), channel_id=1, source_target_pairs={{0,1},{1,2},{2,3},{3,4},{4,5},{5,6},{6,7},{7,0},{8,9},{9,10},{10,1... | collective-permute-start | bytes 98312 | tf_op jit(solution)/shard_map/ppermute | solution.py:53
  57.9 1.6 %collective-permute-start.6 = (f32[1,8,8,1,128]{4,1,2,3,0:T(8,128)S(1)}, f32[1,8,8,1,128]{4,1,2,3,0:T(8,128)S(1)}, u32[]{:S(2)}, u32[]{:S(2)}) collective-permute-start(f32[1,8,8,1,128]{4,1,2,3,0:T(8,128)S(1)} %get-tuple-element.389), channel_id=1, source_target_pairs={{1,0},{2,1},{3,2},{4,3},{5,4},{6,5},{7,6},{0,7},{9,8},{10,9},{11,1... | collective-permute-start | bytes 98312 | tf_op jit(solution)/shard_map/ppermute | solution.py:54
  59.5 0.2 collective-permute-start.5
  59.9 5.8 %collective-permute-done.5 = f32[1,8,8,1,128]{4,2,1,3,0:T(8,128)S(1)} collective-permute-done((f32[1,8,8,1,128]{4,2,1,3,0:T(8,128)S(1)}, f32[1,8,8,1,128]{4,2,1,3,0:T(8,128)S(1)}, u32[]{:S(2)}, u32[]{:S(2)}) %collective-permute-start.5) | collective-permute-done | bytes 32800 | tf_op jit(solution)/shard_map/ppermute | solution.py:53
  65.7 0.1 scatter-add.41
  66.1 0.6 copy-done.1
  66.7 0.4 fusion.8
  67.4 4.8 %collective-permute-start.9 = (f32[1,8,8,1,128]{4,2,1,3,0:T(8,128)S(1)}, f32[1,8,8,1,128]{4,2,1,3,0:T(8,128)S(1)}, u32[]{:S(2)}, u32[]{:S(2)}) collective-permute-start(f32[1,8,8,1,128]{4,2,1,3,0:T(8,128)S(1)} %bitcast.627), channel_id=1, source_target_pairs={{8,0},{16,8},{24,16},{32,24},{40,32},{48,40},{56,48},{64,56},{72,6... | collective-permute-start | bytes 98312 | tf_op jit(solution)/shard_map/ppermute | solution.py:54
  72.2 4.7 %collective-permute-start.11 = (f32[1,8,8,1,128]{4,1,2,3,0:T(8,128)S(1)}, f32[1,8,8,1,128]{4,1,2,3,0:T(8,128)S(1)}, u32[]{:S(2)}, u32[]{:S(2)}) collective-permute-start(f32[1,8,8,1,128]{4,1,2,3,0:T(8,128)S(1)} %get-tuple-element.455), channel_id=1, source_target_pairs={{1,0},{2,1},{3,2},{4,3},{5,4},{6,5},{7,6},{0,7},{9,8},{10,9},{11,1... | collective-permute-start | bytes 98312 | tf_op jit(solution)/shard_map/ppermute | solution.py:54
  77.1 1.0 collective-permute-done.10
  78.1 0.2 scatter.60
  78.3 0.4 scatter.61
  79.3 0.3 fusion.32
  79.8 0.5 multiply_add_fusion.4
  80.4 0.5 multiply_add_fusion.3
  81.0 0.6 add_divide_fusion
  81.7 0.5 multiply_add_fusion.2
  82.3 0.6 multiply_add_fusion.1
  83.0 0.5 multiply_add_fusion
  83.5 0.4 copy_add_fusion
  84.3 5.8 %collective-permute-start.14 = (f32[1,8,8,1,128]{4,1,2,3,0:T(8,128)S(1)}, f32[1,8,8,1,128]{4,1,2,3,0:T(8,128)S(1)}, u32[]{:S(2)}, u32[]{:S(2)}) collective-permute-start(f32[1,8,8,1,128]{4,1,2,3,0:T(8,128)S(1)} %bitcast.626), channel_id=1, source_target_pairs={{1,0},{2,1},{3,2},{4,3},{5,4},{6,5},{7,6},{0,7},{9,8},{10,9},{11,1... | collective-permute-start | bytes 98312 | tf_op jit(solution)/shard_map/ppermute | solution.py:54
  90.5 5.9 %collective-permute-done.13 = f32[1,8,8,1,128]{4,2,1,3,0:T(8,128)S(1)} collective-permute-done((f32[1,8,8,1,128]{4,2,1,3,0:T(8,128)S(1)}, f32[1,8,8,1,128]{4,2,1,3,0:T(8,128)S(1)}, u32[]{:S(2)}, u32[]{:S(2)}) %collective-permute-start.13) | collective-permute-done | bytes 32800 | tf_op jit(solution)/shard_map/ppermute | solution.py:53
  96.4 0.1 scatter-add.51
  96.6 0.2 copy.38
  97.1 0.3 copy.40
  97.4 1.1 %fusion.6 = f32[8,8,8,1,1,128]{5,4,3,2,1,0:T(1,128)} fusion(f32[8,8,8,1,1,128]{5,4,3,2,1,0:T(1,128)S(1)} %add_dynamic-update-slice_fusion, f32[8,8,8,1,1,128]{5,0,2,4,3,1:T(8,128)S(1)} %fusion.16, f32[128]{0:T(128)S(1)} %convolution_bitcast_fusion.1), kind=kLoop, calls=%fused_computation.27 | loop fusion | flops 131072 | bytes 786944 | tf_op jit(solution)/shard_map/add | solution.py:189
  (183 shorter events, 5.4 us)
Async XLA Ops:
  0.0 2.4 %copy-start = (f32[1,1,128,512]{3,2,1,0:T(8,128)S(1)}, f32[1,1,128,512]{3,2,1,0:T(8,128)}, u32[]{:S(2)}) copy-start(f32[1,1,128,512]{3,2,1,0:T(8,128)} %param.69) | copy-start | bytes 786436
  0.0 2.2 %copy-start.4 = (f32[1,1,128,256]{3,2,1,0:T(8,128)S(1)}, f32[1,1,128,256]{3,2,1,0:T(8,128)}, u32[]{:S(2)}) copy-start(f32[1,1,128,256]{3,2,1,0:T(8,128)} %param.68) | copy-start | bytes 393220
  1.4 0.7 copy-start.9
  2.7 11.3 %copy-start.3 = (f32[3,10,10,1,1,128]{5,4,3,2,1,0:T(1,128)S(1)}, f32[3,10,10,1,1,128]{5,4,3,2,1,0:T(1,128)}, u32[]{:S(2)}) copy-start(f32[3,10,10,1,1,128]{5,4,3,2,1,0:T(1,128)} %param.64) | copy-start | bytes 460804
  2.7 13.5 %collective-permute-start.16 = (f32[6,128]{1,0:T(8,128)S(1)}, f32[6,128]{1,0:T(8,128)S(1)}, u32[]{:S(2)}, u32[]{:S(2)}) collective-permute-start(f32[6,128]{1,0:T(8,128)S(1)} %maximum_bitcast_fusion.7), channel_id=1, source_target_pairs={{0,1},{1,0},{2,3},{3,2},{4,5},{5,4},{6,7},{7,6},{8,9},{9,8},{10,11... | collective-permute-start | bytes 9224 | tf_op jit(solution)/shard_map/ppermute | solution.py:24
  6.1 36.7 %collective-permute-start = (f32[1,8,8,1,128]{4,2,1,3,0:T(8,128)S(1)}, f32[1,8,8,1,128]{4,2,1,3,0:T(8,128)S(1)}, u32[]{:S(2)}, u32[]{:S(2)}) collective-permute-start(f32[1,8,8,1,128]{4,2,1,3,0:T(8,128)S(1)} %bitcast.624), channel_id=1, source_target_pairs={{0,8},{8,16},{16,24},{24,32},{32,40},{40,48},{48,56},{56,64},{64,7... | collective-permute-start | bytes 98312 | tf_op jit(solution)/shard_map/ppermute | solution.py:53
  6.2 36.8 %collective-permute-start.1 = (f32[1,8,8,1,128]{4,2,1,3,0:T(8,128)S(1)}, f32[1,8,8,1,128]{4,2,1,3,0:T(8,128)S(1)}, u32[]{:S(2)}, u32[]{:S(2)}) collective-permute-start(f32[1,8,8,1,128]{4,2,1,3,0:T(8,128)S(1)} %bitcast.623), channel_id=1, source_target_pairs={{8,0},{16,8},{24,16},{32,24},{40,32},{48,40},{56,48},{64,56},{72,6... | collective-permute-start | bytes 98312 | tf_op jit(solution)/shard_map/ppermute | solution.py:54
  12.3 31.2 %collective-permute-start.3 = (f32[1,8,8,1,128]{4,1,2,3,0:T(8,128)S(1)}, f32[1,8,8,1,128]{4,1,2,3,0:T(8,128)S(1)}, u32[]{:S(2)}, u32[]{:S(2)}) collective-permute-start(f32[1,8,8,1,128]{4,1,2,3,0:T(8,128)S(1)} %get-tuple-element.461), channel_id=1, source_target_pairs={{1,0},{2,1},{3,2},{4,3},{5,4},{6,5},{7,6},{0,7},{9,8},{10,9},{11,1... | collective-permute-start | bytes 98312 | tf_op jit(solution)/shard_map/ppermute | solution.py:54
  12.6 30.1 %collective-permute-start.2 = (f32[1,8,8,1,128]{4,1,2,3,0:T(8,128)S(1)}, f32[1,8,8,1,128]{4,1,2,3,0:T(8,128)S(1)}, u32[]{:S(2)}, u32[]{:S(2)}) collective-permute-start(f32[1,8,8,1,128]{4,1,2,3,0:T(8,128)S(1)} %get-tuple-element.462), channel_id=1, source_target_pairs={{0,1},{1,2},{2,3},{3,4},{4,5},{5,6},{6,7},{7,0},{8,9},{9,10},{10,1... | collective-permute-start | bytes 98312 | tf_op jit(solution)/shard_map/ppermute | solution.py:53
  14.1 0.7 copy-start.8
  14.9 0.8 copy-start.6
  16.2 2.8 %collective-permute-start.17 = (f32[6,128]{1,0:T(8,128)S(1)}, f32[6,128]{1,0:T(8,128)S(1)}, u32[]{:S(2)}, u32[]{:S(2)}) collective-permute-start(f32[6,128]{1,0:T(8,128)S(1)} %fusion.28), channel_id=1, source_target_pairs={{0,2},{1,3},{2,0},{3,1},{4,6},{5,7},{6,4},{7,5},{8,10},{9,11},{10,... | collective-permute-start | bytes 9224 | tf_op jit(solution)/shard_map/ppermute | solution.py:24
  19.1 4.7 %collective-permute-start.18 = (f32[6,128]{1,0:T(8,128)S(1)}, f32[6,128]{1,0:T(8,128)S(1)}, u32[]{:S(2)}, u32[]{:S(2)}) collective-permute-start(f32[6,128]{1,0:T(8,128)S(1)} %fusion.50), channel_id=1, source_target_pairs={{2,4},{3,5},{4,2},{5,3},{6,0},{7,1},{0,6},{1,7},{10,12},{11,13},{1... | collective-permute-start | bytes 9224 | tf_op jit(solution)/shard_map/ppermute | solution.py:24
  23.8 12.4 %copy-start.7 = (f32[6,128]{1,0:T(8,128)}, f32[6,128]{1,0:T(8,128)S(1)}, u32[]{:S(2)}) copy-start(f32[6,128]{1,0:T(8,128)S(1)} %add.1543) | copy-start | bytes 9220
  23.8 2.5 %collective-permute-start.19 = (f32[4,128]{1,0:T(4,128)S(1)}, f32[4,128]{1,0:T(4,128)S(1)}, u32[]{:S(2)}, u32[]{:S(2)}) collective-permute-start(f32[4,128]{1,0:T(4,128)S(1)} %slice.2125), channel_id=1, source_target_pairs={{0,8},{8,0},{16,24},{24,16},{32,40},{40,32},{48,56},{56,48},{64,72... | collective-permute-start | bytes 6152 | tf_op jit(solution)/shard_map/ppermute | solution.py:24
  26.4 3.6 %collective-permute-start.20 = (f32[4,128]{1,0:T(4,128)S(1)}, f32[4,128]{1,0:T(4,128)S(1)}, u32[]{:S(2)}, u32[]{:S(2)}) collective-permute-start(f32[4,128]{1,0:T(4,128)S(1)} %slice_add_fusion.7), channel_id=1, source_target_pairs={{8,16},{16,8},{24,0},{0,24},{40,48},{48,40},{56,32},{32,56},{72,80... | collective-permute-start | bytes 6152 | tf_op jit(solution)/shard_map/ppermute | solution.py:24
  30.0 2.4 %collective-permute-start.21 = (f32[4,128]{1,0:T(4,128)S(1)}, f32[4,128]{1,0:T(4,128)S(1)}, u32[]{:S(2)}, u32[]{:S(2)}) collective-permute-start(f32[4,128]{1,0:T(4,128)S(1)} %add.1546), channel_id=1, source_target_pairs={{0,32},{8,40},{16,48},{24,56},{32,0},{40,8},{48,16},{56,24},{64,96... | collective-permute-start | bytes 6152 | tf_op jit(solution)/shard_map/ppermute | solution.py:24
  32.5 3.6 %collective-permute-start.22 = (f32[4,128]{1,0:T(4,128)S(1)}, f32[4,128]{1,0:T(4,128)S(1)}, u32[]{:S(2)}, u32[]{:S(2)}) collective-permute-start(f32[4,128]{1,0:T(4,128)S(1)} %add.1547), channel_id=1, source_target_pairs={{32,64},{40,72},{48,80},{56,88},{64,32},{72,40},{80,48},{88,56},{9... | collective-permute-start | bytes 6152 | tf_op jit(solution)/shard_map/ppermute | solution.py:40
  36.1 2.4 %collective-permute-start.23 = (f32[4,128]{1,0:T(4,128)S(1)}, f32[4,128]{1,0:T(4,128)S(1)}, u32[]{:S(2)}, u32[]{:S(2)}) collective-permute-start(f32[4,128]{1,0:T(4,128)S(1)} %collective-permute-done.22), channel_id=1, source_target_pairs={{0,32},{8,40},{16,48},{24,56},{32,0},{40,8},{48,16},{56,24},{64,96... | collective-permute-start | bytes 6152 | tf_op jit(solution)/shard_map/ppermute | solution.py:41
  36.3 3.6 %slice-start = ((f32[6,128]{1,0:T(8,128)}), f32[2,128]{1,0:T(2,128)S(1)}, s32[]{:S(2)}) async-start(f32[6,128]{1,0:T(8,128)} %copy-done.7), calls=%async_computation | async-start | bytes 2048 | tf_op jit(solution)/shard_map/slice | solution.py:162
  38.5 3.6 %collective-permute-start.24 = (f32[4,128]{1,0:T(4,128)S(1)}, f32[4,128]{1,0:T(4,128)S(1)}, u32[]{:S(2)}, u32[]{:S(2)}) collective-permute-start(f32[4,128]{1,0:T(4,128)S(1)} %collective-permute-done.23), channel_id=1, source_target_pairs={{32,64},{40,72},{48,80},{56,88},{64,32},{72,40},{80,48},{88,56},{9... | collective-permute-start | bytes 6152 | tf_op jit(solution)/shard_map/ppermute | solution.py:42
  48.2 11.5 %collective-permute-start.4 = (f32[1,8,8,1,128]{4,2,1,3,0:T(8,128)S(1)}, f32[1,8,8,1,128]{4,2,1,3,0:T(8,128)S(1)}, u32[]{:S(2)}, u32[]{:S(2)}) collective-permute-start(f32[1,8,8,1,128]{4,2,1,3,0:T(8,128)S(1)} %bitcast.619), channel_id=1, source_target_pairs={{8,0},{16,8},{24,16},{32,24},{40,32},{48,40},{56,48},{64,56},{72,6... | collective-permute-start | bytes 98312 | tf_op jit(solution)/shard_map/ppermute | solution.py:54
  49.9 16.0 %collective-permute-start.7 = (f32[1,8,8,1,128]{4,1,2,3,0:T(8,128)S(1)}, f32[1,8,8,1,128]{4,1,2,3,0:T(8,128)S(1)}, u32[]{:S(2)}, u32[]{:S(2)}) collective-permute-start(f32[1,8,8,1,128]{4,1,2,3,0:T(8,128)S(1)} %get-tuple-element.388), channel_id=1, source_target_pairs={{0,1},{1,2},{2,3},{3,4},{4,5},{5,6},{6,7},{7,0},{8,9},{9,10},{10,1... | collective-permute-start | bytes 98312 | tf_op jit(solution)/shard_map/ppermute | solution.py:53
  57.9 8.0 %collective-permute-start.6 = (f32[1,8,8,1,128]{4,1,2,3,0:T(8,128)S(1)}, f32[1,8,8,1,128]{4,1,2,3,0:T(8,128)S(1)}, u32[]{:S(2)}, u32[]{:S(2)}) collective-permute-start(f32[1,8,8,1,128]{4,1,2,3,0:T(8,128)S(1)} %get-tuple-element.389), channel_id=1, source_target_pairs={{1,0},{2,1},{3,2},{4,3},{5,4},{6,5},{7,6},{0,7},{9,8},{10,9},{11,1... | collective-permute-start | bytes 98312 | tf_op jit(solution)/shard_map/ppermute | solution.py:54
  59.5 6.2 %collective-permute-start.5 = (f32[1,8,8,1,128]{4,2,1,3,0:T(8,128)S(1)}, f32[1,8,8,1,128]{4,2,1,3,0:T(8,128)S(1)}, u32[]{:S(2)}, u32[]{:S(2)}) collective-permute-start(f32[1,8,8,1,128]{4,2,1,3,0:T(8,128)S(1)} %bitcast.622), channel_id=1, source_target_pairs={{0,8},{8,16},{16,24},{24,32},{32,40},{40,48},{48,56},{56,64},{64,7... | collective-permute-start | bytes 98312 | tf_op jit(solution)/shard_map/ppermute | solution.py:53
  59.7 6.4 %copy-start.5 = (f32[8,8,8,1,1,128]{5,4,3,2,1,0:T(1,128)S(1)}, f32[8,8,8,1,1,128]{5,4,3,2,1,0:T(1,128)}, u32[]{:S(2)}) copy-start(f32[8,8,8,1,1,128]{5,4,3,2,1,0:T(1,128)} %param.63) | copy-start | bytes 786436
  65.7 1.0 copy-start.1
  65.7 1.0 %copy-start.2 = (f32[8,8,8,1,1,128]{5,4,3,2,1,0:T(1,128)S(1)}, f32[8,8,8,1,1,128]{5,4,3,2,1,0:T(1,128)}, u32[]{:S(2)}) copy-start(f32[8,8,8,1,1,128]{5,4,3,2,1,0:T(1,128)} %param.62) | copy-start | bytes 786436
  67.4 10.7 %collective-permute-start.8 = (f32[1,8,8,1,128]{4,2,1,3,0:T(8,128)S(1)}, f32[1,8,8,1,128]{4,2,1,3,0:T(8,128)S(1)}, u32[]{:S(2)}, u32[]{:S(2)}) collective-permute-start(f32[1,8,8,1,128]{4,2,1,3,0:T(8,128)S(1)} %bitcast.628), channel_id=1, source_target_pairs={{0,8},{8,16},{16,24},{24,32},{32,40},{40,48},{48,56},{56,64},{64,7... | collective-permute-start | bytes 98312 | tf_op jit(solution)/shard_map/ppermute | solution.py:53
  67.4 10.8 %collective-permute-start.9 = (f32[1,8,8,1,128]{4,2,1,3,0:T(8,128)S(1)}, f32[1,8,8,1,128]{4,2,1,3,0:T(8,128)S(1)}, u32[]{:S(2)}, u32[]{:S(2)}) collective-permute-start(f32[1,8,8,1,128]{4,2,1,3,0:T(8,128)S(1)} %bitcast.627), channel_id=1, source_target_pairs={{8,0},{16,8},{24,16},{32,24},{40,32},{48,40},{56,48},{64,56},{72,6... | collective-permute-start | bytes 98312 | tf_op jit(solution)/shard_map/ppermute | solution.py:54
  72.2 6.6 %collective-permute-start.11 = (f32[1,8,8,1,128]{4,1,2,3,0:T(8,128)S(1)}, f32[1,8,8,1,128]{4,1,2,3,0:T(8,128)S(1)}, u32[]{:S(2)}, u32[]{:S(2)}) collective-permute-start(f32[1,8,8,1,128]{4,1,2,3,0:T(8,128)S(1)} %get-tuple-element.455), channel_id=1, source_target_pairs={{1,0},{2,1},{3,2},{4,3},{5,4},{6,5},{7,6},{0,7},{9,8},{10,9},{11,1... | collective-permute-start | bytes 98312 | tf_op jit(solution)/shard_map/ppermute | solution.py:54
  76.9 1.2 %collective-permute-start.10 = (f32[1,8,8,1,128]{4,1,2,3,0:T(8,128)S(1)}, f32[1,8,8,1,128]{4,1,2,3,0:T(8,128)S(1)}, u32[]{:S(2)}, u32[]{:S(2)}) collective-permute-start(f32[1,8,8,1,128]{4,1,2,3,0:T(8,128)S(1)} %get-tuple-element.456), channel_id=1, source_target_pairs={{0,1},{1,2},{2,3},{3,4},{4,5},{5,6},{6,7},{7,0},{8,9},{9,10},{10,1... | collective-permute-start | bytes 98312 | tf_op jit(solution)/shard_map/ppermute | solution.py:53
  84.1 6.3 %collective-permute-start.12 = (f32[1,8,8,1,128]{4,2,1,3,0:T(8,128)S(1)}, f32[1,8,8,1,128]{4,2,1,3,0:T(8,128)S(1)}, u32[]{:S(2)}, u32[]{:S(2)}) collective-permute-start(f32[1,8,8,1,128]{4,2,1,3,0:T(8,128)S(1)} %bitcast.620), channel_id=1, source_target_pairs={{8,0},{16,8},{24,16},{32,24},{40,32},{48,40},{56,48},{64,56},{72,6... | collective-permute-start | bytes 98312 | tf_op jit(solution)/shard_map/ppermute | solution.py:54
  84.3 12.2 %collective-permute-start.14 = (f32[1,8,8,1,128]{4,1,2,3,0:T(8,128)S(1)}, f32[1,8,8,1,128]{4,1,2,3,0:T(8,128)S(1)}, u32[]{:S(2)}, u32[]{:S(2)}) collective-permute-start(f32[1,8,8,1,128]{4,1,2,3,0:T(8,128)S(1)} %bitcast.626), channel_id=1, source_target_pairs={{1,0},{2,1},{3,2},{4,3},{5,4},{6,5},{7,6},{0,7},{9,8},{10,9},{11,1... | collective-permute-start | bytes 98312 | tf_op jit(solution)/shard_map/ppermute | solution.py:54
  90.2 6.6 %collective-permute-start.15 = (f32[1,8,8,1,128]{4,1,2,3,0:T(8,128)S(1)}, f32[1,8,8,1,128]{4,1,2,3,0:T(8,128)S(1)}, u32[]{:S(2)}, u32[]{:S(2)}) collective-permute-start(f32[1,8,8,1,128]{4,1,2,3,0:T(8,128)S(1)} %bitcast.625), channel_id=1, source_target_pairs={{0,1},{1,2},{2,3},{3,4},{4,5},{5,6},{6,7},{7,0},{8,9},{9,10},{10,1... | collective-permute-start | bytes 98312 | tf_op jit(solution)/shard_map/ppermute | solution.py:53
  90.2 6.2 %collective-permute-start.13 = (f32[1,8,8,1,128]{4,2,1,3,0:T(8,128)S(1)}, f32[1,8,8,1,128]{4,2,1,3,0:T(8,128)S(1)}, u32[]{:S(2)}, u32[]{:S(2)}) collective-permute-start(f32[1,8,8,1,128]{4,2,1,3,0:T(8,128)S(1)} %bitcast.621), channel_id=1, source_target_pairs={{0,8},{8,16},{16,24},{24,32},{32,40},{40,48},{48,56},{56,64},{64,7... | collective-permute-start | bytes 98312 | tf_op jit(solution)/shard_map/ppermute | solution.py:53

commit v2 on v1

v2 whole, which is shorter than its diff:
```python
import jax
import jax.numpy as jnp
from jax import lax
from jax.experimental import pallas as pl
from jax.experimental.pallas import tpu as pltpu
from jax.sharding import PartitionSpec as P

sum_scale = 0.015625
F32 = jnp.float32
FACE = 64
LINK = 144
VMEM = pl.BlockSpec(memory_space=pltpu.VMEM)


def swap(length, stride, odd):
    ring = length // stride
    pairs = []
    for low in range(odd, ring, 2):
        high = (low + 1) % ring
        pairs += [(low, high), (high, low)]
    return [(a * stride + r, b * stride + r) for a, b in pairs for r in range(stride)]


def within(length, group, odd):
    pairs = swap(group, 1, odd)
    return [(base + a, base + b) for base in range(0, length, group) for a, b in pairs]


def call(kernel, out_rows, scratch_rows, *args):
    flops = 2 * 60000 * 128 if scratch_rows else 200000
    return pl.pallas_call(
        kernel,
        out_shape=[jax.ShapeDtypeStruct((rows, 128), F32) for rows in out_rows],
        in_specs=[pl.BlockSpec(memory_space=pltpu.SMEM) if a.ndim == 1 else VMEM for a in args],
        out_specs=[VMEM] * len(out_rows),
        scratch_shapes=[pltpu.VMEM((rows, 128), F32) for rows in scratch_rows],
        compiler_params=pltpu.CompilerParams(vmem_limit_bytes=8 * 1024 * 1024),
        cost_estimate=pl.CostEstimate(flops=flops, bytes_accessed=1000000, transcendentals=0),
    )(*args)


def rows8(start):
    return pl.ds(pl.multiple_of(start, 8), 8)


def every(start, stride):
    return pl.ds(start, 8, stride=stride)


def weigh(basis, direction, inputs, first_in, outs, forward):
    results = []
    for out in outs:
        total = None
        for at, tiles in enumerate(inputs):
            pair = (first_in + at, out) if forward else (out, first_in + at)
            coef = basis[pl.ds(direction * 100 + pair[0] * 10 + pair[1], 1), :]
            terms = [coef * tile for tile in tiles]
            total = terms if total is None else [a + b for a, b in zip(total, terms)]
        results.append(total)
    return results


def solve(field, z_low, z_high, x_low, x_high, basis, eigen, out, z0, z9, x0, x9, work, plane, ylow, yhigh, zx):
    all_ten = range(10)
    inner = range(1, 9)

    def y_face_in(face, at, turn):
        lines = [[pltpu.roll(field[every(k * 64 + at, 8), :], turn, 1)] for k in range(8)]
        for k, (value,) in enumerate(weigh(basis, 0, lines, 1, all_ten, True)):
            plane[rows8(k * 8), :] = value
        lines = [[plane[every(i, 8), :], plane[every(64 + i, 8), :]] for i in range(8)]
        for i, (value, rest) in enumerate(weigh(basis, 1, lines, 1, all_ten, True)):
            face[every(i, 10), :] = value
            face[every(80 + i, 10), :] = rest

    y_face_in(ylow, 7, 1)
    y_face_in(yhigh, 0, 127)

    def forward_z(step, carry):
        tiles = [step * 2, step * 2 + 1]
        lines = [[z_low[rows8(i * 8), :] for i in tiles]]
        lines += [[field[rows8(k * 64 + i * 8), :] for i in tiles] for k in range(8)]
        lines += [[z_high[rows8(i * 8), :] for i in tiles]]
        for k, values in enumerate(weigh(basis, 0, lines, 0, all_ten, True)):
            for i, value in zip(tiles, values):
                work[rows8((k * 10 + i + 1) * 8), :] = value
        return carry

    lax.fori_loop(0, 4, forward_z, 0)
    lines = [[x_low[rows8(k * 8), :], x_high[rows8(k * 8), :]] for k in range(8)]
    for k, (low, high) in enumerate(weigh(basis, 0, lines, 1, all_ten, True)):
        work[rows8(k * 80), :] = low
        work[rows8(k * 80 + 72), :] = high

    def turn_x(forward):
        def step_x(step, carry):
            ks = [step * 2, step * 2 + 1]
            lines = [[work[rows8(k * 80 + i * 8), :] for k in ks] for i in range(10)]
            for i, values in enumerate(weigh(basis, 1, lines, 0, all_ten, forward)):
                for k, value in zip(ks, values):
                    work[rows8(k * 80 + i * 8), :] = value
            return carry

        lax.fori_loop(0, 5, step_x, 0)

    turn_x(True)
    for k in range(10):
        zx[pl.ds(k * 10, 10), :] = eigen[pl.ds(k, 1), :] + eigen[pl.ds(10, 10), :]

    def step_y(step, carry):
        rows = rows8(step * 8)
        lines = [[ylow[rows, :]]] + [[work[every(step * 64 + j, 8), :]] for j in range(8)] + [[yhigh[rows, :]]]
        spectral = weigh(basis, 2, lines, 0, all_ten, True)
        sums = zx[rows, :]
        spectral = [[value / (sums + eigen[pl.ds(20 + j, 1), :])] for j, (value,) in enumerate(spectral)]
        solved = weigh(basis, 2, spectral, 0, all_ten, False)
        ylow[rows, :] = solved[0][0]
        yhigh[rows, :] = solved[9][0]
        for j in range(8):
            work[every(step * 64 + j, 8), :] = solved[j + 1][0]
        return carry

    lax.fori_loop(0, 13, step_y, 0)
    turn_x(False)

    def back_z(step, carry):
        tiles = [step * 2, step * 2 + 1]
        lines = [[work[rows8((k * 10 + i + 1) * 8), :] for i in tiles] for k in range(10)]
        for k, values in enumerate(weigh(basis, 0, lines, 0, all_ten, False)):
            for i, value in zip(tiles, values):
                if k == 0:
                    z0[rows8(i * 8), :] = value
                elif k == 9:
                    z9[rows8(i * 8), :] = value
                else:
                    out[rows8((k - 1) * 64 + i * 8), :] = value
        return carry

    lax.fori_loop(0, 4, back_z, 0)
    lines = [[work[rows8(k * 80), :], work[rows8(k * 80 + 72), :]] for k in range(10)]
    for k, (low, high) in enumerate(weigh(basis, 0, lines, 0, inner, False)):
        x0[rows8(k * 8), :] = low
        x9[rows8(k * 8), :] = high

    def y_face_out(face, at, turn):
        lines = [[face[every(i, 10), :], face[every(80 + i, 10), :]] for i in range(10)]
        for i, (value, rest) in enumerate(weigh(basis, 1, lines, 0, inner, False)):
            plane[rows8(i * 16), :] = value
            plane[rows8(i * 16 + 8), :] = rest
        lines = [[plane[every(k, 16), :]] for k in range(10)]
        for k, (value,) in enumerate(weigh(basis, 0, lines, 0, inner, False)):
            out[every(k * 64 + at, 8), :] += pltpu.roll(value, turn, 1)

    y_face_out(ylow, 7, 127)
    y_face_out(yhigh, 0, 1)


SOLVE_SCRATCH = (840, 128, 160, 160, 104)


def layer(k):
    return pl.ds(k * 64, 64)


def put_x(ref, base, array, i):
    for k in range(8):
        ref[pl.ds(base + k * 8, 8), :] = array[pl.ds(k * 64 + i * 8, 8), :]


def pick(flag, array, other, start, rows):
    return jnp.where(flag, array[pl.ds(start, rows), :], other[pl.ds(start, rows), :])


def hand_out(flag, up, down, even, odd):
    even[...] = jnp.where(flag, up[...], down[...])
    odd[...] = jnp.where(flag, down[...], up[...])


def pre_kernel(place, residual, margin, diag, w, c2, ze, zo, xe, xo, zu, zd, xu, xd):
    w[...] = margin[...] * residual[...]
    c2[...] = margin[...] * diag[...]
    for base, source in ((0, w), (FACE, c2)):
        zu[pl.ds(base, FACE), :] = source[layer(7), :]
        zd[pl.ds(base, FACE), :] = source[layer(0), :]
        put_x(xu, base, source, 7)
        put_x(xd, base, source, 0)
    hand_out(place[0] == 0, zu, zd, ze, zo)
    hand_out(place[1] == 0, xu, xd, xe, xo)


def coarse_kernel(w, coarse_map, own, group, top, terms, own_part):
    total = w[pl.ds(0, 8), :]
    for at in range(8, 512, 8):
        total = total + w[pl.ds(at, 8), :]
    element_sum = jnp.sum(total, axis=0, keepdims=True) * sum_scale
    hit = lax.broadcasted_iota(jnp.int32, (128, 128), 0) == coarse_map[pl.ds(0, 1), :]
    rhs = jnp.sum(jnp.where(hit, element_sum, 0.0), axis=1, keepdims=True)
    own_part[...] = jnp.zeros((8, 128), F32)
    own_part[pl.ds(0, 1), :] = jnp.sum(own[...] * rhs, axis=0, keepdims=True)
    terms[...] = jnp.zeros((8, 128), F32)
    for at in range(4):
        terms[pl.ds(at, 1), :] = jnp.sum(top[:, at * 128 : (at + 1) * 128] * rhs, axis=0, keepdims=True)
    for at in range(2):
        terms[pl.ds(4 + at, 1), :] = jnp.sum(group[:, at * 128 : (at + 1) * 128] * rhs, axis=0, keepdims=True)


def correct_kernel(total, grouped, own_part, coarse_map, own, group, top, correction):
    sums = own[...] * own_part[pl.ds(0, 1), :]
    for at in range(2):
        sums = sums + group[:, at * 128 : (at + 1) * 128] * grouped[pl.ds(4 + at, 1), :]
    for at in range(4):
        sums = sums + top[:, at * 128 : (at + 1) * 128] * total[pl.ds(at, 1), :]
    sol = jnp.sum(sums, axis=1, keepdims=True)
    hit = lax.broadcasted_iota(jnp.int32, (128, 128), 0) == coarse_map[pl.ds(0, 1), :]
    correction[...] = jnp.zeros((8, 128), F32)
    correction[pl.ds(0, 1), :] = jnp.sum(jnp.where(hit, sol, 0.0), axis=0, keepdims=True)


def first_kernel(place, w, c2, ze, zo, xe, xo, basis, eigen, r, z0, z9, x0, x9, oe, oo, zl, zh, xl, xh, xu, xd, *work):
    z_low = place[0] == 0
    x_low = place[1] == 0
    zh[...] = pick(z_low, ze, zo, 0, FACE)
    zl[...] = pick(z_low, zo, ze, 0, FACE)
    xh[...] = jnp.where(place[3] == 1, pick(x_low, xe, xo, 0, FACE), 0.0)
    xl[...] = jnp.where(place[2] == 1, pick(x_low, xo, xe, 0, FACE), 0.0)
    solve(w, zl, zh, xl, xh, basis, eigen, r, z0, z9, x0, x9, *work)
    for message, face, i in ((xu, x9, 7), (xd, x0, 0)):
        message[pl.ds(0, FACE), :] = face[...]
        for k in range(8):
            here = pl.ds(k * 64 + i * 8, 8)
            message[pl.ds(FACE + k * 8, 8), :] = w[here, :] - c2[here, :] * r[here, :]
        message[pl.ds(128, 8), :] = z9[pl.ds(i * 8, 8), :]
        message[pl.ds(136, 8), :] = z0[pl.ds(i * 8, 8), :]
    hand_out(x_low, xu, xd, oe, oo)


def middle_kernel(place, r, w, c2, z0, z9, xe, xo, r2, ze, zo, zu, zd):
    x_low = place[1] == 0
    above = jnp.where(place[3] == 1, pick(x_low, xe, xo, 0, LINK), 0.0)
    below = jnp.where(place[2] == 1, pick(x_low, xo, xe, 0, LINK), 0.0)
    r2[...] = r[...]
    for k in range(8):
        r2[pl.ds(k * 64 + 56, 8), :] += above[k * 8 : k * 8 + 8]
        r2[pl.ds(k * 64, 8), :] += below[k * 8 : k * 8 + 8]
    for message, face, k, edge in ((zu, z9, 7, 128), (zd, z0, 0, 136)):
        message[pl.ds(0, FACE), :] = face[...]
        message[pl.ds(FACE, FACE), :] = w[layer(k), :] - c2[layer(k), :] * r2[layer(k), :]
        message[pl.ds(128, 8), :] = below[edge : edge + 8]
        message[pl.ds(136, 8), :] = above[edge : edge + 8]
    hand_out(place[0] == 0, zu, zd, ze, zo)


def second_kernel(
    place, r2, w, c2, z0, z9, x0, x9, aze, azo, axe, axo, xe, xo, ze, zo, basis, eigen,
    first, ce, co, de, do, field, out, zl, zh, xl, xh, s0, s9, t0, t9, *work
):
    z_low = place[0] == 0
    x_low = place[1] == 0
    from_up = lambda start, rows: pick(z_low, ze, zo, start, rows)
    from_down = lambda start, rows: pick(z_low, zo, ze, start, rows)
    first[...] = r2[...]
    first[layer(7), :] += from_up(0, FACE)
    first[layer(0), :] += from_down(0, FACE)
    zh[...] = from_up(FACE, FACE) - pick(z_low, aze, azo, FACE, FACE) * z9[...]
    zl[...] = from_down(FACE, FACE) - pick(z_low, azo, aze, FACE, FACE) * z0[...]
    xh[...] = x9[...]
    xl[...] = x0[...]
    xl[pl.ds(0, 8), :] += from_down(128, 8)
    xl[pl.ds(56, 8), :] += from_up(128, 8)
    xh[pl.ds(0, 8), :] += from_down(136, 8)
    xh[pl.ds(56, 8), :] += from_up(136, 8)
    value = pick(x_low, xe, xo, FACE, FACE) - pick(x_low, axe, axo, FACE, FACE) * xh[...]
    xh[...] = jnp.where(place[3] == 1, value, 0.0)
    value = pick(x_low, xo, xe, FACE, FACE) - pick(x_low, axo, axe, FACE, FACE) * xl[...]
    xl[...] = jnp.where(place[2] == 1, value, 0.0)
    field[...] = w[...] - c2[...] * first[...]
    solve(field, zl, zh, xl, xh, basis, eigen, out, s0, s9, t0, t9, *work)
    first[...] += out[...]
    hand_out(z_low, s9, s0, ce, co)
    hand_out(x_low, t9, t0, de, do)


def last_kernel(place, first, ze, zo, xe, xo, correction, out):
    z_low = place[0] == 0
    x_low = place[1] == 0
    out[...] = first[...] + correction[pl.ds(0, 1), :]
    out[layer(7), :] += pick(z_low, ze, zo, 0, FACE)
    out[layer(0), :] += pick(z_low, zo, ze, 0, FACE)
    above = jnp.where(place[3] == 1, pick(x_low, xe, xo, 0, FACE), 0.0)
    below = jnp.where(place[2] == 1, pick(x_low, xo, xe, 0, FACE), 0.0)
    for k in range(8):
        out[pl.ds(k * 64 + 56, 8), :] += above[k * 8 : k * 8 + 8]
        out[pl.ds(k * 64, 8), :] += below[k * 8 : k * 8 + 8]


def add_over(value, axis, pairs):
    return value + lax.ppermute(value, axis, pairs)


def sum_coarse(value):
    size = lax.axis_size("coarse")
    value = add_over(value, "coarse", within(size, 2, 0))
    value = add_over(value, "coarse", swap(size, 2, 0))
    return add_over(value, "coarse", swap(size, 2, 1))


def sum_dom(value):
    size = lax.axis_size("dom")
    value = add_over(value, "dom", within(size, 4, 0))
    value = add_over(value, "dom", within(size, 4, 1))
    even, odd = swap(size, 4, 0), swap(size, 4, 1)
    value = add_over(value, "dom", even)
    beside = lax.ppermute(value, "dom", odd)
    across = lax.ppermute(beside, "dom", even)
    far = lax.ppermute(across, "dom", odd)
    return value + beside + across + far


def over(axis, even, odd):
    size = lax.axis_size(axis)
    even = lax.ppermute(even, axis, swap(size, 1, 0))
    odd = lax.ppermute(odd, axis, swap(size, 1, 1))
    return even, odd


def body(residual, margin, diag, basis, eigen, coarse_map, own, group, top):
    shape = residual.shape
    residual, margin, diag = (a.reshape(-1, 128) for a in (residual, margin, diag))
    basis, eigen, coarse_map = (a.reshape(-1, 128) for a in (basis, eigen, coarse_map))
    own, group, top = (a.reshape(128, -1) for a in (own, group, top))
    dom, coarse = lax.axis_index("dom"), lax.axis_index("coarse")
    last = lax.axis_size("coarse") - 1
    place = jnp.stack([dom % 2, coarse % 2, (coarse > 0).astype(jnp.int32), (coarse < last).astype(jnp.int32)])
    place = place.astype(jnp.int32)

    w, c2, ze, zo, xe, xo = call(pre_kernel, (512, 512) + (128,) * 4, (128,) * 4, place, residual, margin, diag)
    axe, axo = over("coarse", xe, xo)
    aze, azo = over("dom", ze, zo)
    terms, own_part = call(coarse_kernel, (8, 8), (), w, coarse_map, own, group, top)
    grouped = sum_coarse(terms)
    r, z0, z9, x0, x9, xe, xo = call(
        first_kernel, (512,) + (FACE,) * 4 + (LINK,) * 2, (FACE,) * 4 + (LINK,) * 2 + SOLVE_SCRATCH,
        place, w, c2, aze, azo, axe, axo, basis, eigen,
    )
    xe, xo = over("coarse", xe, xo)
    r2, ze, zo = call(middle_kernel, (512, LINK, LINK), (LINK,) * 2, place, r, w, c2, z0, z9, xe, xo)
    ze, zo = over("dom", ze, zo)
    total = sum_dom(grouped)
    first, ce, co, de, do = call(
        second_kernel, (512,) + (FACE,) * 4, (512, 512) + (FACE,) * 8 + SOLVE_SCRATCH,
        place, r2, w, c2, z0, z9, x0, x9, aze, azo, axe, axo, xe, xo, ze, zo, basis, eigen,
    )
    xe, xo = over("coarse", de, do)
    ze, zo = over("dom", ce, co)
    (correction,) = call(correct_kernel, (8,), (), total, grouped, own_part, coarse_map, own, group, top)
    (out,) = call(last_kernel, (512,), (), place, first, ze, zo, xe, xo, correction)
    return out.reshape(shape)


def solution(mesh):
    field = P(None, None, None, "dom", "coarse", None)
    factor = P("dom", "coarse", None, None)
    in_specs = (field, field, field, field, P(None, None, "dom", "coarse", None), P("dom", "coarse", None))
    in_specs = in_specs + (factor, factor, factor)
    return jax.shard_map(body, mesh=mesh, in_specs=in_specs, out_specs=field, check_vma=False)
```

time: 98.7 us -> 73.4 us (0.74)
  starting transfers between devices: 45.7 us -> 31.1 us
  other arithmetic: 11.1 us -> 0.51 us
  Pallas kernels: 0 us -> 8.89 us
  local copies, waits for them, and re-layouts: 9.01 us -> 4.21 us
  matrix products: 1.64 us -> 0 us
  waiting for transfers between devices: 29.9 us -> 28.3 us
    pallas_call x0 -> x7, Pallas kernels: none -> 8.89 us  [call(): pl.pallas_call(kernel, out_shape=[jax.ShapeDtypeStruct((rows, 128), F32)...]
    ppermute x16 -> x12, starting transfers between devices: 34.6 us -> 27.1 us  [the longest x6 13.7 us: over(): even = lax.ppermute(even, axis, swap(size, 1, 0))]
    add x18 -> x0, other arithmetic: 7.07 us -> none  [the longest x11 5.81 us: contract(): total = term if total is None else total + term]
    ppermute x6, starting transfers between devices: 8.54 us -> 3.85 us  [add_over(): return value + lax.ppermute(value, axis, pairs)]
    ppermute x16 -> x12, waiting for transfers between devices: 12.7 us -> 8.88 us  [the longest x6 7.56 us: over(): odd = lax.ppermute(odd, axis, swap(size, 1, 1))]
    ppermute x6, waiting for transfers between devices: 10.6 us -> 13.4 us  [add_over(): return value + lax.ppermute(value, axis, pairs)]
    scatter x14 -> x0, local copies, waits for them, and re-layouts: 2.28 us -> none  [the longest x4 1.02 us: assemble(): extended.at[0, 1:-1, 1:-1].set(z_low).at[-1, 1:-1, 1:-1].set(z_high)]
    ppermute x1, waiting for transfers between devices: 2.18 us -> 0.01 us  [sum_dom(): far = lax.ppermute(across, 'dom', odd)]
  transfers between devices with their start and end apart: 25 -> 21, of which waited for: 11 -> 13; matrix products, arithmetic and copies ran while one was open for 5% -> 1% of each run, Pallas kernels for 0% -> 5%
where the time goes in v2:
time: 73.4 us; the launch traced here: 73.2 us
  starting transfers between devices  31.1 us (42%)
  waiting for transfers between devices  28.3 us (39%)
  Pallas kernels  8.89 us (12%)
  local copies, waits for them, and re-layouts  4.21 us (6%)
    ppermute x6, starting transfers between devices, over(): even = lax.ppermute(even, axis, swap(size, 1, 0))  13.7 us
    ppermute x6, waiting for transfers between devices, add_over(): return value + lax.ppermute(value, axis, pairs)  13.4 us
    ppermute x6, starting transfers between devices, over(): odd = lax.ppermute(odd, axis, swap(size, 1, 1))  13.4 us
    pallas_call x7, Pallas kernels, call(): pl.pallas_call(kernel, out_shape=[jax.ShapeDtypeStruct((rows, 128), F32)...  8.89 us
    ppermute x6, waiting for transfers between devices, over(): odd = lax.ppermute(odd, axis, swap(size, 1, 1))  7.56 us
    unnamed x18, local copies, waits for them, and re-layouts  4.19 us
    ppermute x6, starting transfers between devices, add_over(): return value + lax.ppermute(value, axis, pairs)  3.85 us
    ppermute x1, waiting for transfers between devices, sum_dom(): beside = lax.ppermute(value, 'dom', odd)  3.58 us
  transfers between devices with their start and end apart: 21, of which 13 were waited for; matrix products, arithmetic and copies ran while one was open for 1% of the time, Pallas kernels for 5%

profile of v2, /device:TPU:1, one launch (start us, length us, event | category | flops | bytes accessed | tf_op | source)
XLA Modules:
  0.0 73.2 jit_solution(4969404070405329996)
XLA Ops:
  0.0 0.1 pad_add_fusion.place
  0.1 0.0 copy-start.3
  0.1 0.9 %copy-done.3 = f32[8,8,8,1,1,128]{5,4,3,2,1,0:T(1,128)S(1)} copy-done((f32[8,8,8,1,1,128]{5,4,3,2,1,0:T(1,128)S(1)}, f32[8,8,8,1,1,128]{5,4,3,2,1,0:T(1,128)}, u32[]{:S(2)}) %copy-start.3) | copy-done | bytes 262168
  1.0 0.0 copy-start.4
  1.0 0.9 %copy-done.4 = f32[8,8,8,1,1,128]{5,4,3,2,1,0:T(1,128)S(1)} copy-done((f32[8,8,8,1,1,128]{5,4,3,2,1,0:T(1,128)S(1)}, f32[8,8,8,1,1,128]{5,4,3,2,1,0:T(1,128)}, u32[]{:S(2)}) %copy-start.4) | copy-done | bytes 262168
  2.0 0.0 copy-start.5
  2.0 0.9 %copy-done.5 = f32[8,8,8,1,1,128]{5,4,3,2,1,0:T(1,128)S(1)} copy-done((f32[8,8,8,1,1,128]{5,4,3,2,1,0:T(1,128)S(1)}, f32[8,8,8,1,1,128]{5,4,3,2,1,0:T(1,128)}, u32[]{:S(2)}) %copy-start.5) | copy-done | bytes 262168
  2.9 0.6 shard_map.91
  3.5 2.1 %collective-permute-start = (f32[128,128]{1,0:T(8,128)S(1)}, f32[128,128]{1,0:T(8,128)S(1)}, u32[]{:S(2)}, u32[]{:S(2)}) collective-permute-start(f32[128,128]{1,0:T(8,128)S(1)} %get-tuple-element.30), channel_id=1, source_target_pairs={{0,8},{8,0},{16,24},{24,16},{32,40},{40,32},{48,56},{56,48},{64,72... | collective-permute-start | bytes 196616 | tf_op jit(solution)/shard_map/ppermute | solution.py:321
  5.7 7.1 %collective-permute-start.1 = (f32[128,128]{1,0:T(8,128)S(1)}, f32[128,128]{1,0:T(8,128)S(1)}, u32[]{:S(2)}, u32[]{:S(2)}) collective-permute-start(f32[128,128]{1,0:T(8,128)S(1)} %get-tuple-element.31), channel_id=1, source_target_pairs={{8,16},{16,8},{24,32},{32,24},{40,48},{48,40},{56,64},{64,56},{72,... | collective-permute-start | bytes 196616 | tf_op jit(solution)/shard_map/ppermute | solution.py:322
  12.8 1.2 %collective-permute-start.2 = (f32[128,128]{1,0:T(8,128)S(1)}, f32[128,128]{1,0:T(8,128)S(1)}, u32[]{:S(2)}, u32[]{:S(2)}) collective-permute-start(f32[128,128]{1,0:T(8,128)S(1)} %get-tuple-element.32), channel_id=1, source_target_pairs={{0,1},{1,0},{2,3},{3,2},{4,5},{5,4},{6,7},{7,6},{8,9},{9,8},{10,11... | collective-permute-start | bytes 196616 | tf_op jit(solution)/shard_map/ppermute | solution.py:321
  14.0 1.2 %collective-permute-start.3 = (f32[128,128]{1,0:T(8,128)S(1)}, f32[128,128]{1,0:T(8,128)S(1)}, u32[]{:S(2)}, u32[]{:S(2)}) collective-permute-start(f32[128,128]{1,0:T(8,128)S(1)} %get-tuple-element.33), channel_id=1, source_target_pairs={{1,2},{2,1},{3,4},{4,3},{5,6},{6,5},{7,0},{0,7},{9,10},{10,9},{11,... | collective-permute-start | bytes 196616 | tf_op jit(solution)/shard_map/ppermute | solution.py:322
  15.2 0.0 copy-done.7
  15.2 0.4 reduce
  15.6 0.0 copy-start.8
  15.6 0.7 copy-done.8
  16.4 0.0 collective-permute-done.ze.aze
  16.4 0.0 collective-permute-done.1.zo.azo
  16.4 0.0 collective-permute-done.2.xe.axe
  16.4 1.6 %collective-permute-done.3.xo.axo = f32[128,128]{1,0:T(8,128)S(1)} collective-permute-done((f32[128,128]{1,0:T(8,128)S(1)}, f32[128,128]{1,0:T(8,128)S(1)}, u32[]{:S(2)}, u32[]{:S(2)}) %collective-permute-start.3) | collective-permute-done | bytes 65568 | tf_op jit(solution)/shard_map/ppermute | solution.py:322
  18.0 3.0 %shard_map.92 = (f32[512,128]{1,0:T(8,128)S(1)}, f32[64,128]{1,0:T(8,128)S(1)}, f32[64,128]{1,0:T(8,128)S(1)}, f32[64,128]{1,0:T(8,128)S(1)}, f32[64,128]{1,0:T(...) custom-call(s32[4]{0:T(128)S(1)} %pad_add_fusion.place, f32[512,128]{1,0:T(8,128)S(1)} %get-tuple-element.28.w, ...), custom_call_target="tpu_custom_call" | custom-call | flops 15360000 | bytes 1000000 | tf_op jit(solution)/shard_map/pallas_call | solution.py:31
  21.0 1.2 %collective-permute-start.4 = (f32[144,128]{1,0:T(8,128)S(1)}, f32[144,128]{1,0:T(8,128)S(1)}, u32[]{:S(2)}, u32[]{:S(2)}) collective-permute-start(f32[144,128]{1,0:T(8,128)S(1)} %get-tuple-element.37), channel_id=1, source_target_pairs={{0,1},{1,0},{2,3},{3,2},{4,5},{5,4},{6,7},{7,6},{8,9},{9,8},{10,11... | collective-permute-start | bytes 221192 | tf_op jit(solution)/shard_map/ppermute | solution.py:321
  22.2 0.3 collective-permute-start.5
  22.5 0.6 collective-permute-done.4.xe
  23.1 3.2 %collective-permute-done.5.xo = f32[144,128]{1,0:T(8,128)S(1)} collective-permute-done((f32[144,128]{1,0:T(8,128)S(1)}, f32[144,128]{1,0:T(8,128)S(1)}, u32[]{:S(2)}, u32[]{:S(2)}) %collective-permute-start.5) | collective-permute-done | bytes 73760 | tf_op jit(solution)/shard_map/ppermute | solution.py:322
  26.3 0.6 shard_map.93
  26.9 0.1 collective-permute-start.6
  27.0 2.3 %collective-permute-start.7 = (f32[144,128]{1,0:T(8,128)S(1)}, f32[144,128]{1,0:T(8,128)S(1)}, u32[]{:S(2)}, u32[]{:S(2)}) collective-permute-start(f32[144,128]{1,0:T(8,128)S(1)} %get-tuple-element.43), channel_id=1, source_target_pairs={{8,16},{16,8},{24,32},{32,24},{40,48},{48,40},{56,64},{64,56},{72,... | collective-permute-start | bytes 221192 | tf_op jit(solution)/shard_map/ppermute | solution.py:322
  29.3 0.0 copy-done
  29.3 0.0 copy-done.1
  29.3 0.0 copy-done.2
  29.3 0.6 copy-done.6
  30.0 0.2 shard_map.95
  30.2 1.5 %collective-permute-start.12 = (f32[8,128]{1,0:T(8,128)S(1)}, f32[8,128]{1,0:T(8,128)S(1)}, u32[]{:S(2)}, u32[]{:S(2)}) collective-permute-start(f32[8,128]{1,0:T(8,128)S(1)} %get-tuple-element.49), channel_id=1, source_target_pairs={{0,1},{1,0},{2,3},{3,2},{4,5},{5,4},{6,7},{7,6},{8,9},{9,8},{10,11... | collective-permute-start | bytes 12296 | tf_op jit(solution)/shard_map/ppermute | solution.py:297
  31.6 0.8 %collective-permute-done.12 = f32[8,128]{1,0:T(8,128)S(1)} collective-permute-done((f32[8,128]{1,0:T(8,128)S(1)}, f32[8,128]{1,0:T(8,128)S(1)}, u32[]{:S(2)}, u32[]{:S(2)}) %collective-permute-start.12) | collective-permute-done | bytes 4128 | tf_op jit(solution)/shard_map/ppermute | solution.py:297
  32.4 0.0 collective-permute-start.13
  32.4 2.7 %collective-permute-done.13 = f32[8,128]{1,0:T(8,128)S(1)} collective-permute-done((f32[8,128]{1,0:T(8,128)S(1)}, f32[8,128]{1,0:T(8,128)S(1)}, u32[]{:S(2)}, u32[]{:S(2)}) %collective-permute-start.13) | collective-permute-done | bytes 4128 | tf_op jit(solution)/shard_map/ppermute | solution.py:297
  35.2 2.4 %collective-permute-start.14 = (f32[8,128]{1,0:T(8,128)S(1)}, f32[8,128]{1,0:T(8,128)S(1)}, u32[]{:S(2)}, u32[]{:S(2)}) collective-permute-start(f32[8,128]{1,0:T(8,128)S(1)} %add.37), channel_id=1, source_target_pairs={{2,4},{3,5},{4,2},{5,3},{6,0},{7,1},{0,6},{1,7},{10,12},{11,13},{1... | collective-permute-start | bytes 12296 | tf_op jit(solution)/shard_map/ppermute | solution.py:297
  37.6 1.3 %collective-permute-done.14 = f32[8,128]{1,0:T(8,128)S(1)} collective-permute-done((f32[8,128]{1,0:T(8,128)S(1)}, f32[8,128]{1,0:T(8,128)S(1)}, u32[]{:S(2)}, u32[]{:S(2)}) %collective-permute-start.14) | collective-permute-done | bytes 4128 | tf_op jit(solution)/shard_map/ppermute | solution.py:297
  38.9 0.0 collective-permute-start.15
  38.9 2.5 %collective-permute-done.15 = f32[8,128]{1,0:T(8,128)S(1)} collective-permute-done((f32[8,128]{1,0:T(8,128)S(1)}, f32[8,128]{1,0:T(8,128)S(1)}, u32[]{:S(2)}, u32[]{:S(2)}) %collective-permute-start.15) | collective-permute-done | bytes 4128 | tf_op jit(solution)/shard_map/ppermute | solution.py:297
  41.3 0.0 collective-permute-start.16
  41.3 3.7 %collective-permute-done.16 = f32[8,128]{1,0:T(8,128)S(1)} collective-permute-done((f32[8,128]{1,0:T(8,128)S(1)}, f32[8,128]{1,0:T(8,128)S(1)}, u32[]{:S(2)}, u32[]{:S(2)}) %collective-permute-start.16) | collective-permute-done | bytes 4128 | tf_op jit(solution)/shard_map/ppermute | solution.py:297
  45.0 0.0 collective-permute-start.17
  45.0 2.5 %collective-permute-done.17 = f32[8,128]{1,0:T(8,128)S(1)} collective-permute-done((f32[8,128]{1,0:T(8,128)S(1)}, f32[8,128]{1,0:T(8,128)S(1)}, u32[]{:S(2)}, u32[]{:S(2)}) %collective-permute-start.17) | collective-permute-done | bytes 4128 | tf_op jit(solution)/shard_map/ppermute | solution.py:297
  47.5 0.1 collective-permute-start.18
  47.6 3.6 %collective-permute-done.18 = f32[8,128]{1,0:T(8,128)S(1)} collective-permute-done((f32[8,128]{1,0:T(8,128)S(1)}, f32[8,128]{1,0:T(8,128)S(1)}, u32[]{:S(2)}, u32[]{:S(2)}) %collective-permute-start.18) | collective-permute-done | bytes 4128 | tf_op jit(solution)/shard_map/ppermute | solution.py:313
  51.1 0.0 collective-permute-start.19
  51.1 2.5 %collective-permute-done.19 = f32[8,128]{1,0:T(8,128)S(1)} collective-permute-done((f32[8,128]{1,0:T(8,128)S(1)}, f32[8,128]{1,0:T(8,128)S(1)}, u32[]{:S(2)}, u32[]{:S(2)}) %collective-permute-start.19) | collective-permute-done | bytes 4128 | tf_op jit(solution)/shard_map/ppermute | solution.py:314
  53.6 0.1 collective-permute-start.20
  53.7 0.0 collective-permute-done.6.ze
  53.7 0.0 collective-permute-done.7.zo
  53.7 3.1 %shard_map.94 = (f32[512,128]{1,0:T(8,128)S(1)}, f32[64,128]{1,0:T(8,128)S(1)}, f32[64,128]{1,0:T(8,128)S(1)}, f32[64,128]{1,0:T(8,128)S(1)}, f32[64,128]{1,0:T(8,128)S(1)}) custom-call(s32[4]{0:T(128)S(1)} %pad_add_fusion.place, f32[512,128]{1,0:T(8,128)S(1)} %get-tuple-element.39.r2, f32[512,128]{1,0:T(8,128)S(1)} %get-tuple-element.28.w, ...), custom_call_target="tpu_custom_call" | custom-call | flops 15360000 | bytes 1000000 | tf_op jit(solution)/shard_map/pallas_call | solution.py:31
  56.8 0.1 collective-permute-start.8
  56.9 2.5 %collective-permute-start.9 = (f32[64,128]{1,0:T(8,128)S(1)}, f32[64,128]{1,0:T(8,128)S(1)}, u32[]{:S(2)}, u32[]{:S(2)}) collective-permute-start(f32[64,128]{1,0:T(8,128)S(1)} %get-tuple-element.46), channel_id=1, source_target_pairs={{8,16},{16,8},{24,32},{32,24},{40,48},{48,40},{56,64},{64,56},{72,... | collective-permute-start | bytes 98312 | tf_op jit(solution)/shard_map/ppermute | solution.py:322
  59.4 8.9 %collective-permute-start.10 = (f32[64,128]{1,0:T(8,128)S(1)}, f32[64,128]{1,0:T(8,128)S(1)}, u32[]{:S(2)}, u32[]{:S(2)}) collective-permute-start(f32[64,128]{1,0:T(8,128)S(1)} %get-tuple-element.47), channel_id=1, source_target_pairs={{0,1},{1,0},{2,3},{3,2},{4,5},{5,4},{6,7},{7,6},{8,9},{9,8},{10,11... | collective-permute-start | bytes 98312 | tf_op jit(solution)/shard_map/ppermute | solution.py:321
  68.3 0.0 collective-permute-start.11
  68.3 0.0 collective-permute-done.20
  68.3 0.1 shard_map.96.correction
  68.4 0.0 collective-permute-done.8.ze
  68.5 0.0 collective-permute-done.9.zo
  68.5 0.7 collective-permute-done.10.xe
  69.2 2.8 %collective-permute-done.11.xo = f32[64,128]{1,0:T(8,128)S(1)} collective-permute-done((f32[64,128]{1,0:T(8,128)S(1)}, f32[64,128]{1,0:T(8,128)S(1)}, u32[]{:S(2)}, u32[]{:S(2)}) %collective-permute-start.11) | collective-permute-done | bytes 32800 | tf_op jit(solution)/shard_map/ppermute | solution.py:322
  71.9 1.3 %shard_map.97 = f32[512,128]{1,0:T(8,128)} custom-call(s32[4]{0:T(128)S(1)} %pad_add_fusion.place, f32[512,128]{1,0:T(8,128)S(1)} %get-tuple-element.44.first, f32[64,128]{1,0:T(8,128)S(1)} %collective-permute-done.8.ze, f32[64,128]{1,0:T(8,128)S(1)} %collective-permute-done.9.zo, f32[64,128]{1,0:T(8,128)S(1)} %collective-permute-done.10.xe, ...), custom_call_target="tpu_custom_call" | custom-call | flops 200000 | bytes 1000000 | tf_op jit(solution)/shard_map/pallas_call | solution.py:31
  (15 shorter events, 0.1 us)
Async XLA Ops:
  0.1 1.0 %copy-start.3 = (f32[8,8,8,1,1,128]{5,4,3,2,1,0:T(1,128)S(1)}, f32[8,8,8,1,1,128]{5,4,3,2,1,0:T(1,128)}, u32[]{:S(2)}) copy-start(f32[8,8,8,1,1,128]{5,4,3,2,1,0:T(1,128)} %param.9) | copy-start | bytes 786436
  1.0 0.9 %copy-start.4 = (f32[8,8,8,1,1,128]{5,4,3,2,1,0:T(1,128)S(1)}, f32[8,8,8,1,1,128]{5,4,3,2,1,0:T(1,128)}, u32[]{:S(2)}) copy-start(f32[8,8,8,1,1,128]{5,4,3,2,1,0:T(1,128)} %param.10) | copy-start | bytes 786436
  2.0 0.9 %copy-start.5 = (f32[8,8,8,1,1,128]{5,4,3,2,1,0:T(1,128)S(1)}, f32[8,8,8,1,1,128]{5,4,3,2,1,0:T(1,128)}, u32[]{:S(2)}) copy-start(f32[8,8,8,1,1,128]{5,4,3,2,1,0:T(1,128)} %param.11) | copy-start | bytes 786436
  2.9 12.3 %copy-start.7 = (f32[3,10,10,1,1,128]{5,4,3,2,1,0:T(1,128)S(1)}, f32[3,10,10,1,1,128]{5,4,3,2,1,0:T(1,128)}, u32[]{:S(2)}) copy-start(f32[3,10,10,1,1,128]{5,4,3,2,1,0:T(1,128)} %param.12) | copy-start | bytes 460804
  3.5 12.8 %collective-permute-start = (f32[128,128]{1,0:T(8,128)S(1)}, f32[128,128]{1,0:T(8,128)S(1)}, u32[]{:S(2)}, u32[]{:S(2)}) collective-permute-start(f32[128,128]{1,0:T(8,128)S(1)} %get-tuple-element.30), channel_id=1, source_target_pairs={{0,8},{8,0},{16,24},{24,16},{32,40},{40,32},{48,56},{56,48},{64,72... | collective-permute-start | bytes 196616 | tf_op jit(solution)/shard_map/ppermute | solution.py:321
  5.7 10.7 %collective-permute-start.1 = (f32[128,128]{1,0:T(8,128)S(1)}, f32[128,128]{1,0:T(8,128)S(1)}, u32[]{:S(2)}, u32[]{:S(2)}) collective-permute-start(f32[128,128]{1,0:T(8,128)S(1)} %get-tuple-element.31), channel_id=1, source_target_pairs={{8,16},{16,8},{24,32},{32,24},{40,48},{48,40},{56,64},{64,56},{72,... | collective-permute-start | bytes 196616 | tf_op jit(solution)/shard_map/ppermute | solution.py:322
  12.8 3.6 %collective-permute-start.2 = (f32[128,128]{1,0:T(8,128)S(1)}, f32[128,128]{1,0:T(8,128)S(1)}, u32[]{:S(2)}, u32[]{:S(2)}) collective-permute-start(f32[128,128]{1,0:T(8,128)S(1)} %get-tuple-element.32), channel_id=1, source_target_pairs={{0,1},{1,0},{2,3},{3,2},{4,5},{5,4},{6,7},{7,6},{8,9},{9,8},{10,11... | collective-permute-start | bytes 196616 | tf_op jit(solution)/shard_map/ppermute | solution.py:321
  14.0 4.0 %collective-permute-start.3 = (f32[128,128]{1,0:T(8,128)S(1)}, f32[128,128]{1,0:T(8,128)S(1)}, u32[]{:S(2)}, u32[]{:S(2)}) collective-permute-start(f32[128,128]{1,0:T(8,128)S(1)} %get-tuple-element.33), channel_id=1, source_target_pairs={{1,2},{2,1},{3,4},{4,3},{5,6},{6,5},{7,0},{0,7},{9,10},{10,9},{11,... | collective-permute-start | bytes 196616 | tf_op jit(solution)/shard_map/ppermute | solution.py:322
  15.6 0.7 copy-start.8
  21.0 2.1 %collective-permute-start.4 = (f32[144,128]{1,0:T(8,128)S(1)}, f32[144,128]{1,0:T(8,128)S(1)}, u32[]{:S(2)}, u32[]{:S(2)}) collective-permute-start(f32[144,128]{1,0:T(8,128)S(1)} %get-tuple-element.37), channel_id=1, source_target_pairs={{0,1},{1,0},{2,3},{3,2},{4,5},{5,4},{6,7},{7,6},{8,9},{9,8},{10,11... | collective-permute-start | bytes 221192 | tf_op jit(solution)/shard_map/ppermute | solution.py:321
  22.2 4.1 %collective-permute-start.5 = (f32[144,128]{1,0:T(8,128)S(1)}, f32[144,128]{1,0:T(8,128)S(1)}, u32[]{:S(2)}, u32[]{:S(2)}) collective-permute-start(f32[144,128]{1,0:T(8,128)S(1)} %get-tuple-element.38), channel_id=1, source_target_pairs={{1,2},{2,1},{3,4},{4,3},{5,6},{6,5},{7,0},{0,7},{9,10},{10,9},{11,... | collective-permute-start | bytes 221192 | tf_op jit(solution)/shard_map/ppermute | solution.py:322
  26.3 3.0 %copy-start = (f32[1,1,128,512]{3,2,1,0:T(8,128)S(1)}, f32[1,1,128,512]{3,2,1,0:T(8,128)}, u32[]{:S(2)}) copy-start(f32[1,1,128,512]{3,2,1,0:T(8,128)} %param.17) | copy-start | bytes 786436
  26.3 3.0 %copy-start.1 = (f32[1,1,128,256]{3,2,1,0:T(8,128)S(1)}, f32[1,1,128,256]{3,2,1,0:T(8,128)}, u32[]{:S(2)}) copy-start(f32[1,1,128,256]{3,2,1,0:T(8,128)} %param.16) | copy-start | bytes 393220
  26.3 3.0 %copy-start.2 = (f32[1,1,128,128]{3,2,1,0:T(8,128)S(1)}, f32[1,1,128,128]{3,2,1,0:T(8,128)}, u32[]{:S(2)}) copy-start(f32[1,1,128,128]{3,2,1,0:T(8,128)} %param.15) | copy-start | bytes 196612
  26.9 26.8 %collective-permute-start.6 = (f32[144,128]{1,0:T(8,128)S(1)}, f32[144,128]{1,0:T(8,128)S(1)}, u32[]{:S(2)}, u32[]{:S(2)}) collective-permute-start(f32[144,128]{1,0:T(8,128)S(1)} %get-tuple-element.42), channel_id=1, source_target_pairs={{0,8},{8,0},{16,24},{24,16},{32,40},{40,32},{48,56},{56,48},{64,72... | collective-permute-start | bytes 221192 | tf_op jit(solution)/shard_map/ppermute | solution.py:321
  27.0 26.7 %collective-permute-start.7 = (f32[144,128]{1,0:T(8,128)S(1)}, f32[144,128]{1,0:T(8,128)S(1)}, u32[]{:S(2)}, u32[]{:S(2)}) collective-permute-start(f32[144,128]{1,0:T(8,128)S(1)} %get-tuple-element.43), channel_id=1, source_target_pairs={{8,16},{16,8},{24,32},{32,24},{40,48},{48,40},{56,64},{64,56},{72,... | collective-permute-start | bytes 221192 | tf_op jit(solution)/shard_map/ppermute | solution.py:322
  29.3 0.7 copy-start.6
  30.2 2.3 %collective-permute-start.12 = (f32[8,128]{1,0:T(8,128)S(1)}, f32[8,128]{1,0:T(8,128)S(1)}, u32[]{:S(2)}, u32[]{:S(2)}) collective-permute-start(f32[8,128]{1,0:T(8,128)S(1)} %get-tuple-element.49), channel_id=1, source_target_pairs={{0,1},{1,0},{2,3},{3,2},{4,5},{5,4},{6,7},{7,6},{8,9},{9,8},{10,11... | collective-permute-start | bytes 12296 | tf_op jit(solution)/shard_map/ppermute | solution.py:297
  32.4 2.8 %collective-permute-start.13 = (f32[8,128]{1,0:T(8,128)S(1)}, f32[8,128]{1,0:T(8,128)S(1)}, u32[]{:S(2)}, u32[]{:S(2)}) collective-permute-start(f32[8,128]{1,0:T(8,128)S(1)} %add.36), channel_id=1, source_target_pairs={{0,2},{1,3},{2,0},{3,1},{4,6},{5,7},{6,4},{7,5},{8,10},{9,11},{10,... | collective-permute-start | bytes 12296 | tf_op jit(solution)/shard_map/ppermute | solution.py:297
  35.2 3.7 %collective-permute-start.14 = (f32[8,128]{1,0:T(8,128)S(1)}, f32[8,128]{1,0:T(8,128)S(1)}, u32[]{:S(2)}, u32[]{:S(2)}) collective-permute-start(f32[8,128]{1,0:T(8,128)S(1)} %add.37), channel_id=1, source_target_pairs={{2,4},{3,5},{4,2},{5,3},{6,0},{7,1},{0,6},{1,7},{10,12},{11,13},{1... | collective-permute-start | bytes 12296 | tf_op jit(solution)/shard_map/ppermute | solution.py:297
  38.9 2.5 %collective-permute-start.15 = (f32[8,128]{1,0:T(8,128)S(1)}, f32[8,128]{1,0:T(8,128)S(1)}, u32[]{:S(2)}, u32[]{:S(2)}) collective-permute-start(f32[8,128]{1,0:T(8,128)S(1)} %add.38.grouped), channel_id=1, source_target_pairs={{0,8},{8,0},{16,24},{24,16},{32,40},{40,32},{48,56},{56,48},{64,72... | collective-permute-start | bytes 12296 | tf_op jit(solution)/shard_map/ppermute | solution.py:297
  41.3 3.7 %collective-permute-start.16 = (f32[8,128]{1,0:T(8,128)S(1)}, f32[8,128]{1,0:T(8,128)S(1)}, u32[]{:S(2)}, u32[]{:S(2)}) collective-permute-start(f32[8,128]{1,0:T(8,128)S(1)} %add.39), channel_id=1, source_target_pairs={{8,16},{16,8},{24,0},{0,24},{40,48},{48,40},{56,32},{32,56},{72,80... | collective-permute-start | bytes 12296 | tf_op jit(solution)/shard_map/ppermute | solution.py:297
  45.0 2.5 %collective-permute-start.17 = (f32[8,128]{1,0:T(8,128)S(1)}, f32[8,128]{1,0:T(8,128)S(1)}, u32[]{:S(2)}, u32[]{:S(2)}) collective-permute-start(f32[8,128]{1,0:T(8,128)S(1)} %add.40), channel_id=1, source_target_pairs={{0,32},{8,40},{16,48},{24,56},{32,0},{40,8},{48,16},{56,24},{64,96... | collective-permute-start | bytes 12296 | tf_op jit(solution)/shard_map/ppermute | solution.py:297
  47.5 3.7 %collective-permute-start.18 = (f32[8,128]{1,0:T(8,128)S(1)}, f32[8,128]{1,0:T(8,128)S(1)}, u32[]{:S(2)}, u32[]{:S(2)}) collective-permute-start(f32[8,128]{1,0:T(8,128)S(1)} %add.41), channel_id=1, source_target_pairs={{32,64},{40,72},{48,80},{56,88},{64,32},{72,40},{80,48},{88,56},{9... | collective-permute-start | bytes 12296 | tf_op jit(solution)/shard_map/ppermute | solution.py:313
  51.1 2.5 %collective-permute-start.19 = (f32[8,128]{1,0:T(8,128)S(1)}, f32[8,128]{1,0:T(8,128)S(1)}, u32[]{:S(2)}, u32[]{:S(2)}) collective-permute-start(f32[8,128]{1,0:T(8,128)S(1)} %collective-permute-done.18), channel_id=1, source_target_pairs={{0,32},{8,40},{16,48},{24,56},{32,0},{40,8},{48,16},{56,24},{64,96... | collective-permute-start | bytes 12296 | tf_op jit(solution)/shard_map/ppermute | solution.py:314
  53.6 14.7 %collective-permute-start.20 = (f32[8,128]{1,0:T(8,128)S(1)}, f32[8,128]{1,0:T(8,128)S(1)}, u32[]{:S(2)}, u32[]{:S(2)}) collective-permute-start(f32[8,128]{1,0:T(8,128)S(1)} %collective-permute-done.19), channel_id=1, source_target_pairs={{32,64},{40,72},{48,80},{56,88},{64,32},{72,40},{80,48},{88,56},{9... | collective-permute-start | bytes 12296 | tf_op jit(solution)/shard_map/ppermute | solution.py:315
  56.8 11.7 %collective-permute-start.8 = (f32[64,128]{1,0:T(8,128)S(1)}, f32[64,128]{1,0:T(8,128)S(1)}, u32[]{:S(2)}, u32[]{:S(2)}) collective-permute-start(f32[64,128]{1,0:T(8,128)S(1)} %get-tuple-element.45), channel_id=1, source_target_pairs={{0,8},{8,0},{16,24},{24,16},{32,40},{40,32},{48,56},{56,48},{64,72... | collective-permute-start | bytes 98312 | tf_op jit(solution)/shard_map/ppermute | solution.py:321
  56.9 11.6 %collective-permute-start.9 = (f32[64,128]{1,0:T(8,128)S(1)}, f32[64,128]{1,0:T(8,128)S(1)}, u32[]{:S(2)}, u32[]{:S(2)}) collective-permute-start(f32[64,128]{1,0:T(8,128)S(1)} %get-tuple-element.46), channel_id=1, source_target_pairs={{8,16},{16,8},{24,32},{32,24},{40,48},{48,40},{56,64},{64,56},{72,... | collective-permute-start | bytes 98312 | tf_op jit(solution)/shard_map/ppermute | solution.py:322
  59.4 9.8 %collective-permute-start.10 = (f32[64,128]{1,0:T(8,128)S(1)}, f32[64,128]{1,0:T(8,128)S(1)}, u32[]{:S(2)}, u32[]{:S(2)}) collective-permute-start(f32[64,128]{1,0:T(8,128)S(1)} %get-tuple-element.47), channel_id=1, source_target_pairs={{0,1},{1,0},{2,3},{3,2},{4,5},{5,4},{6,7},{7,6},{8,9},{9,8},{10,11... | collective-permute-start | bytes 98312 | tf_op jit(solution)/shard_map/ppermute | solution.py:321
  68.3 3.6 %collective-permute-start.11 = (f32[64,128]{1,0:T(8,128)S(1)}, f32[64,128]{1,0:T(8,128)S(1)}, u32[]{:S(2)}, u32[]{:S(2)}) collective-permute-start(f32[64,128]{1,0:T(8,128)S(1)} %get-tuple-element.48), channel_id=1, source_target_pairs={{1,2},{2,1},{3,4},{4,3},{5,6},{6,5},{7,0},{0,7},{9,10},{10,9},{11,... | collective-permute-start | bytes 98312 | tf_op jit(solution)/shard_map/ppermute | solution.py:322

commit v3 on v2

--- a/solution.py
+++ b/solution.py
@@ -26,14 +26,19 @@
     return [(base + a, base + b) for base in range(0, length, group) for a, b in pairs]
 
 
-def call(kernel, out_rows, scratch_rows, *args):
-    flops = 2 * 60000 * 128 if scratch_rows else 200000
+def call(kernel, outs, scratch_rows, *args, in_hbm=(), scratch=(), flops=2 * 60000 * 128):
+    outs = [jax.ShapeDtypeStruct((out, 128), F32) if isinstance(out, int) else out for out in outs]
+    specs = [pl.BlockSpec(memory_space=pltpu.SMEM) if a.ndim == 1 else VMEM for a in args]
+    args = list(args)
+    for at in in_hbm:
+        specs[at] = pl.BlockSpec(memory_space=pltpu.HBM)
+        args[at] = pltpu.with_memory_space_constraint(args[at], pltpu.HBM)
     return pl.pallas_call(
         kernel,
-        out_shape=[jax.ShapeDtypeStruct((rows, 128), F32) for rows in out_rows],
-        in_specs=[pl.BlockSpec(memory_space=pltpu.SMEM) if a.ndim == 1 else VMEM for a in args],
-        out_specs=[VMEM] * len(out_rows),
-        scratch_shapes=[pltpu.VMEM((rows, 128), F32) for rows in scratch_rows],
+        out_shape=outs,
+        in_specs=specs,
+        out_specs=[VMEM] * len(outs),
+        scratch_shapes=[pltpu.VMEM((rows, 128), F32) for rows in scratch_rows] + list(scratch),
         compiler_params=pltpu.CompilerParams(vmem_limit_bytes=8 * 1024 * 1024),
         cost_estimate=pl.CostEstimate(flops=flops, bytes_accessed=1000000, transcendentals=0),
     )(*args)
@@ -53,7 +58,7 @@
         total = None
         for at, tiles in enumerate(inputs):
             pair = (first_in + at, out) if forward else (out, first_in + at)
-            coef = basis[pl.ds(direction * 100 + pair[0] * 10 + pair[1], 1), :]
+            coef = basis[direction * 100 + pair[0] * 10 + pair[1]]
             terms = [coef * tile for tile in tiles]
             total = terms if total is None else [a + b for a, b in zip(total, terms)]
         results.append(total)
@@ -105,14 +110,15 @@
 
     turn_x(True)
     for k in range(10):
-        zx[pl.ds(k * 10, 10), :] = eigen[pl.ds(k, 1), :] + eigen[pl.ds(10, 10), :]
+        for i in range(10):
+            zx[pl.ds(k * 10 + i, 1), :] = eigen[k] + eigen[10 + i]
 
     def step_y(step, carry):
         rows = rows8(step * 8)
         lines = [[ylow[rows, :]]] + [[work[every(step * 64 + j, 8), :]] for j in range(8)] + [[yhigh[rows, :]]]
         spectral = weigh(basis, 2, lines, 0, all_ten, True)
         sums = zx[rows, :]
-        spectral = [[value / (sums + eigen[pl.ds(20 + j, 1), :])] for j, (value,) in enumerate(spectral)]
+        spectral = [[value / (sums + eigen[20 + j])] for j, (value,) in enumerate(spectral)]
         solved = weigh(basis, 2, spectral, 0, all_ten, False)
         ylow[rows, :] = solved[0][0]
         yhigh[rows, :] = solved[9][0]
@@ -176,19 +182,36 @@
     odd[...] = jnp.where(flag, down[...], up[...])
 
 
-def pre_kernel(place, residual, margin, diag, w, c2, ze, zo, xe, xo, zu, zd, xu, xd):
+def pre_kernel(
+    place, residual_hbm, margin_hbm, diag_hbm, map_hbm, own_hbm, group_hbm, top_hbm,
+    xe, zo, ze, xo, w, c2, terms, own_part, coarse_map, own, group, top,
+    residual, margin, diag, zu, zd, xu, xd, sems
+):
+    copies = [
+        pltpu.make_async_copy(source, target, sems.at[at])
+        for at, (source, target) in enumerate((
+            (residual_hbm, residual), (margin_hbm, margin), (diag_hbm, diag), (map_hbm, coarse_map),
+            (own_hbm, own), (group_hbm, group), (top_hbm, top),
+        ))
+    ]
+    for copy in copies:
+        copy.start()
+    copies[0].wait()
+    copies[1].wait()
     w[...] = margin[...] * residual[...]
+    copies[2].wait()
     c2[...] = margin[...] * diag[...]
     for base, source in ((0, w), (FACE, c2)):
         zu[pl.ds(base, FACE), :] = source[layer(7), :]
         zd[pl.ds(base, FACE), :] = source[layer(0), :]
         put_x(xu, base, source, 7)
         put_x(xd, base, source, 0)
-    hand_out(place[0] == 0, zu, zd, ze, zo)
-    hand_out(place[1] == 0, xu, xd, xe, xo)
-
-
-def coarse_kernel(w, coarse_map, own, group, top, terms, own_part):
+    z_low, x_low = place[0] == 0, place[1] == 0
+    hand_out(z_low, zu, zd, ze, zo)
+    xo[...] = jnp.where(x_low, xd[...], xu[...])
+    xe[pl.ds(0, 128), :] = jnp.where(x_low, xu[...], xd[...])
+    for copy in copies[3:]:
+        copy.wait()
     total = w[pl.ds(0, 8), :]
     for at in range(8, 512, 8):
         total = total + w[pl.ds(at, 8), :]
@@ -202,21 +225,21 @@
         terms[pl.ds(at, 1), :] = jnp.sum(top[:, at * 128 : (at + 1) * 128] * rhs, axis=0, keepdims=True)
     for at in range(2):
         terms[pl.ds(4 + at, 1), :] = jnp.sum(group[:, at * 128 : (at + 1) * 128] * rhs, axis=0, keepdims=True)
-
-
-def correct_kernel(total, grouped, own_part, coarse_map, own, group, top, correction):
+    xe[pl.ds(128, 8), :] = terms[...]
+
+
+def correct(total, grouped, own_part, coarse_map, own, group, top):
     sums = own[...] * own_part[pl.ds(0, 1), :]
     for at in range(2):
-        sums = sums + group[:, at * 128 : (at + 1) * 128] * grouped[pl.ds(4 + at, 1), :]
+        sums = sums + group[:, at * 128 : (at + 1) * 128] * grouped[4 + at : 5 + at]
     for at in range(4):
-        sums = sums + top[:, at * 128 : (at + 1) * 128] * total[pl.ds(at, 1), :]
+        sums = sums + top[:, at * 128 : (at + 1) * 128] * total[at : at + 1]
     sol = jnp.sum(sums, axis=1, keepdims=True)
     hit = lax.broadcasted_iota(jnp.int32, (128, 128), 0) == coarse_map[pl.ds(0, 1), :]
-    correction[...] = jnp.zeros((8, 128), F32)
-    correction[pl.ds(0, 1), :] = jnp.sum(jnp.where(hit, sol, 0.0), axis=0, keepdims=True)
-
-
-def first_kernel(place, w, c2, ze, zo, xe, xo, basis, eigen, r, z0, z9, x0, x9, oe, oo, zl, zh, xl, xh, xu, xd, *work):
+    return jnp.sum(jnp.where(hit, sol, 0.0), axis=0, keepdims=True)
+
+
+def first_kernel(place, w, c2, ze, zo, xe, xo, basis, eigen, oe, oo, r, z0, z9, x0, x9, zl, zh, xl, xh, xu, xd, *work):
     z_low = place[0] == 0
     x_low = place[1] == 0
     zh[...] = pick(z_low, ze, zo, 0, FACE)
@@ -231,10 +254,11 @@
             message[pl.ds(FACE + k * 8, 8), :] = w[here, :] - c2[here, :] * r[here, :]
         message[pl.ds(128, 8), :] = z9[pl.ds(i * 8, 8), :]
         message[pl.ds(136, 8), :] = z0[pl.ds(i * 8, 8), :]
-    hand_out(x_low, xu, xd, oe, oo)
-
-
-def middle_kernel(place, r, w, c2, z0, z9, xe, xo, r2, ze, zo, zu, zd):
+    oe[...] = jnp.where(x_low, xu[...], xd[...])
+    oo[pl.ds(0, LINK), :] = jnp.where(x_low, xd[...], xu[...])
+
+
+def middle_kernel(place, r, w, c2, z0, z9, xe, xo, terms, ze, zo, r2, grouped, zu, zd):
     x_low = place[1] == 0
     above = jnp.where(place[3] == 1, pick(x_low, xe, xo, 0, LINK), 0.0)
     below = jnp.where(place[2] == 1, pick(x_low, xo, xe, 0, LINK), 0.0)
@@ -247,12 +271,15 @@
         message[pl.ds(FACE, FACE), :] = w[layer(k), :] - c2[layer(k), :] * r2[layer(k), :]
         message[pl.ds(128, 8), :] = below[edge : edge + 8]
         message[pl.ds(136, 8), :] = above[edge : edge + 8]
-    hand_out(place[0] == 0, zu, zd, ze, zo)
+    ze[pl.ds(0, LINK), :] = jnp.where(place[0] == 0, zu[...], zd[...])
+    zo[...] = jnp.where(place[0] == 0, zd[...], zu[...])
+    grouped[...] = terms[...] + xo[pl.ds(LINK, 8), :]
+    ze[pl.ds(LINK, 8), :] = grouped[...]
 
 
 def second_kernel(
     place, r2, w, c2, z0, z9, x0, x9, aze, azo, axe, axo, xe, xo, ze, zo, basis, eigen,
-    first, ce, co, de, do, field, out, zl, zh, xl, xh, s0, s9, t0, t9, *work
+    co, ce, de, do, first, field, out, zl, zh, xl, xh, s0, s9, t0, t9, *work
 ):
     z_low = place[0] == 0
     x_low = place[1] == 0
@@ -276,14 +303,16 @@
     field[...] = w[...] - c2[...] * first[...]
     solve(field, zl, zh, xl, xh, basis, eigen, out, s0, s9, t0, t9, *work)
     first[...] += out[...]
-    hand_out(z_low, s9, s0, ce, co)
+    ce[...] = jnp.where(z_low, s9[...], s0[...])
+    co[pl.ds(0, FACE), :] = jnp.where(z_low, s0[...], s9[...])
     hand_out(x_low, t9, t0, de, do)
 
 
-def last_kernel(place, first, ze, zo, xe, xo, correction, out):
+def last_kernel(place, first, ze, zo, xe, xo, terms, grouped, own_part, coarse_map, own, group, top, out):
     z_low = place[0] == 0
     x_low = place[1] == 0
-    out[...] = first[...] + correction[pl.ds(0, 1), :]
+    total = terms[...] + zo[pl.ds(FACE, 8), :]
+    out[...] = first[...] + correct(total, grouped[...], own_part, coarse_map, own, group, top)
     out[layer(7), :] += pick(z_low, ze, zo, 0, FACE)
     out[layer(0), :] += pick(z_low, zo, ze, 0, FACE)
     above = jnp.where(place[3] == 1, pick(x_low, xe, xo, 0, FACE), 0.0)
@@ -293,67 +322,62 @@
         out[pl.ds(k * 64, 8), :] += below[k * 8 : k * 8 + 8]
 
 
-def add_over(value, axis, pairs):
-    return value + lax.ppermute(value, axis, pairs)
-
-
-def sum_coarse(value):
-    size = lax.axis_size("coarse")
-    value = add_over(value, "coarse", within(size, 2, 0))
-    value = add_over(value, "coarse", swap(size, 2, 0))
-    return add_over(value, "coarse", swap(size, 2, 1))
-
-
-def sum_dom(value):
-    size = lax.axis_size("dom")
-    value = add_over(value, "dom", within(size, 4, 0))
-    value = add_over(value, "dom", within(size, 4, 1))
-    even, odd = swap(size, 4, 0), swap(size, 4, 1)
-    value = add_over(value, "dom", even)
-    beside = lax.ppermute(value, "dom", odd)
-    across = lax.ppermute(beside, "dom", even)
-    far = lax.ppermute(across, "dom", odd)
-    return value + beside + across + far
-
-
-def over(axis, even, odd):
-    size = lax.axis_size(axis)
-    even = lax.ppermute(even, axis, swap(size, 1, 0))
-    odd = lax.ppermute(odd, axis, swap(size, 1, 1))
-    return even, odd
+def move(value, axis, pairs):
+    return lax.ppermute(value, axis, pairs)
 
 
 def body(residual, margin, diag, basis, eigen, coarse_map, own, group, top):
     shape = residual.shape
     residual, margin, diag = (a.reshape(-1, 128) for a in (residual, margin, diag))
-    basis, eigen, coarse_map = (a.reshape(-1, 128) for a in (basis, eigen, coarse_map))
+    basis, eigen = (a.reshape(-1, 1, 128) for a in (basis, eigen))
+    coarse_map = coarse_map.reshape(1, 128)
     own, group, top = (a.reshape(128, -1) for a in (own, group, top))
     dom, coarse = lax.axis_index("dom"), lax.axis_index("coarse")
-    last = lax.axis_size("coarse") - 1
-    place = jnp.stack([dom % 2, coarse % 2, (coarse > 0).astype(jnp.int32), (coarse < last).astype(jnp.int32)])
-    place = place.astype(jnp.int32)
-
-    w, c2, ze, zo, xe, xo = call(pre_kernel, (512, 512) + (128,) * 4, (128,) * 4, place, residual, margin, diag)
-    axe, axo = over("coarse", xe, xo)
-    aze, azo = over("dom", ze, zo)
-    terms, own_part = call(coarse_kernel, (8, 8), (), w, coarse_map, own, group, top)
-    grouped = sum_coarse(terms)
-    r, z0, z9, x0, x9, xe, xo = call(
-        first_kernel, (512,) + (FACE,) * 4 + (LINK,) * 2, (FACE,) * 4 + (LINK,) * 2 + SOLVE_SCRATCH,
+    doms, coarses = lax.axis_size("dom"), lax.axis_size("coarse")
+    place = jnp.stack([dom % 2, coarse % 2, coarse > 0, coarse < coarses - 1]).astype(jnp.int32)
+    z_even, z_odd = swap(doms, 1, 0), swap(doms, 1, 1)
+    x_even, x_odd = swap(coarses, 1, 0), swap(coarses, 1, 1)
+    is_top = jnp.arange(8)[:, None] < 4
+    held = [jax.ShapeDtypeStruct(a.shape, a.dtype) for a in (coarse_map, own, group, top)]
+
+    xe, zo, ze, xo, w, c2, terms, own_part, coarse_map, own, group, top = call(
+        pre_kernel, [136, 128, 128, 128, 512, 512, 8, 8] + held, (512,) * 3 + (128,) * 4,
+        place, residual, margin, diag, coarse_map, own, group, top,
+        in_hbm=range(1, 8), scratch=[pltpu.SemaphoreType.DMA((7,))], flops=300000,
+    )
+    axe = move(xe, "coarse", x_even)
+    azo, aze = move(zo, "dom", z_odd), move(ze, "dom", z_even)
+    axo = move(xo, "coarse", x_odd)
+    terms = terms + axe[128:]
+    beside = move(terms, "dom", swap(doms, 4, 0))
+    terms = terms + jnp.where(is_top, beside, 0.0)
+    beside = move(terms, "coarse", swap(coarses, 4, 0))
+    xe, xo, r, z0, z9, x0, x9 = call(
+        first_kernel, (LINK, LINK + 8, 512) + (FACE,) * 4, (FACE,) * 4 + (LINK,) * 2 + SOLVE_SCRATCH,
         place, w, c2, aze, azo, axe, axo, basis, eigen,
     )
-    xe, xo = over("coarse", xe, xo)
-    r2, ze, zo = call(middle_kernel, (512, LINK, LINK), (LINK,) * 2, place, r, w, c2, z0, z9, xe, xo)
-    ze, zo = over("dom", ze, zo)
-    total = sum_dom(grouped)
-    first, ce, co, de, do = call(
-        second_kernel, (512,) + (FACE,) * 4, (512, 512) + (FACE,) * 8 + SOLVE_SCRATCH,
+    terms = terms + beside
+    xo = lax.dynamic_update_slice(xo, terms, (LINK, 0))
+    xe, xo = move(xe, "coarse", x_even), move(xo, "coarse", x_odd)
+    ze, zo, r2, grouped = call(
+        middle_kernel, (LINK + 8, LINK, 512, 8), (LINK,) * 2, place, r, w, c2, z0, z9, xe, xo, terms, flops=300000
+    )
+    zo, ze = move(zo, "dom", z_odd), move(ze, "dom", z_even)
+    terms = grouped + ze[LINK:]
+    terms = terms + move(terms, "dom", swap(doms, 8, 0))
+    beside = move(terms, "dom", swap(doms, 8, 1))
+    co, ce, de, do, first = call(
+        second_kernel, (FACE + 8, FACE, FACE, FACE, 512), (512, 512) + (FACE,) * 8 + SOLVE_SCRATCH,
         place, r2, w, c2, z0, z9, x0, x9, aze, azo, axe, axo, xe, xo, ze, zo, basis, eigen,
     )
-    xe, xo = over("coarse", de, do)
-    ze, zo = over("dom", ce, co)
-    (correction,) = call(correct_kernel, (8,), (), total, grouped, own_part, coarse_map, own, group, top)
-    (out,) = call(last_kernel, (512,), (), place, first, ze, zo, xe, xo, correction)
+    terms = terms + beside
+    co = lax.dynamic_update_slice(co, terms, (FACE, 0))
+    zo, ze = move(co, "dom", z_odd), move(ce, "dom", z_even)
+    xe, xo = move(de, "coarse", x_even), move(do, "coarse", x_odd)
+    (out,) = call(
+        last_kernel, (512,), (),
+        place, first, ze, zo, xe, xo, terms, grouped, own_part, coarse_map, own, group, top, flops=300000,
+    )
     return out.reshape(shape)
 
 

time: 73.4 us -> 50.6 us (0.69)
  waiting for transfers between devices: 28.3 us -> 14.4 us
  starting transfers between devices: 31.1 us -> 25.6 us
  local copies, waits for them, and re-layouts: 4.21 us -> 0.01 us
  Pallas kernels: 8.89 us -> 10.3 us
    ppermute x21 -> x16, waiting for transfers between devices: 28.3 us -> 14.4 us  [move(): return lax.ppermute(value, axis, pairs)]
    ppermute x21 -> x16, starting transfers between devices: 31.1 us -> 25.6 us  [move(): return lax.ppermute(value, axis, pairs)]
    unnamed x18 -> x4, local copies, waits for them, and re-layouts: 4.19 us -> 0.01 us
    pallas_call x7 -> x5, Pallas kernels: 8.89 us -> 10.3 us  [call(): pl.pallas_call(kernel, out_shape=outs, in_specs=specs, out_specs=[VMEM] *...]
  transfers between devices with their start and end apart: 21 -> 16, of which waited for: 13 -> 8; matrix products, arithmetic and copies ran while one was open for 1% -> 0% of each run, Pallas kernels for 5% -> 12%
where the time goes in v3:
time: 50.6 us; the launch traced here: 50.5 us
  starting transfers between devices  25.6 us (51%)
  waiting for transfers between devices  14.4 us (28%)
  Pallas kernels  10.3 us (20%)
    ppermute x16, starting transfers between devices, move(): return lax.ppermute(value, axis, pairs)  25.6 us
    ppermute x16, waiting for transfers between devices, move(): return lax.ppermute(value, axis, pairs)  14.4 us
    pallas_call x5, Pallas kernels, call(): pl.pallas_call(kernel, out_shape=outs, in_specs=specs, out_specs=[VMEM] *...  10.3 us
  transfers between devices with their start and end apart: 16, of which 8 were waited for; matrix products, arithmetic and copies ran while one was open for 0% of the time, Pallas kernels for 12%

profile of v3, /device:TPU:1, one launch (start us, length us, event | category | flops | bytes accessed | tf_op | source)
XLA Modules:
  0.0 50.5 jit_solution(91465335299830402)
XLA Ops:
  0.0 0.1 pad_add_fusion.place
  0.1 0.0 copy-start
  0.1 2.1 %shard_map.91 = (f32[136,128]{1,0:T(8,128)S(1)}, f32[128,128]{1,0:T(8,128)S(1)}, f32[128,128]{1,0:T(8,128)S(1)}, f32[128,128]{1,0:T(8,128)S(1)}, f32[512,128]{1,...) custom-call(s32[4]{0:T(128)S(1)} %pad_add_fusion.place, ...), custom_call_target="tpu_custom_call" | custom-call | flops 300000 | bytes 1000000 | tf_op jit(solution)/shard_map/pallas_call | solution.py:36
  2.1 3.3 %collective-permute-start.2 = (f32[136,128]{1,0:T(8,128)S(1)}, f32[136,128]{1,0:T(8,128)S(1)}, u32[]{:S(2)}, u32[]{:S(2)}) collective-permute-start(f32[136,128]{1,0:T(8,128)S(1)} %get-tuple-element.37), channel_id=1, source_target_pairs={{0,1},{1,0},{2,3},{3,2},{4,5},{5,4},{6,7},{7,6},{8,9},{9,8},{10,11... | collective-permute-start | bytes 208904 | tf_op jit(solution)/shard_map/ppermute | solution.py:326
  5.5 0.0 collective-permute-start
  5.5 6.6 %collective-permute-start.1 = (f32[128,128]{1,0:T(8,128)S(1)}, f32[128,128]{1,0:T(8,128)S(1)}, u32[]{:S(2)}, u32[]{:S(2)}) collective-permute-start(f32[128,128]{1,0:T(8,128)S(1)} %get-tuple-element.36), channel_id=1, source_target_pairs={{8,16},{16,8},{24,32},{32,24},{40,48},{48,40},{56,64},{64,56},{72,... | collective-permute-start | bytes 196616 | tf_op jit(solution)/shard_map/ppermute | solution.py:326
  12.1 1.8 %collective-permute-start.3 = (f32[128,128]{1,0:T(8,128)S(1)}, f32[128,128]{1,0:T(8,128)S(1)}, u32[]{:S(2)}, u32[]{:S(2)}) collective-permute-start(f32[128,128]{1,0:T(8,128)S(1)} %get-tuple-element.38), channel_id=1, source_target_pairs={{1,2},{2,1},{3,4},{4,3},{5,6},{6,5},{7,0},{0,7},{9,10},{10,9},{11,... | collective-permute-start | bytes 196616 | tf_op jit(solution)/shard_map/ppermute | solution.py:326
  13.9 0.0 collective-permute-done.2.xe.axe
  13.9 0.0 copy-start.1
  13.9 0.1 collective-permute-start.5
  14.0 2.7 %collective-permute-done.5 = f32[8,128]{1,0:T(8,128)S(1)} collective-permute-done((f32[8,128]{1,0:T(8,128)S(1)}, f32[8,128]{1,0:T(8,128)S(1)}, u32[]{:S(2)}, u32[]{:S(2)}) %collective-permute-start.5) | collective-permute-done | bytes 4128 | tf_op jit(solution)/shard_map/ppermute | solution.py:326
  16.8 0.1 select_add_fusion
  16.8 2.3 %collective-permute-start.6 = (f32[8,128]{1,0:T(8,128)S(1)}, f32[8,128]{1,0:T(8,128)S(1)}, u32[]{:S(2)}, u32[]{:S(2)}) collective-permute-start(f32[8,128]{1,0:T(8,128)S(1)} %select_add_fusion), channel_id=1, source_target_pairs={{0,4},{1,5},{2,6},{3,7},{4,0},{5,1},{6,2},{7,3},{8,12},{9,13},{10,... | collective-permute-start | bytes 12296 | tf_op jit(solution)/shard_map/ppermute | solution.py:326
  19.2 0.0 collective-permute-done.ze.aze
  19.2 0.0 collective-permute-done.1.zo.azo
  19.2 0.0 collective-permute-done.3.xo.axo
  19.2 0.0 copy-done
  19.2 0.0 copy-done.1
  19.2 3.1 %shard_map.92 = (f32[144,128]{1,0:T(8,128)S(1)}, f32[152,128]{1,0:T(8,128)S(1)}, f32[512,128]{1,0:T(8,128)S(1)}, f32[64,128]{1,0:T(8,128)S(1)}, f32[64,128]{1,0:...) custom-call(s32[4]{0:T(128)S(1)} %pad_add_fusion.place, f32[512,128]{1,0:T(8,128)S(1)} %get-tuple-element.33.w, ...), custom_call_target="tpu_custom_call" | custom-call | flops 15360000 | bytes 1000000 | tf_op jit(solution)/shard_map/pallas_call | solution.py:36
  22.3 0.0 collective-permute-done.6
  22.3 1.1 %collective-permute-start.7 = (f32[152,128]{1,0:T(8,128)S(1)}, f32[152,128]{1,0:T(8,128)S(1)}, u32[]{:S(2)}, u32[]{:S(2)}) collective-permute-start(f32[152,128]{1,0:T(8,128)S(1)} %get-tuple-element.63), channel_id=1, source_target_pairs={{1,2},{2,1},{3,4},{4,3},{5,6},{6,5},{7,0},{0,7},{9,10},{10,9},{11,... | collective-permute-start | bytes 233480 | tf_op jit(solution)/shard_map/ppermute | solution.py:326
  23.4 0.7 %collective-permute-start.4 = (f32[144,128]{1,0:T(8,128)S(1)}, f32[144,128]{1,0:T(8,128)S(1)}, u32[]{:S(2)}, u32[]{:S(2)}) collective-permute-start(f32[144,128]{1,0:T(8,128)S(1)} %get-tuple-element.42), channel_id=1, source_target_pairs={{0,1},{1,0},{2,3},{3,2},{4,5},{5,4},{6,7},{7,6},{8,9},{9,8},{10,11... | collective-permute-start | bytes 221192 | tf_op jit(solution)/shard_map/ppermute | solution.py:326
  24.1 0.9 %collective-permute-done.4.xe = f32[144,128]{1,0:T(8,128)S(1)} collective-permute-done((f32[144,128]{1,0:T(8,128)S(1)}, f32[144,128]{1,0:T(8,128)S(1)}, u32[]{:S(2)}, u32[]{:S(2)}) %collective-permute-start.4) | collective-permute-done | bytes 73760 | tf_op jit(solution)/shard_map/ppermute | solution.py:326
  25.0 1.2 %collective-permute-done.7.xo = f32[152,128]{1,0:T(8,128)S(1)} collective-permute-done((f32[152,128]{1,0:T(8,128)S(1)}, f32[152,128]{1,0:T(8,128)S(1)}, u32[]{:S(2)}, u32[]{:S(2)}) %collective-permute-start.7) | collective-permute-done | bytes 77856 | tf_op jit(solution)/shard_map/ppermute | solution.py:326
  26.2 0.6 %shard_map.93 = (f32[152,128]{1,0:T(8,128)S(1)}, f32[144,128]{1,0:T(8,128)S(1)}, f32[512,128]{1,0:T(8,128)S(1)}, f32[8,128]{1,0:T(8,128)S(1)}) custom-call(s32[4]{0:T(128)S(1)} %pad_add_fusion.place, f32[512,128]{1,0:T(8,128)S(1)} %get-tuple-element.39.r, f32[512,128]{1,0:T(8,128)S(1)} %get-tuple-element.33.w, f32[512,128]{1,0:T(8,128)S(1)} %get-tuple-element.34.c2, ...), custom_call_target="tpu_custom_call" | custom-call | flops 300000 | bytes 1000000 | tf_op jit(solution)/shard_map/pallas_call | solution.py:36
  26.8 0.1 collective-permute-start.8
  26.9 0.9 %collective-permute-start.9 = (f32[144,128]{1,0:T(8,128)S(1)}, f32[144,128]{1,0:T(8,128)S(1)}, u32[]{:S(2)}, u32[]{:S(2)}) collective-permute-start(f32[144,128]{1,0:T(8,128)S(1)} %get-tuple-element.49), channel_id=1, source_target_pairs={{8,16},{16,8},{24,32},{32,24},{40,48},{48,40},{56,64},{64,56},{72,... | collective-permute-start | bytes 221192 | tf_op jit(solution)/shard_map/ppermute | solution.py:326
  27.8 2.3 %collective-permute-done.8.ze = f32[152,128]{1,0:T(8,128)S(1)} collective-permute-done((f32[152,128]{1,0:T(8,128)S(1)}, f32[152,128]{1,0:T(8,128)S(1)}, u32[]{:S(2)}, u32[]{:S(2)}) %collective-permute-start.8) | collective-permute-done | bytes 77856 | tf_op jit(solution)/shard_map/ppermute | solution.py:326
  30.1 0.0 collective-permute-start.11
  30.1 3.4 %collective-permute-done.11 = f32[8,128]{1,0:T(8,128)S(1)} collective-permute-done((f32[8,128]{1,0:T(8,128)S(1)}, f32[8,128]{1,0:T(8,128)S(1)}, u32[]{:S(2)}, u32[]{:S(2)}) %collective-permute-start.11) | collective-permute-done | bytes 4128 | tf_op jit(solution)/shard_map/ppermute | solution.py:326
  33.5 1.2 %collective-permute-start.12 = (f32[8,128]{1,0:T(8,128)S(1)}, f32[8,128]{1,0:T(8,128)S(1)}, u32[]{:S(2)}, u32[]{:S(2)}) collective-permute-start(f32[8,128]{1,0:T(8,128)S(1)} %add.31), channel_id=1, source_target_pairs={{64,128},{72,136},{80,144},{88,152},{96,160},{104,168},{112,176},{... | collective-permute-start | bytes 12296 | tf_op jit(solution)/shard_map/ppermute | solution.py:326
  34.7 0.0 collective-permute-done.9.zo
  34.7 3.1 %shard_map.94 = (f32[72,128]{1,0:T(8,128)S(1)}, f32[64,128]{1,0:T(8,128)S(1)}, f32[64,128]{1,0:T(8,128)S(1)}, f32[64,128]{1,0:T(8,128)S(1)}, f32[512,128]{1,0:T(8,128)S(1)}) custom-call(s32[4]{0:T(128)S(1)} %pad_add_fusion.place, f32[512,128]{1,0:T(8,128)S(1)} %get-tuple-element.45.r2, f32[512,128]{1,0:T(8,128)S(1)} %get-tuple-element.33.w, ...), custom_call_target="tpu_custom_call" | custom-call | flops 15360000 | bytes 1000000 | tf_op jit(solution)/shard_map/pallas_call | solution.py:36
  37.8 0.2 collective-permute-done.12
  38.1 1.6 %collective-permute-start.13 = (f32[72,128]{1,0:T(8,128)S(1)}, f32[72,128]{1,0:T(8,128)S(1)}, u32[]{:S(2)}, u32[]{:S(2)}) collective-permute-start(f32[72,128]{1,0:T(8,128)S(1)} %get-tuple-element.61), channel_id=1, source_target_pairs={{8,16},{16,8},{24,32},{32,24},{40,48},{48,40},{56,64},{64,56},{72,... | collective-permute-start | bytes 110600 | tf_op jit(solution)/shard_map/ppermute | solution.py:326
  39.7 0.0 collective-permute-start.10
  39.7 5.8 %collective-permute-start.14 = (f32[64,128]{1,0:T(8,128)S(1)}, f32[64,128]{1,0:T(8,128)S(1)}, u32[]{:S(2)}, u32[]{:S(2)}) collective-permute-start(f32[64,128]{1,0:T(8,128)S(1)} %get-tuple-element.54), channel_id=1, source_target_pairs={{0,1},{1,0},{2,3},{3,2},{4,5},{5,4},{6,7},{7,6},{8,9},{9,8},{10,11... | collective-permute-start | bytes 98312 | tf_op jit(solution)/shard_map/ppermute | solution.py:326
  45.5 0.0 collective-permute-start.15
  45.5 0.0 collective-permute-done.10.ze
  45.5 0.9 %collective-permute-done.14.xe = f32[64,128]{1,0:T(8,128)S(1)} collective-permute-done((f32[64,128]{1,0:T(8,128)S(1)}, f32[64,128]{1,0:T(8,128)S(1)}, u32[]{:S(2)}, u32[]{:S(2)}) %collective-permute-start.14) | collective-permute-done | bytes 32800 | tf_op jit(solution)/shard_map/ppermute | solution.py:326
  46.4 2.8 %collective-permute-done.15.xo = f32[64,128]{1,0:T(8,128)S(1)} collective-permute-done((f32[64,128]{1,0:T(8,128)S(1)}, f32[64,128]{1,0:T(8,128)S(1)}, u32[]{:S(2)}, u32[]{:S(2)}) %collective-permute-start.15) | collective-permute-done | bytes 32800 | tf_op jit(solution)/shard_map/ppermute | solution.py:326
  49.1 0.0 collective-permute-done.13.zo
  49.1 1.4 %shard_map.95 = f32[512,128]{1,0:T(8,128)} custom-call(s32[4]{0:T(128)S(1)} %pad_add_fusion.place, f32[512,128]{1,0:T(8,128)S(1)} %get-tuple-element.50.first, f32[64,128]{1,0:T(8,128)S(1)} %collective-permute-done.10.ze, f32[72,128]{1,0:T(8,128)S(1)} %collective-permute-done.13.zo, f32[64,128]{1,0:T(8,128)S(1)} %collective-permute-done.14.xe, ...), custom_call_target="tpu_custom_call" | custom-call | flops 300000 | bytes 1000000 | tf_op jit(solution)/shard_map/pallas_call | solution.py:36
  (6 shorter events, 0.0 us)
Async XLA Ops:
  0.1 19.1 %copy-start = (f32[3,10,10,1,1,128]{5,4,3,2,1,0:T(1,128)S(1)}, f32[3,10,10,1,1,128]{5,4,3,2,1,0:T(1,128)}, u32[]{:S(2)}) copy-start(f32[3,10,10,1,1,128]{5,4,3,2,1,0:T(1,128)} %param.12) | copy-start | bytes 460804
  2.1 11.8 %collective-permute-start.2 = (f32[136,128]{1,0:T(8,128)S(1)}, f32[136,128]{1,0:T(8,128)S(1)}, u32[]{:S(2)}, u32[]{:S(2)}) collective-permute-start(f32[136,128]{1,0:T(8,128)S(1)} %get-tuple-element.37), channel_id=1, source_target_pairs={{0,1},{1,0},{2,3},{3,2},{4,5},{5,4},{6,7},{7,6},{8,9},{9,8},{10,11... | collective-permute-start | bytes 208904 | tf_op jit(solution)/shard_map/ppermute | solution.py:326
  5.5 13.7 %collective-permute-start = (f32[128,128]{1,0:T(8,128)S(1)}, f32[128,128]{1,0:T(8,128)S(1)}, u32[]{:S(2)}, u32[]{:S(2)}) collective-permute-start(f32[128,128]{1,0:T(8,128)S(1)} %get-tuple-element.35), channel_id=1, source_target_pairs={{0,8},{8,0},{16,24},{24,16},{32,40},{40,32},{48,56},{56,48},{64,72... | collective-permute-start | bytes 196616 | tf_op jit(solution)/shard_map/ppermute | solution.py:326
  5.5 13.7 %collective-permute-start.1 = (f32[128,128]{1,0:T(8,128)S(1)}, f32[128,128]{1,0:T(8,128)S(1)}, u32[]{:S(2)}, u32[]{:S(2)}) collective-permute-start(f32[128,128]{1,0:T(8,128)S(1)} %get-tuple-element.36), channel_id=1, source_target_pairs={{8,16},{16,8},{24,32},{32,24},{40,48},{48,40},{56,64},{64,56},{72,... | collective-permute-start | bytes 196616 | tf_op jit(solution)/shard_map/ppermute | solution.py:326
  12.1 7.1 %collective-permute-start.3 = (f32[128,128]{1,0:T(8,128)S(1)}, f32[128,128]{1,0:T(8,128)S(1)}, u32[]{:S(2)}, u32[]{:S(2)}) collective-permute-start(f32[128,128]{1,0:T(8,128)S(1)} %get-tuple-element.38), channel_id=1, source_target_pairs={{1,2},{2,1},{3,4},{4,3},{5,6},{6,5},{7,0},{0,7},{9,10},{10,9},{11,... | collective-permute-start | bytes 196616 | tf_op jit(solution)/shard_map/ppermute | solution.py:326
  13.9 5.3 %copy-start.1 = (f32[3,10,1,1,128]{4,3,2,1,0:T(1,128)S(1)}, f32[3,10,1,1,128]{4,3,2,1,0:T(1,128)}, u32[]{:S(2)}) copy-start(f32[3,10,1,1,128]{4,3,2,1,0:T(1,128)} %param.13) | copy-start | bytes 46084
  13.9 2.8 %collective-permute-start.5 = (f32[8,128]{1,0:T(8,128)S(1)}, f32[8,128]{1,0:T(8,128)S(1)}, u32[]{:S(2)}, u32[]{:S(2)}) collective-permute-start(f32[8,128]{1,0:T(8,128)S(1)} %slice_add_fusion.1), channel_id=1, source_target_pairs={{0,32},{8,40},{16,48},{24,56},{32,0},{40,8},{48,16},{56,24},{64,96... | collective-permute-start | bytes 12296 | tf_op jit(solution)/shard_map/ppermute | solution.py:326
  16.8 5.4 %collective-permute-start.6 = (f32[8,128]{1,0:T(8,128)S(1)}, f32[8,128]{1,0:T(8,128)S(1)}, u32[]{:S(2)}, u32[]{:S(2)}) collective-permute-start(f32[8,128]{1,0:T(8,128)S(1)} %select_add_fusion), channel_id=1, source_target_pairs={{0,4},{1,5},{2,6},{3,7},{4,0},{5,1},{6,2},{7,3},{8,12},{9,13},{10,... | collective-permute-start | bytes 12296 | tf_op jit(solution)/shard_map/ppermute | solution.py:326
  22.3 3.9 %collective-permute-start.7 = (f32[152,128]{1,0:T(8,128)S(1)}, f32[152,128]{1,0:T(8,128)S(1)}, u32[]{:S(2)}, u32[]{:S(2)}) collective-permute-start(f32[152,128]{1,0:T(8,128)S(1)} %get-tuple-element.63), channel_id=1, source_target_pairs={{1,2},{2,1},{3,4},{4,3},{5,6},{6,5},{7,0},{0,7},{9,10},{10,9},{11,... | collective-permute-start | bytes 233480 | tf_op jit(solution)/shard_map/ppermute | solution.py:326
  23.4 1.6 %collective-permute-start.4 = (f32[144,128]{1,0:T(8,128)S(1)}, f32[144,128]{1,0:T(8,128)S(1)}, u32[]{:S(2)}, u32[]{:S(2)}) collective-permute-start(f32[144,128]{1,0:T(8,128)S(1)} %get-tuple-element.42), channel_id=1, source_target_pairs={{0,1},{1,0},{2,3},{3,2},{4,5},{5,4},{6,7},{7,6},{8,9},{9,8},{10,11... | collective-permute-start | bytes 221192 | tf_op jit(solution)/shard_map/ppermute | solution.py:326
  26.8 3.3 %collective-permute-start.8 = (f32[152,128]{1,0:T(8,128)S(1)}, f32[152,128]{1,0:T(8,128)S(1)}, u32[]{:S(2)}, u32[]{:S(2)}) collective-permute-start(f32[152,128]{1,0:T(8,128)S(1)} %get-tuple-element.48), channel_id=1, source_target_pairs={{0,8},{8,0},{16,24},{24,16},{32,40},{40,32},{48,56},{56,48},{64,72... | collective-permute-start | bytes 233480 | tf_op jit(solution)/shard_map/ppermute | solution.py:326
  26.9 7.8 %collective-permute-start.9 = (f32[144,128]{1,0:T(8,128)S(1)}, f32[144,128]{1,0:T(8,128)S(1)}, u32[]{:S(2)}, u32[]{:S(2)}) collective-permute-start(f32[144,128]{1,0:T(8,128)S(1)} %get-tuple-element.49), channel_id=1, source_target_pairs={{8,16},{16,8},{24,32},{32,24},{40,48},{48,40},{56,64},{64,56},{72,... | collective-permute-start | bytes 221192 | tf_op jit(solution)/shard_map/ppermute | solution.py:326
  30.1 3.4 %collective-permute-start.11 = (f32[8,128]{1,0:T(8,128)S(1)}, f32[8,128]{1,0:T(8,128)S(1)}, u32[]{:S(2)}, u32[]{:S(2)}) collective-permute-start(f32[8,128]{1,0:T(8,128)S(1)} %slice_add_fusion), channel_id=1, source_target_pairs={{0,64},{8,72},{16,80},{24,88},{32,96},{40,104},{48,112},{56,120},{... | collective-permute-start | bytes 12296 | tf_op jit(solution)/shard_map/ppermute | solution.py:326
  33.5 4.6 %collective-permute-start.12 = (f32[8,128]{1,0:T(8,128)S(1)}, f32[8,128]{1,0:T(8,128)S(1)}, u32[]{:S(2)}, u32[]{:S(2)}) collective-permute-start(f32[8,128]{1,0:T(8,128)S(1)} %add.31), channel_id=1, source_target_pairs={{64,128},{72,136},{80,144},{88,152},{96,160},{104,168},{112,176},{... | collective-permute-start | bytes 12296 | tf_op jit(solution)/shard_map/ppermute | solution.py:326
  38.1 11.1 %collective-permute-start.13 = (f32[72,128]{1,0:T(8,128)S(1)}, f32[72,128]{1,0:T(8,128)S(1)}, u32[]{:S(2)}, u32[]{:S(2)}) collective-permute-start(f32[72,128]{1,0:T(8,128)S(1)} %get-tuple-element.61), channel_id=1, source_target_pairs={{8,16},{16,8},{24,32},{32,24},{40,48},{48,40},{56,64},{64,56},{72,... | collective-permute-start | bytes 110600 | tf_op jit(solution)/shard_map/ppermute | solution.py:326
  39.7 5.8 %collective-permute-start.10 = (f32[64,128]{1,0:T(8,128)S(1)}, f32[64,128]{1,0:T(8,128)S(1)}, u32[]{:S(2)}, u32[]{:S(2)}) collective-permute-start(f32[64,128]{1,0:T(8,128)S(1)} %get-tuple-element.51), channel_id=1, source_target_pairs={{0,8},{8,0},{16,24},{24,16},{32,40},{40,32},{48,56},{56,48},{64,72... | collective-permute-start | bytes 98312 | tf_op jit(solution)/shard_map/ppermute | solution.py:326
  39.7 6.7 %collective-permute-start.14 = (f32[64,128]{1,0:T(8,128)S(1)}, f32[64,128]{1,0:T(8,128)S(1)}, u32[]{:S(2)}, u32[]{:S(2)}) collective-permute-start(f32[64,128]{1,0:T(8,128)S(1)} %get-tuple-element.54), channel_id=1, source_target_pairs={{0,1},{1,0},{2,3},{3,2},{4,5},{5,4},{6,7},{7,6},{8,9},{9,8},{10,11... | collective-permute-start | bytes 98312 | tf_op jit(solution)/shard_map/ppermute | solution.py:326
  45.5 3.6 %collective-permute-start.15 = (f32[64,128]{1,0:T(8,128)S(1)}, f32[64,128]{1,0:T(8,128)S(1)}, u32[]{:S(2)}, u32[]{:S(2)}) collective-permute-start(f32[64,128]{1,0:T(8,128)S(1)} %get-tuple-element.55), channel_id=1, source_target_pairs={{1,2},{2,1},{3,4},{4,3},{5,6},{6,5},{7,0},{0,7},{9,10},{10,9},{11,... | collective-permute-start | bytes 98312 | tf_op jit(solution)/shard_map/ppermute | solution.py:326

commit v4 on v3

v4 whole, which is shorter than its diff:
```python
import jax
import jax.numpy as jnp
from jax import lax
from jax.experimental import pallas as pl
from jax.experimental.pallas import tpu as pltpu
from jax.sharding import PartitionSpec as P

sum_scale = 0.015625
F32 = jnp.float32
FACE = 64
LINK = 144
RELAY = 32
VMEM = pl.BlockSpec(memory_space=pltpu.VMEM)


def swap(length, stride, odd):
    ring = length // stride
    pairs = []
    for low in range(odd, ring, 2):
        high = (low + 1) % ring
        pairs += [(low, high), (high, low)]
    return [(a * stride + r, b * stride + r) for a, b in pairs for r in range(stride)]


def within(length, group, odd):
    pairs = swap(group, 1, odd)
    return [(base + a, base + b) for base in range(0, length, group) for a, b in pairs]


def call(kernel, outs, scratch_rows, *args, in_hbm=(), scratch=(), flops=2 * 60000 * 128):
    outs = [jax.ShapeDtypeStruct((out, 128), F32) if isinstance(out, int) else out for out in outs]
    specs = [pl.BlockSpec(memory_space=pltpu.SMEM) if a.ndim == 1 else VMEM for a in args]
    args = list(args)
    for at in in_hbm:
        specs[at] = pl.BlockSpec(memory_space=pltpu.HBM)
        args[at] = pltpu.with_memory_space_constraint(args[at], pltpu.HBM)
    return pl.pallas_call(
        kernel,
        out_shape=outs,
        in_specs=specs,
        out_specs=[VMEM] * len(outs),
        scratch_shapes=[pltpu.VMEM((rows, 128), F32) for rows in scratch_rows] + list(scratch),
        compiler_params=pltpu.CompilerParams(vmem_limit_bytes=8 * 1024 * 1024),
        cost_estimate=pl.CostEstimate(flops=flops, bytes_accessed=1000000, transcendentals=0),
    )(*args)


def rows8(start):
    return pl.ds(pl.multiple_of(start, 8), 8)


def every(start, stride):
    return pl.ds(start, 8, stride=stride)


def weigh(basis, direction, inputs, first_in, outs, forward):
    results = []
    for out in outs:
        total = None
        for at, tiles in enumerate(inputs):
            pair = (first_in + at, out) if forward else (out, first_in + at)
            coef = basis[direction * 100 + pair[0] * 10 + pair[1]]
            terms = [coef * tile for tile in tiles]
            total = terms if total is None else [a + b for a, b in zip(total, terms)]
        results.append(total)
    return results


ALL_TEN = range(10)
INNER = range(1, 9)


def forward_own(field, basis, work, ylow, yhigh, plane):
    def y_face_in(face, at, turn):
        lines = [[pltpu.roll(field[every(k * 64 + at, 8), :], turn, 1)] for k in range(8)]
        for k, (value,) in enumerate(weigh(basis, 0, lines, 1, ALL_TEN, True)):
            plane[rows8(k * 8), :] = value
        lines = [[plane[every(i, 8), :], plane[every(64 + i, 8), :]] for i in range(8)]
        for i, (value, rest) in enumerate(weigh(basis, 1, lines, 1, ALL_TEN, True)):
            face[every(i, 10), :] = value
            face[every(80 + i, 10), :] = rest

    y_face_in(ylow, 7, 1)
    y_face_in(yhigh, 0, 127)

    def forward_z(step, carry):
        tiles = [step * 2, step * 2 + 1]
        lines = [[field[rows8(k * 64 + i * 8), :] for i in tiles] for k in range(8)]
        for k, values in enumerate(weigh(basis, 0, lines, 1, ALL_TEN, True)):
            for i, value in zip(tiles, values):
                work[rows8((k * 10 + i + 1) * 8), :] = value
        return carry

    lax.fori_loop(0, 4, forward_z, 0)


def solve(work_in, ylow_in, yhigh_in, z_low, z_high, x_low, x_high, basis, inverse, work, ylow, yhigh):
    def add_z(step, carry):
        tiles = [step * 2, step * 2 + 1]
        low = [z_low[rows8(i * 8), :] for i in tiles]
        high = [z_high[rows8(i * 8), :] for i in tiles]
        for k in ALL_TEN:
            for i, a, b in zip(tiles, low, high):
                rows = rows8((k * 10 + i + 1) * 8)
                work[rows, :] = work_in[rows, :] + basis[k] * a + basis[90 + k] * b
        return carry

    lax.fori_loop(0, 4, add_z, 0)
    lines = [[x_low[rows8(k * 8), :], x_high[rows8(k * 8), :]] for k in range(8)]
    for k, (low, high) in enumerate(weigh(basis, 0, lines, 1, ALL_TEN, True)):
        work[rows8(k * 80), :] = low
        work[rows8(k * 80 + 72), :] = high

    def turn_x(forward):
        def step_x(step, carry):
            ks = [step * 2, step * 2 + 1]
            lines = [[work[rows8(k * 80 + i * 8), :] for k in ks] for i in range(10)]
            for i, values in enumerate(weigh(basis, 1, lines, 0, ALL_TEN, forward)):
                for k, value in zip(ks, values):
                    work[rows8(k * 80 + i * 8), :] = value
            return carry

        lax.fori_loop(0, 5, step_x, 0)

    turn_x(True)

    def step_y(step, carry):
        rows = rows8(step * 8)
        lines = [[ylow_in[rows, :]]] + [[work[every(step * 64 + j, 8), :]] for j in range(8)] + [[yhigh_in[rows, :]]]
        spectral = weigh(basis, 2, lines, 0, ALL_TEN, True)
        spectral = [[value * inverse[rows8(j * 104 + step * 8), :]] for j, (value,) in enumerate(spectral)]
        solved = weigh(basis, 2, spectral, 0, ALL_TEN, False)
        ylow[rows, :] = solved[0][0]
        yhigh[rows, :] = solved[9][0]
        for j in range(8):
            work[every(step * 64 + j, 8), :] = solved[j + 1][0]
        return carry

    lax.fori_loop(0, 13, step_y, 0)
    turn_x(False)


def back_faces(work, basis, z_face, x_face):
    def back_z(step, carry):
        tiles = [step * 2, step * 2 + 1]
        lines = [[work[rows8((k * 10 + i + 1) * 8), :] for i in tiles] for k in range(10)]
        for at, values in enumerate(weigh(basis, 0, lines, 0, (0, 9), False)):
            for i, value in zip(tiles, values):
                z_face[rows8(at * FACE + i * 8), :] = value
        return carry

    lax.fori_loop(0, 4, back_z, 0)
    lines = [[work[rows8(k * 80), :], work[rows8(k * 80 + 72), :]] for k in range(10)]
    for k, (low, high) in enumerate(weigh(basis, 0, lines, 0, INNER, False)):
        x_face[rows8(k * 8), :] = low
        x_face[rows8(FACE + k * 8), :] = high


def back_inner(work, ylow, yhigh, basis, out, plane, plus=None):
    def back_z(step, carry):
        tiles = [step * 2, step * 2 + 1]
        lines = [[work[rows8((k * 10 + i + 1) * 8), :] for i in tiles] for k in range(10)]
        for k, values in enumerate(weigh(basis, 0, lines, 0, INNER, False)):
            for i, value in zip(tiles, values):
                rows = rows8(k * 64 + i * 8)
                out[rows, :] = value if plus is None else value + plus[rows, :]
        return carry

    lax.fori_loop(0, 4, back_z, 0)

    def y_face_out(face, at, turn):
        lines = [[face[every(i, 10), :], face[every(80 + i, 10), :]] for i in range(10)]
        for i, (value, rest) in enumerate(weigh(basis, 1, lines, 0, INNER, False)):
            plane[rows8(i * 16), :] = value
            plane[rows8(i * 16 + 8), :] = rest
        lines = [[plane[every(k, 16), :]] for k in range(10)]
        for k, (value,) in enumerate(weigh(basis, 0, lines, 0, INNER, False)):
            out[every(k * 64 + at, 8), :] += pltpu.roll(value, turn, 1)

    y_face_out(ylow, 7, 127)
    y_face_out(yhigh, 0, 1)


def layer(k):
    return pl.ds(pl.multiple_of(k * 64, 64), 64)


def face(at):
    return pl.ds(pl.multiple_of(at * FACE, FACE), FACE)


def put_x(ref, base, array, i):
    for k in range(8):
        ref[pl.ds(base + k * 8, 8), :] = array[rows8(k * 64 + i * 8), :]


def pick(flag, array, other, start, rows):
    return jnp.where(flag, array[pl.ds(start, rows), :], other[pl.ds(start, rows), :])


def keep(flag, value):
    return jnp.where(flag == 1, value, 0.0)


def first_kernel(
    place, residual_hbm, margin_hbm, diag_hbm, map_hbm, own_hbm, group_hbm, top_hbm,
    zo, ze, xe, xo, w, c2, terms, own_part, coarse_map, own, group, top, residual, margin, diag, sems
):
    sources = (residual_hbm, margin_hbm, diag_hbm, map_hbm, own_hbm, group_hbm, top_hbm)
    targets = (residual, margin, diag, coarse_map, own, group, top)
    copies = [pltpu.make_async_copy(a, b, sems.at[at]) for at, (a, b) in enumerate(zip(sources, targets))]
    for copy in copies:
        copy.start()
    copies[0].wait()
    copies[1].wait()
    w[...] = margin[...] * residual[...]
    copies[2].wait()
    c2[...] = margin[...] * diag[...]
    z_up, x_up = place[0], place[1]
    for base, source in ((0, w), (FACE, c2)):
        zo[pl.ds(base, FACE), :] = source[layer(z_up * 7), :]
        ze[pl.ds(base, FACE), :] = source[layer(7 - z_up * 7), :]
        put_x(xo, base, source, x_up * 7)
        put_x(xe, base, source, 7 - x_up * 7)
    zo[pl.ds(128, 16), :] = jnp.zeros((16, 128), F32)
    total = w[pl.ds(0, 8), :]
    for at in range(8, 512, 8):
        total = total + w[pl.ds(at, 8), :]
    element_sum = jnp.sum(total, axis=0, keepdims=True) * sum_scale
    for copy in copies[3:]:
        copy.wait()
    hit = lax.broadcasted_iota(jnp.int32, (128, 128), 0) == coarse_map[pl.ds(0, 1), :]
    rhs = jnp.sum(jnp.where(hit, element_sum, 0.0), axis=1, keepdims=True)
    own_part[...] = jnp.zeros((8, 128), F32)
    own_part[pl.ds(0, 1), :] = jnp.sum(own[...] * rhs, axis=0, keepdims=True)
    terms[...] = jnp.zeros((8, 128), F32)
    for at in range(4):
        terms[pl.ds(at, 1), :] = jnp.sum(top[:, at * 128 : (at + 1) * 128] * rhs, axis=0, keepdims=True)
    for at in range(2):
        terms[pl.ds(4 + at, 1), :] = jnp.sum(group[:, at * 128 : (at + 1) * 128] * rhs, axis=0, keepdims=True)
    xe[pl.ds(128, 8), :] = terms[...]
    ze[pl.ds(128, 8), :] = terms[...]


def own_kernel(w, basis, eigen, terms, work, ylow, yhigh, inverse, same, plane, zx):
    same[...] = terms[...]
    forward_own(w, basis, work, ylow, yhigh, plane)
    for k in range(10):
        for i in range(10):
            zx[pl.ds(k * 10 + i, 1), :] = eigen[k] + eigen[10 + i]
    for j in range(10):
        inverse[pl.ds(j * 104, 104), :] = 1.0 / (zx[...] + eigen[20 + j])


def pass_kernel(
    place, w, c2, azo, aze, axo, axe, basis, work_in, ylow_in, yhigh_in, inverse,
    zo, ze, xo, xe, r, z_face, x_face, zl, zh, xl, xh, work, ylow, yhigh, plane
):
    z_low, x_low = place[0] == 0, place[1] == 0
    zh[...] = pick(z_low, aze, azo, 0, FACE)
    zl[...] = pick(z_low, azo, aze, 0, FACE)
    xh[...] = keep(place[3], pick(x_low, axe, axo, 0, FACE))
    xl[...] = keep(place[2], pick(x_low, axo, axe, 0, FACE))
    solve(work_in, ylow_in, yhigh_in, zl, zh, xl, xh, basis, inverse, work, ylow, yhigh)
    back_faces(work, basis, z_face, x_face)
    back_inner(work, ylow, yhigh, basis, r, plane)
    for message, up in ((zo, place[0]), (ze, 1 - place[0])):
        here = layer(up * 7)
        message[pl.ds(0, FACE), :] = z_face[face(up), :]
        message[pl.ds(FACE, FACE), :] = w[here, :] - c2[here, :] * r[here, :]
        message[pl.ds(128, 8), :] = x_face[rows8(FACE + up * 56), :]
        message[pl.ds(136, 8), :] = x_face[rows8(up * 56), :]
    zo[pl.ds(LINK, 8), :] = jnp.zeros((8, 128), F32)
    for message, up in ((xo, place[1]), (xe, 1 - place[1])):
        message[pl.ds(0, FACE), :] = x_face[face(up), :]
        for k in range(8):
            here = rows8(k * 64 + up * 56)
            message[pl.ds(FACE + k * 8, 8), :] = w[here, :] - c2[here, :] * r[here, :]


def relay_kernel(place, zo, ze, terms, ro, re, same):
    same[...] = terms[...]
    z_low = place[0] == 0
    for message, up in ((ro, place[1]), (re, 1 - place[1])):
        edge = rows8(136 - up * 8)
        line = rows8(up * 56)
        message[pl.ds(0, 8), :] = jnp.where(z_low, zo[edge, :], ze[edge, :])
        message[pl.ds(8, 8), :] = jnp.where(z_low, ze[edge, :], zo[edge, :])
        message[pl.ds(16, 8), :] = jnp.where(z_low, zo[line, :], ze[line, :])
        message[pl.ds(24, 8), :] = jnp.where(z_low, ze[line, :], zo[line, :])


def second_own_kernel(place, w, c2, r, zo, ze, xo, xe, basis, terms, first, work, ylow, yhigh, same, field, plane):
    same[...] = terms[...]
    z_low, x_low = place[0] == 0, place[1] == 0
    first[...] = r[...]
    first[layer(7), :] += pick(z_low, ze, zo, 0, FACE)
    first[layer(0), :] += pick(z_low, zo, ze, 0, FACE)
    above = keep(place[3], pick(x_low, xe, xo, 0, FACE))
    below = keep(place[2], pick(x_low, xo, xe, 0, FACE))
    for k in range(8):
        first[pl.ds(k * 64 + 56, 8), :] += above[k * 8 : k * 8 + 8]
        first[pl.ds(k * 64, 8), :] += below[k * 8 : k * 8 + 8]
    field[...] = w[...] - c2[...] * first[...]
    forward_own(field, basis, work, ylow, yhigh, plane)


def second_pass_kernel(
    place, azo, aze, axo, axe, z_face, x_face, zo, ze, xo, xe, ro, re, basis, work_in, ylow_in, yhigh_in, inverse,
    co, ce, do, de, work, ylow, yhigh, zl, zh, xl, xh, s_face, t_face
):
    z_low, x_low = place[0] == 0, place[1] == 0
    above = keep(place[3], pick(x_low, re, ro, 0, RELAY))
    below = keep(place[2], pick(x_low, ro, re, 0, RELAY))
    for halo, start, edge in ((zl, 0, 0), (zh, FACE, 8)):
        halo[...] = z_face[pl.ds(start, FACE), :]
        halo[pl.ds(0, 8), :] += below[edge : edge + 8]
        halo[pl.ds(56, 8), :] += above[edge : edge + 8]
    for halo, start, edges in ((xl, 0, below), (xh, FACE, above)):
        halo[...] = x_face[pl.ds(start, FACE), :]
        halo[pl.ds(0, 8), :] += edges[16:24]
        halo[pl.ds(56, 8), :] += edges[24:32]
    zh[...] = pick(z_low, ze, zo, FACE, FACE) - pick(z_low, aze, azo, FACE, FACE) * zh[...]
    zl[...] = pick(z_low, zo, ze, FACE, FACE) - pick(z_low, azo, aze, FACE, FACE) * zl[...]
    xh[...] = keep(place[3], pick(x_low, xe, xo, FACE, FACE) - pick(x_low, axe, axo, FACE, FACE) * xh[...])
    xl[...] = keep(place[2], pick(x_low, xo, xe, FACE, FACE) - pick(x_low, axo, axe, FACE, FACE) * xl[...])
    solve(work_in, ylow_in, yhigh_in, zl, zh, xl, xh, basis, inverse, work, ylow, yhigh)
    back_faces(work, basis, s_face, t_face)
    for message, up in ((co, place[0]), (ce, 1 - place[0])):
        message[pl.ds(0, FACE), :] = s_face[face(up), :]
    for message, up in ((do, place[1]), (de, 1 - place[1])):
        message[...] = t_face[face(up), :]


def inner_kernel(first, work, ylow, yhigh, basis, grouped, own_part, own, group, out, base, plane):
    back_inner(work, ylow, yhigh, basis, out, plane, first)
    sums = own[...] * own_part[pl.ds(0, 1), :]
    for at in range(2):
        sums = sums + group[:, at * 128 : (at + 1) * 128] * grouped[pl.ds(4 + at, 1), :]
    base[...] = sums


def last_kernel(place, inner, base, zo, ze, xo, xe, terms, coarse_map, top, out):
    z_low, x_low = place[0] == 0, place[1] == 0
    total = terms[...] + zo[pl.ds(FACE, 8), :]
    sums = base[...]
    for at in range(4):
        sums = sums + top[:, at * 128 : (at + 1) * 128] * total[at : at + 1]
    sol = jnp.sum(sums, axis=1, keepdims=True)
    hit = lax.broadcasted_iota(jnp.int32, (128, 128), 0) == coarse_map[pl.ds(0, 1), :]
    out[...] = inner[...] + jnp.sum(jnp.where(hit, sol, 0.0), axis=0, keepdims=True)
    out[layer(7), :] += pick(z_low, ze, zo, 0, FACE)
    out[layer(0), :] += pick(z_low, zo, ze, 0, FACE)
    above = keep(place[3], pick(x_low, xe, xo, 0, FACE))
    below = keep(place[2], pick(x_low, xo, xe, 0, FACE))
    for k in range(8):
        out[pl.ds(k * 64 + 56, 8), :] += above[k * 8 : k * 8 + 8]
        out[pl.ds(k * 64, 8), :] += below[k * 8 : k * 8 + 8]


def move(value, axis, pairs):
    return lax.ppermute(value, axis, pairs)


def body(residual, margin, diag, basis, eigen, coarse_map, own, group, top):
    shape = residual.shape
    residual, margin, diag = (a.reshape(-1, 128) for a in (residual, margin, diag))
    basis, eigen = (a.reshape(-1, 1, 128) for a in (basis, eigen))
    coarse_map = coarse_map.reshape(1, 128)
    own, group, top = (a.reshape(128, -1) for a in (own, group, top))
    dom, coarse = lax.axis_index("dom"), lax.axis_index("coarse")
    doms, coarses = lax.axis_size("dom"), lax.axis_size("coarse")
    place = jnp.stack([dom % 2, coarse % 2, coarse > 0, coarse < coarses - 1]).astype(jnp.int32)
    z_even, z_odd = swap(doms, 1, 0), swap(doms, 1, 1)
    x_even, x_odd = swap(coarses, 1, 0), swap(coarses, 1, 1)
    inner_rows = (840, 160, 160)

    both = [(i, i ^ (coarses + 1)) for i in range(doms * coarses)]
    is_top = jnp.arange(8)[:, None] < 4
    held = [jax.ShapeDtypeStruct(a.shape, a.dtype) for a in (coarse_map, own, group, top)]

    zo, ze, xe, xo, w, c2, terms, own_part, coarse_map, own, group, top = call(
        first_kernel, [144, 136, 136, 128, 512, 512, 8, 8] + held, (512,) * 3,
        place, residual, margin, diag, coarse_map, own, group, top,
        in_hbm=range(1, 8), scratch=[pltpu.SemaphoreType.DMA((7,))], flops=300000,
    )
    azo, aze = move(zo, "dom", z_odd), move(ze, "dom", z_even)
    axe, axo = move(xe, "coarse", x_even), move(xo, "coarse", x_odd)
    across = move(terms, ("dom", "coarse"), both)
    work, ylow, yhigh, inverse, terms = call(
        own_kernel, inner_rows + (1040, 8), (128, 104), w, basis, eigen, terms, flops=20000000
    )
    terms = terms + axe[128:] + jnp.where(is_top, aze[128:] + across, 0.0)
    beside = move(terms, "coarse", swap(coarses, 4, 0))
    zo, ze, xo, xe, r, z_face, x_face = call(
        pass_kernel, (LINK + 8, LINK, 136, 128, 512, 128, 128), (FACE,) * 4 + inner_rows + (128,),
        place, w, c2, azo, aze, axo, axe, basis, work, ylow, yhigh, inverse,
    )
    terms = terms + beside
    zo, ze = move(zo, "dom", z_odd), move(ze, "dom", z_even)
    xo = move(lax.dynamic_update_slice(xo, terms, (128, 0)), "coarse", x_odd)
    xe = move(xe, "coarse", x_even)
    grouped = terms + xo[128:]
    terms = grouped + move(grouped, "dom", swap(doms, 4, 0))
    ro, re, terms = call(relay_kernel, (RELAY, RELAY, 8), (), place, zo, ze, terms, flops=1000)
    re, ro = move(re, "coarse", x_even), move(ro, "coarse", x_odd)
    beside = move(terms, "dom", swap(doms, 8, 0))
    first, work, ylow, yhigh, terms = call(
        second_own_kernel, (512,) + inner_rows + (8,), (512, 128), place, w, c2, r, zo, ze, xo, xe, basis, terms, flops=1000
    )
    terms = terms + beside
    beside = move(terms, "dom", swap(doms, 8, 1))
    co, ce, do, de, work, ylow, yhigh = call(
        second_pass_kernel, (FACE + 8, FACE, FACE, FACE) + inner_rows, (FACE,) * 4 + (128,) * 2,
        place, azo, aze, axo, axe, z_face, x_face, zo, ze, xo, xe, ro, re, basis, work, ylow, yhigh, inverse,
    )
    terms = terms + beside
    zo = move(lax.dynamic_update_slice(co, terms, (FACE, 0)), "dom", z_odd)
    ze = move(ce, "dom", z_even)
    xe, xo = move(de, "coarse", x_even), move(do, "coarse", x_odd)
    inner, base = call(
        inner_kernel, (512, 128), (128,), first, work, ylow, yhigh, basis, grouped, own_part, own, group, flops=1000
    )
    (out,) = call(last_kernel, (512,), (), place, inner, base, zo, ze, xo, xe, terms, coarse_map, top, flops=300000)
    return out.reshape(shape)


def solution(mesh):
    field = P(None, None, None, "dom", "coarse", None)
    factor = P("dom", "coarse", None, None)
    in_specs = (field, field, field, field, P(None, None, "dom", "coarse", None), P("dom", "coarse", None))
    in_specs = in_specs + (factor, factor, factor)
    return jax.shard_map(body, mesh=mesh, in_specs=in_specs, out_specs=field, check_vma=False)
```

time: 50.6 us -> 50.2 us (level)
  waiting for transfers between devices: 14.4 us -> 7.67 us
  starting transfers between devices: 25.6 us -> 30.9 us
    ppermute x16 -> x19, waiting for transfers between devices: 14.4 us -> 7.67 us  [move(): return lax.ppermute(value, axis, pairs)]
    ppermute x16 -> x19, starting transfers between devices: 25.6 us -> 30.9 us  [move(): return lax.ppermute(value, axis, pairs)]
    pallas_call x5 -> x8, Pallas kernels: 10.3 us -> 10.8 us  [call(): pl.pallas_call(kernel, out_shape=outs, in_specs=specs, out_specs=[VMEM] *...]
  transfers between devices with their start and end apart: 16 -> 19, of which waited for: 8 -> 5; matrix products, arithmetic and copies ran while one was open for 0% -> 0% of each run, Pallas kernels for 12% -> 15%
where the time goes in v4:
time: 50.2 us; the launch traced here: 49.7 us
  starting transfers between devices  30.9 us (62%)
  Pallas kernels  10.8 us (22%)
  waiting for transfers between devices  7.67 us (15%)
    ppermute x19, starting transfers between devices, move(): return lax.ppermute(value, axis, pairs)  30.9 us
    pallas_call x8, Pallas kernels, call(): pl.pallas_call(kernel, out_shape=outs, in_specs=specs, out_specs=[VMEM] *...  10.8 us
    ppermute x19, waiting for transfers between devices, move(): return lax.ppermute(value, axis, pairs)  7.67 us
  transfers between devices with their start and end apart: 19, of which 5 were waited for; matrix products, arithmetic and copies ran while one was open for 0% of the time, Pallas kernels for 15%

profile of v4, /device:TPU:1, one launch (start us, length us, event | category | flops | bytes accessed | tf_op | source)
XLA Modules:
  0.0 49.7 jit_solution(5742166649170973070)
XLA Ops:
  0.0 0.1 pad_add_fusion.place
  0.1 0.0 copy-start
  0.1 2.0 %shard_map.91 = (f32[144,128]{1,0:T(8,128)S(1)}, f32[136,128]{1,0:T(8,128)S(1)}, f32[136,128]{1,0:T(8,128)S(1)}, f32[128,128]{1,0:T(8,128)S(1)}, f32[512,128]{1,...) custom-call(s32[4]{0:T(128)S(1)} %pad_add_fusion.place, ...), custom_call_target="tpu_custom_call" | custom-call | flops 300000 | bytes 1000000 | tf_op jit(solution)/shard_map/pallas_call | solution.py:37
  2.1 0.0 copy-start.1
  2.1 2.1 %collective-permute-start.1 = (f32[136,128]{1,0:T(8,128)S(1)}, f32[136,128]{1,0:T(8,128)S(1)}, u32[]{:S(2)}, u32[]{:S(2)}) collective-permute-start(f32[136,128]{1,0:T(8,128)S(1)} %get-tuple-element.49), channel_id=1, source_target_pairs={{0,8},{8,0},{16,24},{24,16},{32,40},{40,32},{48,56},{56,48},{64,72... | collective-permute-start | bytes 208904 | tf_op jit(solution)/shard_map/ppermute | solution.py:362
  4.2 1.3 %collective-permute-start.3 = (f32[136,128]{1,0:T(8,128)S(1)}, f32[136,128]{1,0:T(8,128)S(1)}, u32[]{:S(2)}, u32[]{:S(2)}) collective-permute-start(f32[136,128]{1,0:T(8,128)S(1)} %get-tuple-element.51), channel_id=1, source_target_pairs={{0,1},{1,0},{2,3},{3,2},{4,5},{5,4},{6,7},{7,6},{8,9},{9,8},{10,11... | collective-permute-start | bytes 208904 | tf_op jit(solution)/shard_map/ppermute | solution.py:362
  5.5 1.5 %collective-permute-start.6 = (f32[8,128]{1,0:T(8,128)S(1)}, f32[8,128]{1,0:T(8,128)S(1)}, u32[]{:S(2)}, u32[]{:S(2)}) collective-permute-start(f32[8,128]{1,0:T(8,128)S(1)} %get-tuple-element.52.terms), channel_id=1, source_target_pairs={{0,9},{1,8},{2,11},{3,10},{4,13},{5,12},{6,15},{7,14},{8,1},{9,0},... | collective-permute-start | bytes 12296 | tf_op jit(solution)/shard_map/ppermute | solution.py:362
  7.0 6.0 %collective-permute-start = (f32[144,128]{1,0:T(8,128)S(1)}, f32[144,128]{1,0:T(8,128)S(1)}, u32[]{:S(2)}, u32[]{:S(2)}) collective-permute-start(f32[144,128]{1,0:T(8,128)S(1)} %get-tuple-element.48), channel_id=1, source_target_pairs={{8,16},{16,8},{24,32},{32,24},{40,48},{48,40},{56,64},{64,56},{72,... | collective-permute-start | bytes 221192 | tf_op jit(solution)/shard_map/ppermute | solution.py:362
  13.1 2.0 %collective-permute-start.2 = (f32[128,128]{1,0:T(8,128)S(1)}, f32[128,128]{1,0:T(8,128)S(1)}, u32[]{:S(2)}, u32[]{:S(2)}) collective-permute-start(f32[128,128]{1,0:T(8,128)S(1)} %get-tuple-element.50), channel_id=1, source_target_pairs={{1,2},{2,1},{3,4},{4,3},{5,6},{6,5},{7,0},{0,7},{9,10},{10,9},{11,... | collective-permute-start | bytes 196616 | tf_op jit(solution)/shard_map/ppermute | solution.py:362
  15.1 0.0 copy-done
  15.1 0.0 copy-done.1
  15.1 0.5 %shard_map.92 = (f32[840,128]{1,0:T(8,128)S(1)}, f32[160,128]{1,0:T(8,128)S(1)}, f32[160,128]{1,0:T(8,128)S(1)}, f32[1040,128]{1,0:T(8,128)S(1)}, f32[8,128]{1,0:T(8,128)S(1)}) custom-call(f32[512,128]{1,0:T(8,128)S(1)} %get-tuple-element.46.w, f32[300,1,128]{2,1,0:T(1,128)S(1)} %bitcast.16, f32[30,1,128]{2,1,0:T(1,128)S(1)} %bitcast.21, ...), custom_call_target="tpu_custom_call" | custom-call | flops 20000000 | bytes 1000000 | tf_op jit(solution)/shard_map/pallas_call | solution.py:37
  15.6 0.0 collective-permute-done.6
  15.6 0.0 collective-permute-done.1.aze
  15.6 0.0 collective-permute-done.3.axe
  15.6 0.1 fusion.1
  15.7 2.6 %collective-permute-start.7 = (f32[8,128]{1,0:T(8,128)S(1)}, f32[8,128]{1,0:T(8,128)S(1)}, u32[]{:S(2)}, u32[]{:S(2)}) collective-permute-start(f32[8,128]{1,0:T(8,128)S(1)} %fusion.1), channel_id=1, source_target_pairs={{0,4},{1,5},{2,6},{3,7},{4,0},{5,1},{6,2},{7,3},{8,12},{9,13},{10,... | collective-permute-start | bytes 12296 | tf_op jit(solution)/shard_map/ppermute | solution.py:362
  18.3 0.0 collective-permute-done.2.axo
  18.3 0.0 collective-permute-done.azo
  18.3 2.7 %shard_map.93 = (f32[152,128]{1,0:T(8,128)S(1)}, f32[144,128]{1,0:T(8,128)S(1)}, f32[136,128]{1,0:T(8,128)S(1)}, f32[128,128]{1,0:T(8,128)S(1)}, f32[512,128]{1,...) custom-call(s32[4]{0:T(128)S(1)} %pad_add_fusion.place, f32[512,128]{1,0:T(8,128)S(1)} %get-tuple-element.46.w, ...), custom_call_target="tpu_custom_call" | custom-call | flops 15360000 | bytes 1000000 | tf_op jit(solution)/shard_map/pallas_call | solution.py:37
  21.0 0.0 collective-permute-done.7
  21.1 0.5 collective-permute-start.8
  21.6 3.7 %collective-permute-start.4 = (f32[152,128]{1,0:T(8,128)S(1)}, f32[152,128]{1,0:T(8,128)S(1)}, u32[]{:S(2)}, u32[]{:S(2)}) collective-permute-start(f32[152,128]{1,0:T(8,128)S(1)} %get-tuple-element.58), channel_id=1, source_target_pairs={{8,16},{16,8},{24,32},{32,24},{40,48},{48,40},{56,64},{64,56},{72,... | collective-permute-start | bytes 233480 | tf_op jit(solution)/shard_map/ppermute | solution.py:362
  25.3 0.0 collective-permute-start.5
  25.3 0.6 %collective-permute-start.9 = (f32[128,128]{1,0:T(8,128)S(1)}, f32[128,128]{1,0:T(8,128)S(1)}, u32[]{:S(2)}, u32[]{:S(2)}) collective-permute-start(f32[128,128]{1,0:T(8,128)S(1)} %get-tuple-element.62), channel_id=1, source_target_pairs={{0,1},{1,0},{2,3},{3,2},{4,5},{5,4},{6,7},{7,6},{8,9},{9,8},{10,11... | collective-permute-start | bytes 196616 | tf_op jit(solution)/shard_map/ppermute | solution.py:362
  25.8 0.0 collective-permute-done.8.xo
  25.8 0.0 collective-permute-start.10
  25.8 2.5 %collective-permute-done.10 = f32[8,128]{1,0:T(8,128)S(1)} collective-permute-done((f32[8,128]{1,0:T(8,128)S(1)}, f32[8,128]{1,0:T(8,128)S(1)}, u32[]{:S(2)}, u32[]{:S(2)}) %collective-permute-start.10) | collective-permute-done | bytes 4128 | tf_op jit(solution)/shard_map/ppermute | solution.py:362
  28.3 0.2 collective-permute-done.5.ze
  28.5 0.0 collective-permute-done.4.zo
  28.5 0.6 %shard_map.94 = (f32[32,128]{1,0:T(8,128)S(1)}, f32[32,128]{1,0:T(8,128)S(1)}, f32[8,128]{1,0:T(8,128)S(1)}) custom-call(s32[4]{0:T(128)S(1)} %pad_add_fusion.place, f32[152,128]{1,0:T(8,128)S(1)} %collective-permute-done.4.zo, f32[144,128]{1,0:T(8,128)S(1)} %collective-permute-done.5.ze, f32[8,128]{1,0:T(8,128)S(1)} %add.38.terms), custom_call_target="tpu_custom_call" | custom-call | flops 1000 | bytes 1000000 | tf_op jit(solution)/shard_map/pallas_call | solution.py:37
  29.0 2.5 %collective-permute-start.11 = (f32[32,128]{1,0:T(8,128)S(1)}, f32[32,128]{1,0:T(8,128)S(1)}, u32[]{:S(2)}, u32[]{:S(2)}) collective-permute-start(f32[32,128]{1,0:T(8,128)S(1)} %get-tuple-element.67), channel_id=1, source_target_pairs={{1,2},{2,1},{3,4},{4,3},{5,6},{6,5},{7,0},{0,7},{9,10},{10,9},{11,... | collective-permute-start | bytes 49160 | tf_op jit(solution)/shard_map/ppermute | solution.py:362
  31.5 0.9 %collective-permute-start.12 = (f32[32,128]{1,0:T(8,128)S(1)}, f32[32,128]{1,0:T(8,128)S(1)}, u32[]{:S(2)}, u32[]{:S(2)}) collective-permute-start(f32[32,128]{1,0:T(8,128)S(1)} %get-tuple-element.68), channel_id=1, source_target_pairs={{0,1},{1,0},{2,3},{3,2},{4,5},{5,4},{6,7},{7,6},{8,9},{9,8},{10,11... | collective-permute-start | bytes 49160 | tf_op jit(solution)/shard_map/ppermute | solution.py:362
  32.4 0.0 collective-permute-start.13
  32.4 0.0 collective-permute-done.9.xe
  32.4 1.0 %shard_map.95 = (f32[512,128]{1,0:T(8,128)S(1)}, f32[840,128]{1,0:T(8,128)S(1)}, f32[160,128]{1,0:T(8,128)S(1)}, f32[160,128]{1,0:T(8,128)S(1)}, f32[8,128]{1,0:T(8,128)S(1)}) custom-call(s32[4]{0:T(128)S(1)} %pad_add_fusion.place, f32[512,128]{1,0:T(8,128)S(1)} %get-tuple-element.46.w, f32[512,128]{1,0:T(8,128)S(1)} %get-tuple-element.47.c2, ...), custom_call_target="tpu_custom_call" | custom-call | flops 1000 | bytes 1000000 | tf_op jit(solution)/shard_map/pallas_call | solution.py:37
  33.4 2.4 %collective-permute-done.13 = f32[8,128]{1,0:T(8,128)S(1)} collective-permute-done((f32[8,128]{1,0:T(8,128)S(1)}, f32[8,128]{1,0:T(8,128)S(1)}, u32[]{:S(2)}, u32[]{:S(2)}) %collective-permute-start.13) | collective-permute-done | bytes 4128 | tf_op jit(solution)/shard_map/ppermute | solution.py:362
  35.8 1.1 %collective-permute-start.14 = (f32[8,128]{1,0:T(8,128)S(1)}, f32[8,128]{1,0:T(8,128)S(1)}, u32[]{:S(2)}, u32[]{:S(2)}) collective-permute-start(f32[8,128]{1,0:T(8,128)S(1)} %add.39), channel_id=1, source_target_pairs={{64,128},{72,136},{80,144},{88,152},{96,160},{104,168},{112,176},{... | collective-permute-start | bytes 12296 | tf_op jit(solution)/shard_map/ppermute | solution.py:362
  36.8 0.0 collective-permute-done.11.ro
  36.8 0.0 collective-permute-done.12.re
  36.8 2.3 %shard_map.96 = (f32[72,128]{1,0:T(8,128)S(1)}, f32[64,128]{1,0:T(8,128)S(1)}, f32[64,128]{1,0:T(8,128)S(1)}, f32[64,128]{1,0:T(8,128)S(1)}, f32[840,128]{1,0:T(...) custom-call(s32[4]{0:T(128)S(1)} %pad_add_fusion.place, f32[144,128]{1,0:T(8,128)S(1)} %collective-permute-done.azo, ...), custom_call_target="tpu_custom_call" | custom-call | flops 15360000 | bytes 1000000 | tf_op jit(solution)/shard_map/pallas_call | solution.py:37
  39.1 1.2 %collective-permute-done.14 = f32[8,128]{1,0:T(8,128)S(1)} collective-permute-done((f32[8,128]{1,0:T(8,128)S(1)}, f32[8,128]{1,0:T(8,128)S(1)}, u32[]{:S(2)}, u32[]{:S(2)}) %collective-permute-start.14) | collective-permute-done | bytes 4128 | tf_op jit(solution)/shard_map/ppermute | solution.py:362
  40.3 2.3 %collective-permute-start.15 = (f32[72,128]{1,0:T(8,128)S(1)}, f32[72,128]{1,0:T(8,128)S(1)}, u32[]{:S(2)}, u32[]{:S(2)}) collective-permute-start(f32[72,128]{1,0:T(8,128)S(1)} %get-tuple-element.87), channel_id=1, source_target_pairs={{8,16},{16,8},{24,32},{32,24},{40,48},{48,40},{56,64},{64,56},{72,... | collective-permute-start | bytes 110600 | tf_op jit(solution)/shard_map/ppermute | solution.py:362
  42.6 0.0 collective-permute-start.16
  42.6 3.8 %collective-permute-start.17 = (f32[64,128]{1,0:T(8,128)S(1)}, f32[64,128]{1,0:T(8,128)S(1)}, u32[]{:S(2)}, u32[]{:S(2)}) collective-permute-start(f32[64,128]{1,0:T(8,128)S(1)} %get-tuple-element.83), channel_id=1, source_target_pairs={{1,2},{2,1},{3,4},{4,3},{5,6},{6,5},{7,0},{0,7},{9,10},{10,9},{11,... | collective-permute-start | bytes 98312 | tf_op jit(solution)/shard_map/ppermute | solution.py:362
  46.4 0.0 collective-permute-start.18
  46.4 0.4 shard_map.97
  46.9 0.0 collective-permute-done.16.ze
  46.9 1.5 %collective-permute-done.17.xo = f32[64,128]{1,0:T(8,128)S(1)} collective-permute-done((f32[64,128]{1,0:T(8,128)S(1)}, f32[64,128]{1,0:T(8,128)S(1)}, u32[]{:S(2)}, u32[]{:S(2)}) %collective-permute-start.17) | collective-permute-done | bytes 32800 | tf_op jit(solution)/shard_map/ppermute | solution.py:362
  48.3 0.0 collective-permute-done.18.xe
  48.3 0.0 collective-permute-done.15.zo
  48.3 1.4 %shard_map.98 = f32[512,128]{1,0:T(8,128)} custom-call(s32[4]{0:T(128)S(1)} %pad_add_fusion.place, f32[512,128]{1,0:T(8,128)S(1)} %get-tuple-element.78.inner, f32[128,128]{1,0:T(8,128)S(1)} %get-tuple-element.79.base, f32[72,128]{1,0:T(8,128)S(1)} %collective-permute-done.15.zo, f32[64,128]{1,0:T(8,128)S(1)} %collective-permute-done.16.ze, ...), custom_call_target="tpu_custom_call" | custom-call | flops 300000 | bytes 1000000 | tf_op jit(solution)/shard_map/pallas_call | solution.py:37
  (6 shorter events, 0.0 us)
Async XLA Ops:
  0.1 15.0 %copy-start = (f32[3,10,10,1,1,128]{5,4,3,2,1,0:T(1,128)S(1)}, f32[3,10,10,1,1,128]{5,4,3,2,1,0:T(1,128)}, u32[]{:S(2)}) copy-start(f32[3,10,10,1,1,128]{5,4,3,2,1,0:T(1,128)} %param.12) | copy-start | bytes 460804
  2.1 13.0 %copy-start.1 = (f32[3,10,1,1,128]{4,3,2,1,0:T(1,128)S(1)}, f32[3,10,1,1,128]{4,3,2,1,0:T(1,128)}, u32[]{:S(2)}) copy-start(f32[3,10,1,1,128]{4,3,2,1,0:T(1,128)} %param.13) | copy-start | bytes 46084
  2.1 13.5 %collective-permute-start.1 = (f32[136,128]{1,0:T(8,128)S(1)}, f32[136,128]{1,0:T(8,128)S(1)}, u32[]{:S(2)}, u32[]{:S(2)}) collective-permute-start(f32[136,128]{1,0:T(8,128)S(1)} %get-tuple-element.49), channel_id=1, source_target_pairs={{0,8},{8,0},{16,24},{24,16},{32,40},{40,32},{48,56},{56,48},{64,72... | collective-permute-start | bytes 208904 | tf_op jit(solution)/shard_map/ppermute | solution.py:362
  4.2 11.4 %collective-permute-start.3 = (f32[136,128]{1,0:T(8,128)S(1)}, f32[136,128]{1,0:T(8,128)S(1)}, u32[]{:S(2)}, u32[]{:S(2)}) collective-permute-start(f32[136,128]{1,0:T(8,128)S(1)} %get-tuple-element.51), channel_id=1, source_target_pairs={{0,1},{1,0},{2,3},{3,2},{4,5},{5,4},{6,7},{7,6},{8,9},{9,8},{10,11... | collective-permute-start | bytes 208904 | tf_op jit(solution)/shard_map/ppermute | solution.py:362
  5.5 10.1 %collective-permute-start.6 = (f32[8,128]{1,0:T(8,128)S(1)}, f32[8,128]{1,0:T(8,128)S(1)}, u32[]{:S(2)}, u32[]{:S(2)}) collective-permute-start(f32[8,128]{1,0:T(8,128)S(1)} %get-tuple-element.52.terms), channel_id=1, source_target_pairs={{0,9},{1,8},{2,11},{3,10},{4,13},{5,12},{6,15},{7,14},{8,1},{9,0},... | collective-permute-start | bytes 12296 | tf_op jit(solution)/shard_map/ppermute | solution.py:362
  7.0 11.3 %collective-permute-start = (f32[144,128]{1,0:T(8,128)S(1)}, f32[144,128]{1,0:T(8,128)S(1)}, u32[]{:S(2)}, u32[]{:S(2)}) collective-permute-start(f32[144,128]{1,0:T(8,128)S(1)} %get-tuple-element.48), channel_id=1, source_target_pairs={{8,16},{16,8},{24,32},{32,24},{40,48},{48,40},{56,64},{64,56},{72,... | collective-permute-start | bytes 221192 | tf_op jit(solution)/shard_map/ppermute | solution.py:362
  13.1 5.3 %collective-permute-start.2 = (f32[128,128]{1,0:T(8,128)S(1)}, f32[128,128]{1,0:T(8,128)S(1)}, u32[]{:S(2)}, u32[]{:S(2)}) collective-permute-start(f32[128,128]{1,0:T(8,128)S(1)} %get-tuple-element.50), channel_id=1, source_target_pairs={{1,2},{2,1},{3,4},{4,3},{5,6},{6,5},{7,0},{0,7},{9,10},{10,9},{11,... | collective-permute-start | bytes 196616 | tf_op jit(solution)/shard_map/ppermute | solution.py:362
  15.7 5.4 %collective-permute-start.7 = (f32[8,128]{1,0:T(8,128)S(1)}, f32[8,128]{1,0:T(8,128)S(1)}, u32[]{:S(2)}, u32[]{:S(2)}) collective-permute-start(f32[8,128]{1,0:T(8,128)S(1)} %fusion.1), channel_id=1, source_target_pairs={{0,4},{1,5},{2,6},{3,7},{4,0},{5,1},{6,2},{7,3},{8,12},{9,13},{10,... | collective-permute-start | bytes 12296 | tf_op jit(solution)/shard_map/ppermute | solution.py:362
  21.1 4.8 %collective-permute-start.8 = (f32[136,128]{1,0:T(8,128)S(1)}, f32[136,128]{1,0:T(8,128)S(1)}, u32[]{:S(2)}, u32[]{:S(2)}) collective-permute-start(f32[136,128]{1,0:T(8,128)S(1)} %get-tuple-element.89), channel_id=1, source_target_pairs={{1,2},{2,1},{3,4},{4,3},{5,6},{6,5},{7,0},{0,7},{9,10},{10,9},{11,... | collective-permute-start | bytes 208904 | tf_op jit(solution)/shard_map/ppermute | solution.py:362
  21.6 6.9 %collective-permute-start.4 = (f32[152,128]{1,0:T(8,128)S(1)}, f32[152,128]{1,0:T(8,128)S(1)}, u32[]{:S(2)}, u32[]{:S(2)}) collective-permute-start(f32[152,128]{1,0:T(8,128)S(1)} %get-tuple-element.58), channel_id=1, source_target_pairs={{8,16},{16,8},{24,32},{32,24},{40,48},{48,40},{56,64},{64,56},{72,... | collective-permute-start | bytes 233480 | tf_op jit(solution)/shard_map/ppermute | solution.py:362
  25.3 3.2 %collective-permute-start.5 = (f32[144,128]{1,0:T(8,128)S(1)}, f32[144,128]{1,0:T(8,128)S(1)}, u32[]{:S(2)}, u32[]{:S(2)}) collective-permute-start(f32[144,128]{1,0:T(8,128)S(1)} %get-tuple-element.59), channel_id=1, source_target_pairs={{0,8},{8,0},{16,24},{24,16},{32,40},{40,32},{48,56},{56,48},{64,72... | collective-permute-start | bytes 221192 | tf_op jit(solution)/shard_map/ppermute | solution.py:362
  25.3 7.1 %collective-permute-start.9 = (f32[128,128]{1,0:T(8,128)S(1)}, f32[128,128]{1,0:T(8,128)S(1)}, u32[]{:S(2)}, u32[]{:S(2)}) collective-permute-start(f32[128,128]{1,0:T(8,128)S(1)} %get-tuple-element.62), channel_id=1, source_target_pairs={{0,1},{1,0},{2,3},{3,2},{4,5},{5,4},{6,7},{7,6},{8,9},{9,8},{10,11... | collective-permute-start | bytes 196616 | tf_op jit(solution)/shard_map/ppermute | solution.py:362
  25.8 2.5 %collective-permute-start.10 = (f32[8,128]{1,0:T(8,128)S(1)}, f32[8,128]{1,0:T(8,128)S(1)}, u32[]{:S(2)}, u32[]{:S(2)}) collective-permute-start(f32[8,128]{1,0:T(8,128)S(1)} %slice_add_fusion.grouped), channel_id=1, source_target_pairs={{0,32},{8,40},{16,48},{24,56},{32,0},{40,8},{48,16},{56,24},{64,96... | collective-permute-start | bytes 12296 | tf_op jit(solution)/shard_map/ppermute | solution.py:362
  29.0 7.8 %collective-permute-start.11 = (f32[32,128]{1,0:T(8,128)S(1)}, f32[32,128]{1,0:T(8,128)S(1)}, u32[]{:S(2)}, u32[]{:S(2)}) collective-permute-start(f32[32,128]{1,0:T(8,128)S(1)} %get-tuple-element.67), channel_id=1, source_target_pairs={{1,2},{2,1},{3,4},{4,3},{5,6},{6,5},{7,0},{0,7},{9,10},{10,9},{11,... | collective-permute-start | bytes 49160 | tf_op jit(solution)/shard_map/ppermute | solution.py:362
  31.5 5.4 %collective-permute-start.12 = (f32[32,128]{1,0:T(8,128)S(1)}, f32[32,128]{1,0:T(8,128)S(1)}, u32[]{:S(2)}, u32[]{:S(2)}) collective-permute-start(f32[32,128]{1,0:T(8,128)S(1)} %get-tuple-element.68), channel_id=1, source_target_pairs={{0,1},{1,0},{2,3},{3,2},{4,5},{5,4},{6,7},{7,6},{8,9},{9,8},{10,11... | collective-permute-start | bytes 49160 | tf_op jit(solution)/shard_map/ppermute | solution.py:362
  32.4 3.4 %collective-permute-start.13 = (f32[8,128]{1,0:T(8,128)S(1)}, f32[8,128]{1,0:T(8,128)S(1)}, u32[]{:S(2)}, u32[]{:S(2)}) collective-permute-start(f32[8,128]{1,0:T(8,128)S(1)} %get-tuple-element.63.terms), channel_id=1, source_target_pairs={{0,64},{8,72},{16,80},{24,88},{32,96},{40,104},{48,112},{56,120},{... | collective-permute-start | bytes 12296 | tf_op jit(solution)/shard_map/ppermute | solution.py:362
  35.8 4.6 %collective-permute-start.14 = (f32[8,128]{1,0:T(8,128)S(1)}, f32[8,128]{1,0:T(8,128)S(1)}, u32[]{:S(2)}, u32[]{:S(2)}) collective-permute-start(f32[8,128]{1,0:T(8,128)S(1)} %add.39), channel_id=1, source_target_pairs={{64,128},{72,136},{80,144},{88,152},{96,160},{104,168},{112,176},{... | collective-permute-start | bytes 12296 | tf_op jit(solution)/shard_map/ppermute | solution.py:362
  40.3 8.0 %collective-permute-start.15 = (f32[72,128]{1,0:T(8,128)S(1)}, f32[72,128]{1,0:T(8,128)S(1)}, u32[]{:S(2)}, u32[]{:S(2)}) collective-permute-start(f32[72,128]{1,0:T(8,128)S(1)} %get-tuple-element.87), channel_id=1, source_target_pairs={{8,16},{16,8},{24,32},{32,24},{40,48},{48,40},{56,64},{64,56},{72,... | collective-permute-start | bytes 110600 | tf_op jit(solution)/shard_map/ppermute | solution.py:362
  42.6 4.3 %collective-permute-start.16 = (f32[64,128]{1,0:T(8,128)S(1)}, f32[64,128]{1,0:T(8,128)S(1)}, u32[]{:S(2)}, u32[]{:S(2)}) collective-permute-start(f32[64,128]{1,0:T(8,128)S(1)} %get-tuple-element.82), channel_id=1, source_target_pairs={{0,8},{8,0},{16,24},{24,16},{32,40},{40,32},{48,56},{56,48},{64,72... | collective-permute-start | bytes 98312 | tf_op jit(solution)/shard_map/ppermute | solution.py:362
  42.6 5.7 %collective-permute-start.17 = (f32[64,128]{1,0:T(8,128)S(1)}, f32[64,128]{1,0:T(8,128)S(1)}, u32[]{:S(2)}, u32[]{:S(2)}) collective-permute-start(f32[64,128]{1,0:T(8,128)S(1)} %get-tuple-element.83), channel_id=1, source_target_pairs={{1,2},{2,1},{3,4},{4,3},{5,6},{6,5},{7,0},{0,7},{9,10},{10,9},{11,... | collective-permute-start | bytes 98312 | tf_op jit(solution)/shard_map/ppermute | solution.py:362
  46.4 1.9 %collective-permute-start.18 = (f32[64,128]{1,0:T(8,128)S(1)}, f32[64,128]{1,0:T(8,128)S(1)}, u32[]{:S(2)}, u32[]{:S(2)}) collective-permute-start(f32[64,128]{1,0:T(8,128)S(1)} %get-tuple-element.84), channel_id=1, source_target_pairs={{0,1},{1,0},{2,3},{3,2},{4,5},{5,4},{6,7},{7,6},{8,9},{9,8},{10,11... | collective-permute-start | bytes 98312 | tf_op jit(solution)/shard_map/ppermute | solution.py:362

commit v5 on v4

--- a/solution.py
+++ b/solution.py
@@ -11,6 +11,12 @@
 LINK = 144
 RELAY = 32
 VMEM = pl.BlockSpec(memory_space=pltpu.VMEM)
+
+
+def where_am_i():
+    dom, coarse = lax.axis_index("dom"), lax.axis_index("coarse")
+    last = lax.axis_size("coarse") - 1
+    return dom % 2, coarse % 2, (coarse > 0).astype(jnp.int32), (coarse < last).astype(jnp.int32)
 
 
 def swap(length, stride, odd):
@@ -29,7 +35,7 @@
 
 def call(kernel, outs, scratch_rows, *args, in_hbm=(), scratch=(), flops=2 * 60000 * 128):
     outs = [jax.ShapeDtypeStruct((out, 128), F32) if isinstance(out, int) else out for out in outs]
-    specs = [pl.BlockSpec(memory_space=pltpu.SMEM) if a.ndim == 1 else VMEM for a in args]
+    specs = [VMEM] * len(args)
     args = list(args)
     for at in in_hbm:
         specs[at] = pl.BlockSpec(memory_space=pltpu.HBM)
@@ -203,9 +209,10 @@
 
 
 def first_kernel(
-    place, residual_hbm, margin_hbm, diag_hbm, map_hbm, own_hbm, group_hbm, top_hbm,
+    residual_hbm, margin_hbm, diag_hbm, map_hbm, own_hbm, group_hbm, top_hbm,
     zo, ze, xe, xo, w, c2, terms, own_part, coarse_map, own, group, top, residual, margin, diag, sems
 ):
+    place = where_am_i()
     sources = (residual_hbm, margin_hbm, diag_hbm, map_hbm, own_hbm, group_hbm, top_hbm)
     targets = (residual, margin, diag, coarse_map, own, group, top)
     copies = [pltpu.make_async_copy(a, b, sems.at[at]) for at, (a, b) in enumerate(zip(sources, targets))]
@@ -253,9 +260,10 @@
 
 
 def pass_kernel(
-    place, w, c2, azo, aze, axo, axe, basis, work_in, ylow_in, yhigh_in, inverse,
+    w, c2, azo, aze, axo, axe, basis, work_in, ylow_in, yhigh_in, inverse,
     zo, ze, xo, xe, r, z_face, x_face, zl, zh, xl, xh, work, ylow, yhigh, plane
 ):
+    place = where_am_i()
     z_low, x_low = place[0] == 0, place[1] == 0
     zh[...] = pick(z_low, aze, azo, 0, FACE)
     zl[...] = pick(z_low, azo, aze, 0, FACE)
@@ -278,7 +286,8 @@
             message[pl.ds(FACE + k * 8, 8), :] = w[here, :] - c2[here, :] * r[here, :]
 
 
-def relay_kernel(place, zo, ze, terms, ro, re, same):
+def relay_kernel(zo, ze, terms, ro, re, same):
+    place = where_am_i()
     same[...] = terms[...]
     z_low = place[0] == 0
     for message, up in ((ro, place[1]), (re, 1 - place[1])):
@@ -290,7 +299,8 @@
         message[pl.ds(24, 8), :] = jnp.where(z_low, ze[line, :], zo[line, :])
 
 
-def second_own_kernel(place, w, c2, r, zo, ze, xo, xe, basis, terms, first, work, ylow, yhigh, same, field, plane):
+def second_own_kernel(w, c2, r, zo, ze, xo, xe, basis, terms, first, work, ylow, yhigh, same, field, plane):
+    place = where_am_i()
     same[...] = terms[...]
     z_low, x_low = place[0] == 0, place[1] == 0
     first[...] = r[...]
@@ -306,9 +316,10 @@
 
 
 def second_pass_kernel(
-    place, azo, aze, axo, axe, z_face, x_face, zo, ze, xo, xe, ro, re, basis, work_in, ylow_in, yhigh_in, inverse,
+    azo, aze, axo, axe, z_face, x_face, zo, ze, xo, xe, ro, re, basis, work_in, ylow_in, yhigh_in, inverse,
     co, ce, do, de, work, ylow, yhigh, zl, zh, xl, xh, s_face, t_face
 ):
+    place = where_am_i()
     z_low, x_low = place[0] == 0, place[1] == 0
     above = keep(place[3], pick(x_low, re, ro, 0, RELAY))
     below = keep(place[2], pick(x_low, ro, re, 0, RELAY))
@@ -340,7 +351,8 @@
     base[...] = sums
 
 
-def last_kernel(place, inner, base, zo, ze, xo, xe, terms, coarse_map, top, out):
+def last_kernel(inner, base, zo, ze, xo, xe, terms, coarse_map, top, out):
+    place = where_am_i()
     z_low, x_low = place[0] == 0, place[1] == 0
     total = terms[...] + zo[pl.ds(FACE, 8), :]
     sums = base[...]
@@ -368,9 +380,7 @@
     basis, eigen = (a.reshape(-1, 1, 128) for a in (basis, eigen))
     coarse_map = coarse_map.reshape(1, 128)
     own, group, top = (a.reshape(128, -1) for a in (own, group, top))
-    dom, coarse = lax.axis_index("dom"), lax.axis_index("coarse")
     doms, coarses = lax.axis_size("dom"), lax.axis_size("coarse")
-    place = jnp.stack([dom % 2, coarse % 2, coarse > 0, coarse < coarses - 1]).astype(jnp.int32)
     z_even, z_odd = swap(doms, 1, 0), swap(doms, 1, 1)
     x_even, x_odd = swap(coarses, 1, 0), swap(coarses, 1, 1)
     inner_rows = (840, 160, 160)
@@ -381,8 +391,8 @@
 
     zo, ze, xe, xo, w, c2, terms, own_part, coarse_map, own, group, top = call(
         first_kernel, [144, 136, 136, 128, 512, 512, 8, 8] + held, (512,) * 3,
-        place, residual, margin, diag, coarse_map, own, group, top,
-        in_hbm=range(1, 8), scratch=[pltpu.SemaphoreType.DMA((7,))], flops=300000,
+        residual, margin, diag, coarse_map, own, group, top,
+        in_hbm=range(7), scratch=[pltpu.SemaphoreType.DMA((7,))], flops=300000,
     )
     azo, aze = move(zo, "dom", z_odd), move(ze, "dom", z_even)
     axe, axo = move(xe, "coarse", x_even), move(xo, "coarse", x_odd)
@@ -394,7 +404,7 @@
     beside = move(terms, "coarse", swap(coarses, 4, 0))
     zo, ze, xo, xe, r, z_face, x_face = call(
         pass_kernel, (LINK + 8, LINK, 136, 128, 512, 128, 128), (FACE,) * 4 + inner_rows + (128,),
-        place, w, c2, azo, aze, axo, axe, basis, work, ylow, yhigh, inverse,
+        w, c2, azo, aze, axo, axe, basis, work, ylow, yhigh, inverse,
     )
     terms = terms + beside
     zo, ze = move(zo, "dom", z_odd), move(ze, "dom", z_even)
@@ -402,17 +412,17 @@
     xe = move(xe, "coarse", x_even)
     grouped = terms + xo[128:]
     terms = grouped + move(grouped, "dom", swap(doms, 4, 0))
-    ro, re, terms = call(relay_kernel, (RELAY, RELAY, 8), (), place, zo, ze, terms, flops=1000)
+    ro, re, terms = call(relay_kernel, (RELAY, RELAY, 8), (), zo, ze, terms, flops=1000)
     re, ro = move(re, "coarse", x_even), move(ro, "coarse", x_odd)
     beside = move(terms, "dom", swap(doms, 8, 0))
     first, work, ylow, yhigh, terms = call(
-        second_own_kernel, (512,) + inner_rows + (8,), (512, 128), place, w, c2, r, zo, ze, xo, xe, basis, terms, flops=1000
+        second_own_kernel, (512,) + inner_rows + (8,), (512, 128), w, c2, r, zo, ze, xo, xe, basis, terms, flops=1000
     )
     terms = terms + beside
     beside = move(terms, "dom", swap(doms, 8, 1))
     co, ce, do, de, work, ylow, yhigh = call(
         second_pass_kernel, (FACE + 8, FACE, FACE, FACE) + inner_rows, (FACE,) * 4 + (128,) * 2,
-        place, azo, aze, axo, axe, z_face, x_face, zo, ze, xo, xe, ro, re, basis, work, ylow, yhigh, inverse,
+        azo, aze, axo, axe, z_face, x_face, zo, ze, xo, xe, ro, re, basis, work, ylow, yhigh, inverse,
     )
     terms = terms + beside
     zo = move(lax.dynamic_update_slice(co, terms, (FACE, 0)), "dom", z_odd)
@@ -421,7 +431,7 @@
     inner, base = call(
         inner_kernel, (512, 128), (128,), first, work, ylow, yhigh, basis, grouped, own_part, own, group, flops=1000
     )
-    (out,) = call(last_kernel, (512,), (), place, inner, base, zo, ze, xo, xe, terms, coarse_map, top, flops=300000)
+    (out,) = call(last_kernel, (512,), (), inner, base, zo, ze, xo, xe, terms, coarse_map, top, flops=300000)
     return out.reshape(shape)
 
 

time: 50.2 us -> 49.2 us (0.980)
  the two profiles are of different devices: /device:TPU:1 before, /device:TPU:2 now
where the time goes in v5:
time: 49.2 us; the launch traced here: 49.1 us
  starting transfers between devices  27.2 us (55%)
  waiting for transfers between devices  13.9 us (28%)
  Pallas kernels  7.74 us (16%)
    ppermute x19, starting transfers between devices, move(): return lax.ppermute(value, axis, pairs)  27.2 us
    ppermute x19, waiting for transfers between devices, move(): return lax.ppermute(value, axis, pairs)  13.9 us
    pallas_call x8, Pallas kernels, call(): pl.pallas_call(kernel, out_shape=outs, in_specs=specs, out_specs=[VMEM] *...  7.74 us
  transfers between devices with their start and end apart: 19, of which 7 were waited for; matrix products, arithmetic and copies ran while one was open for 0% of the time, Pallas kernels for 11%

profile of v5, /device:TPU:2, one launch (start us, length us, event | category | flops | bytes accessed | tf_op | source)
XLA Modules:
  0.0 49.1 jit_solution(1598826800728958258)
XLA Ops:
  0.0 0.0 copy-start
  0.0 1.5 %shard_map.91 = (f32[144,128]{1,0:T(8,128)S(1)}, f32[136,128]{1,0:T(8,128)S(1)}, f32[136,128]{1,0:T(8,128)S(1)}, f32[128,128]{1,0:T(8,128)S(1)}, f32[512,128]{1,...) custom-call(f32[512,128]{1,0:T(8,128)} %bitcast.18, ...), custom_call_target="tpu_custom_call" | custom-call | flops 300000 | bytes 1000000 | tf_op jit(solution)/shard_map/pallas_call | solution.py:43
  1.5 0.0 copy-start.1
  1.5 2.4 %collective-permute-start.1 = (f32[136,128]{1,0:T(8,128)S(1)}, f32[136,128]{1,0:T(8,128)S(1)}, u32[]{:S(2)}, u32[]{:S(2)}) collective-permute-start(f32[136,128]{1,0:T(8,128)S(1)} %get-tuple-element.49), channel_id=1, source_target_pairs={{0,8},{8,0},{16,24},{24,16},{32,40},{40,32},{48,56},{56,48},{64,72... | collective-permute-start | bytes 208904 | tf_op jit(solution)/shard_map/ppermute | solution.py:374
  3.9 0.0 collective-permute-start.3
  3.9 0.4 collective-permute-start
  4.3 2.8 %collective-permute-start.2 = (f32[128,128]{1,0:T(8,128)S(1)}, f32[128,128]{1,0:T(8,128)S(1)}, u32[]{:S(2)}, u32[]{:S(2)}) collective-permute-start(f32[128,128]{1,0:T(8,128)S(1)} %get-tuple-element.50), channel_id=1, source_target_pairs={{1,2},{2,1},{3,4},{4,3},{5,6},{6,5},{7,0},{0,7},{9,10},{10,9},{11,... | collective-permute-start | bytes 196616 | tf_op jit(solution)/shard_map/ppermute | solution.py:374
  7.1 5.2 %collective-permute-start.6 = (f32[8,128]{1,0:T(8,128)S(1)}, f32[8,128]{1,0:T(8,128)S(1)}, u32[]{:S(2)}, u32[]{:S(2)}) collective-permute-start(f32[8,128]{1,0:T(8,128)S(1)} %get-tuple-element.52.terms), channel_id=1, source_target_pairs={{0,9},{1,8},{2,11},{3,10},{4,13},{5,12},{6,15},{7,14},{8,1},{9,0},... | collective-permute-start | bytes 12296 | tf_op jit(solution)/shard_map/ppermute | solution.py:374
  12.3 0.0 copy-done
  12.3 0.0 copy-done.1
  12.3 0.5 %shard_map.92 = (f32[840,128]{1,0:T(8,128)S(1)}, f32[160,128]{1,0:T(8,128)S(1)}, f32[160,128]{1,0:T(8,128)S(1)}, f32[1040,128]{1,0:T(8,128)S(1)}, f32[8,128]{1,0:T(8,128)S(1)}) custom-call(f32[512,128]{1,0:T(8,128)S(1)} %get-tuple-element.46.w, f32[300,1,128]{2,1,0:T(1,128)S(1)} %bitcast.12, f32[30,1,128]{2,1,0:T(1,128)S(1)} %bitcast.17, ...), custom_call_target="tpu_custom_call" | custom-call | flops 20000000 | bytes 1000000 | tf_op jit(solution)/shard_map/pallas_call | solution.py:43
  12.8 0.8 %collective-permute-done.6 = f32[8,128]{1,0:T(8,128)S(1)} collective-permute-done((f32[8,128]{1,0:T(8,128)S(1)}, f32[8,128]{1,0:T(8,128)S(1)}, u32[]{:S(2)}, u32[]{:S(2)}) %collective-permute-start.6) | collective-permute-done | bytes 4128 | tf_op jit(solution)/shard_map/ppermute | solution.py:374
  13.6 0.0 collective-permute-done.1.aze
  13.6 0.0 collective-permute-done.3.axe
  13.6 0.1 fusion.1
  13.7 2.9 %collective-permute-start.7 = (f32[8,128]{1,0:T(8,128)S(1)}, f32[8,128]{1,0:T(8,128)S(1)}, u32[]{:S(2)}, u32[]{:S(2)}) collective-permute-start(f32[8,128]{1,0:T(8,128)S(1)} %fusion.1), channel_id=1, source_target_pairs={{0,4},{1,5},{2,6},{3,7},{4,0},{5,1},{6,2},{7,3},{8,12},{9,13},{10,... | collective-permute-start | bytes 12296 | tf_op jit(solution)/shard_map/ppermute | solution.py:374
  16.6 0.0 collective-permute-done.2.axo
  16.6 0.0 collective-permute-done.azo
  16.6 2.2 %shard_map.93 = (f32[152,128]{1,0:T(8,128)S(1)}, f32[144,128]{1,0:T(8,128)S(1)}, f32[136,128]{1,0:T(8,128)S(1)}, f32[128,128]{1,0:T(8,128)S(1)}, f32[512,128]{1,...) custom-call(f32[512,128]{1,0:T(8,128)S(1)} %get-tuple-element.46.w, f32[512,128]{1,0:T(8,128)S(1)} %get-tuple-element.47.c2, ...), custom_call_target="tpu_custom_call" | custom-call | flops 15360000 | bytes 1000000 | tf_op jit(solution)/shard_map/pallas_call | solution.py:43
  18.8 0.0 collective-permute-done.7
  18.9 0.8 %collective-permute-start.8 = (f32[136,128]{1,0:T(8,128)S(1)}, f32[136,128]{1,0:T(8,128)S(1)}, u32[]{:S(2)}, u32[]{:S(2)}) collective-permute-start(f32[136,128]{1,0:T(8,128)S(1)} %get-tuple-element.89), channel_id=1, source_target_pairs={{1,2},{2,1},{3,4},{4,3},{5,6},{6,5},{7,0},{0,7},{9,10},{10,9},{11,... | collective-permute-start | bytes 208904 | tf_op jit(solution)/shard_map/ppermute | solution.py:374
  19.7 0.0 collective-permute-start.4
  19.7 4.0 %collective-permute-start.5 = (f32[144,128]{1,0:T(8,128)S(1)}, f32[144,128]{1,0:T(8,128)S(1)}, u32[]{:S(2)}, u32[]{:S(2)}) collective-permute-start(f32[144,128]{1,0:T(8,128)S(1)} %get-tuple-element.59), channel_id=1, source_target_pairs={{0,8},{8,0},{16,24},{24,16},{32,40},{40,32},{48,56},{56,48},{64,72... | collective-permute-start | bytes 221192 | tf_op jit(solution)/shard_map/ppermute | solution.py:374
  23.6 0.0 collective-permute-start.9
  23.6 0.2 collective-permute-done.8.xo
  23.9 0.0 collective-permute-start.10
  23.9 3.6 %collective-permute-done.10 = f32[8,128]{1,0:T(8,128)S(1)} collective-permute-done((f32[8,128]{1,0:T(8,128)S(1)}, f32[8,128]{1,0:T(8,128)S(1)}, u32[]{:S(2)}, u32[]{:S(2)}) %collective-permute-start.10) | collective-permute-done | bytes 4128 | tf_op jit(solution)/shard_map/ppermute | solution.py:374
  27.5 0.0 collective-permute-done.5.ze
  27.5 0.0 collective-permute-done.4.zo
  27.5 0.1 collective-permute-start.11
  27.6 0.4 collective-permute-start.12
  28.0 0.0 collective-permute-start.13
  28.0 0.0 collective-permute-done.9.xe
  28.0 0.5 shard_map.95
  28.5 4.0 %collective-permute-done.13 = f32[8,128]{1,0:T(8,128)S(1)} collective-permute-done((f32[8,128]{1,0:T(8,128)S(1)}, f32[8,128]{1,0:T(8,128)S(1)}, u32[]{:S(2)}, u32[]{:S(2)}) %collective-permute-start.13) | collective-permute-done | bytes 4128 | tf_op jit(solution)/shard_map/ppermute | solution.py:374
  32.5 2.5 %collective-permute-start.14 = (f32[8,128]{1,0:T(8,128)S(1)}, f32[8,128]{1,0:T(8,128)S(1)}, u32[]{:S(2)}, u32[]{:S(2)}) collective-permute-start(f32[8,128]{1,0:T(8,128)S(1)} %add.30), channel_id=1, source_target_pairs={{64,128},{72,136},{80,144},{88,152},{96,160},{104,168},{112,176},{... | collective-permute-start | bytes 12296 | tf_op jit(solution)/shard_map/ppermute | solution.py:374
  35.1 0.0 collective-permute-done.11.ro
  35.1 0.0 collective-permute-done.12.re
  35.1 1.8 %shard_map.96 = (f32[72,128]{1,0:T(8,128)S(1)}, f32[64,128]{1,0:T(8,128)S(1)}, f32[64,128]{1,0:T(8,128)S(1)}, f32[64,128]{1,0:T(8,128)S(1)}, f32[840,128]{1,0:T(...) custom-call(f32[144,128]{1,0:T(8,128)S(1)} %collective-permute-done.azo, ...), custom_call_target="tpu_custom_call" | custom-call | flops 15360000 | bytes 1000000 | tf_op jit(solution)/shard_map/pallas_call | solution.py:43
  36.9 1.4 %collective-permute-done.14 = f32[8,128]{1,0:T(8,128)S(1)} collective-permute-done((f32[8,128]{1,0:T(8,128)S(1)}, f32[8,128]{1,0:T(8,128)S(1)}, u32[]{:S(2)}, u32[]{:S(2)}) %collective-permute-start.14) | collective-permute-done | bytes 4128 | tf_op jit(solution)/shard_map/ppermute | solution.py:374
  38.3 0.4 collective-permute-start.15
  38.7 5.0 %collective-permute-start.16 = (f32[64,128]{1,0:T(8,128)S(1)}, f32[64,128]{1,0:T(8,128)S(1)}, u32[]{:S(2)}, u32[]{:S(2)}) collective-permute-start(f32[64,128]{1,0:T(8,128)S(1)} %get-tuple-element.82), channel_id=1, source_target_pairs={{0,8},{8,0},{16,24},{24,16},{32,40},{40,32},{48,56},{56,48},{64,72... | collective-permute-start | bytes 98312 | tf_op jit(solution)/shard_map/ppermute | solution.py:374
  43.7 0.0 collective-permute-start.17
  43.7 0.3 collective-permute-start.18
  43.9 0.4 shard_map.97
  44.4 1.2 %collective-permute-done.16.ze = f32[64,128]{1,0:T(8,128)S(1)} collective-permute-done((f32[64,128]{1,0:T(8,128)S(1)}, f32[64,128]{1,0:T(8,128)S(1)}, u32[]{:S(2)}, u32[]{:S(2)}) %collective-permute-start.16) | collective-permute-done | bytes 32800 | tf_op jit(solution)/shard_map/ppermute | solution.py:374
  45.6 2.7 %collective-permute-done.17.xo = f32[64,128]{1,0:T(8,128)S(1)} collective-permute-done((f32[64,128]{1,0:T(8,128)S(1)}, f32[64,128]{1,0:T(8,128)S(1)}, u32[]{:S(2)}, u32[]{:S(2)}) %collective-permute-start.17) | collective-permute-done | bytes 32800 | tf_op jit(solution)/shard_map/ppermute | solution.py:374
  48.2 0.0 collective-permute-done.18.xe
  48.2 0.0 collective-permute-done.15.zo
  48.2 0.8 %shard_map.98 = f32[512,128]{1,0:T(8,128)} custom-call(f32[512,128]{1,0:T(8,128)S(1)} %get-tuple-element.78.inner, f32[128,128]{1,0:T(8,128)S(1)} %get-tuple-element.79.base, f32[72,128]{1,0:T(8,128)S(1)} %collective-permute-done.15.zo, f32[64,128]{1,0:T(8,128)S(1)} %collective-permute-done.16.ze, f32[64,128]{1,0:T(8,128)S(1)} %collective-permute-done.17.xo, ...), custom_call_target="tpu_custom_call" | custom-call | flops 300000 | bytes 1000000 | tf_op jit(solution)/shard_map/pallas_call | solution.py:43
  (7 shorter events, 0.0 us)
Async XLA Ops:
  0.0 12.3 %copy-start = (f32[3,10,10,1,1,128]{5,4,3,2,1,0:T(1,128)S(1)}, f32[3,10,10,1,1,128]{5,4,3,2,1,0:T(1,128)}, u32[]{:S(2)}) copy-start(f32[3,10,10,1,1,128]{5,4,3,2,1,0:T(1,128)} %param.12) | copy-start | bytes 460804
  1.5 10.8 %copy-start.1 = (f32[3,10,1,1,128]{4,3,2,1,0:T(1,128)S(1)}, f32[3,10,1,1,128]{4,3,2,1,0:T(1,128)}, u32[]{:S(2)}) copy-start(f32[3,10,1,1,128]{4,3,2,1,0:T(1,128)} %param.13) | copy-start | bytes 46084
  1.5 12.1 %collective-permute-start.1 = (f32[136,128]{1,0:T(8,128)S(1)}, f32[136,128]{1,0:T(8,128)S(1)}, u32[]{:S(2)}, u32[]{:S(2)}) collective-permute-start(f32[136,128]{1,0:T(8,128)S(1)} %get-tuple-element.49), channel_id=1, source_target_pairs={{0,8},{8,0},{16,24},{24,16},{32,40},{40,32},{48,56},{56,48},{64,72... | collective-permute-start | bytes 208904 | tf_op jit(solution)/shard_map/ppermute | solution.py:374
  3.9 9.8 %collective-permute-start.3 = (f32[136,128]{1,0:T(8,128)S(1)}, f32[136,128]{1,0:T(8,128)S(1)}, u32[]{:S(2)}, u32[]{:S(2)}) collective-permute-start(f32[136,128]{1,0:T(8,128)S(1)} %get-tuple-element.51), channel_id=1, source_target_pairs={{0,1},{1,0},{2,3},{3,2},{4,5},{5,4},{6,7},{7,6},{8,9},{9,8},{10,11... | collective-permute-start | bytes 208904 | tf_op jit(solution)/shard_map/ppermute | solution.py:374
  3.9 12.8 %collective-permute-start = (f32[144,128]{1,0:T(8,128)S(1)}, f32[144,128]{1,0:T(8,128)S(1)}, u32[]{:S(2)}, u32[]{:S(2)}) collective-permute-start(f32[144,128]{1,0:T(8,128)S(1)} %get-tuple-element.48), channel_id=1, source_target_pairs={{8,16},{16,8},{24,32},{32,24},{40,48},{48,40},{56,64},{64,56},{72,... | collective-permute-start | bytes 221192 | tf_op jit(solution)/shard_map/ppermute | solution.py:374
  4.3 12.4 %collective-permute-start.2 = (f32[128,128]{1,0:T(8,128)S(1)}, f32[128,128]{1,0:T(8,128)S(1)}, u32[]{:S(2)}, u32[]{:S(2)}) collective-permute-start(f32[128,128]{1,0:T(8,128)S(1)} %get-tuple-element.50), channel_id=1, source_target_pairs={{1,2},{2,1},{3,4},{4,3},{5,6},{6,5},{7,0},{0,7},{9,10},{10,9},{11,... | collective-permute-start | bytes 196616 | tf_op jit(solution)/shard_map/ppermute | solution.py:374
  7.1 6.5 %collective-permute-start.6 = (f32[8,128]{1,0:T(8,128)S(1)}, f32[8,128]{1,0:T(8,128)S(1)}, u32[]{:S(2)}, u32[]{:S(2)}) collective-permute-start(f32[8,128]{1,0:T(8,128)S(1)} %get-tuple-element.52.terms), channel_id=1, source_target_pairs={{0,9},{1,8},{2,11},{3,10},{4,13},{5,12},{6,15},{7,14},{8,1},{9,0},... | collective-permute-start | bytes 12296 | tf_op jit(solution)/shard_map/ppermute | solution.py:374
  13.7 5.1 %collective-permute-start.7 = (f32[8,128]{1,0:T(8,128)S(1)}, f32[8,128]{1,0:T(8,128)S(1)}, u32[]{:S(2)}, u32[]{:S(2)}) collective-permute-start(f32[8,128]{1,0:T(8,128)S(1)} %fusion.1), channel_id=1, source_target_pairs={{0,4},{1,5},{2,6},{3,7},{4,0},{5,1},{6,2},{7,3},{8,12},{9,13},{10,... | collective-permute-start | bytes 12296 | tf_op jit(solution)/shard_map/ppermute | solution.py:374
  18.9 5.0 %collective-permute-start.8 = (f32[136,128]{1,0:T(8,128)S(1)}, f32[136,128]{1,0:T(8,128)S(1)}, u32[]{:S(2)}, u32[]{:S(2)}) collective-permute-start(f32[136,128]{1,0:T(8,128)S(1)} %get-tuple-element.89), channel_id=1, source_target_pairs={{1,2},{2,1},{3,4},{4,3},{5,6},{6,5},{7,0},{0,7},{9,10},{10,9},{11,... | collective-permute-start | bytes 208904 | tf_op jit(solution)/shard_map/ppermute | solution.py:374
  19.7 7.8 %collective-permute-start.4 = (f32[152,128]{1,0:T(8,128)S(1)}, f32[152,128]{1,0:T(8,128)S(1)}, u32[]{:S(2)}, u32[]{:S(2)}) collective-permute-start(f32[152,128]{1,0:T(8,128)S(1)} %get-tuple-element.58), channel_id=1, source_target_pairs={{8,16},{16,8},{24,32},{32,24},{40,48},{48,40},{56,64},{64,56},{72,... | collective-permute-start | bytes 233480 | tf_op jit(solution)/shard_map/ppermute | solution.py:374
  19.7 7.8 %collective-permute-start.5 = (f32[144,128]{1,0:T(8,128)S(1)}, f32[144,128]{1,0:T(8,128)S(1)}, u32[]{:S(2)}, u32[]{:S(2)}) collective-permute-start(f32[144,128]{1,0:T(8,128)S(1)} %get-tuple-element.59), channel_id=1, source_target_pairs={{0,8},{8,0},{16,24},{24,16},{32,40},{40,32},{48,56},{56,48},{64,72... | collective-permute-start | bytes 221192 | tf_op jit(solution)/shard_map/ppermute | solution.py:374
  23.6 4.4 %collective-permute-start.9 = (f32[128,128]{1,0:T(8,128)S(1)}, f32[128,128]{1,0:T(8,128)S(1)}, u32[]{:S(2)}, u32[]{:S(2)}) collective-permute-start(f32[128,128]{1,0:T(8,128)S(1)} %get-tuple-element.62), channel_id=1, source_target_pairs={{0,1},{1,0},{2,3},{3,2},{4,5},{5,4},{6,7},{7,6},{8,9},{9,8},{10,11... | collective-permute-start | bytes 196616 | tf_op jit(solution)/shard_map/ppermute | solution.py:374
  23.9 3.6 %collective-permute-start.10 = (f32[8,128]{1,0:T(8,128)S(1)}, f32[8,128]{1,0:T(8,128)S(1)}, u32[]{:S(2)}, u32[]{:S(2)}) collective-permute-start(f32[8,128]{1,0:T(8,128)S(1)} %slice_add_fusion.grouped), channel_id=1, source_target_pairs={{0,32},{8,40},{16,48},{24,56},{32,0},{40,8},{48,16},{56,24},{64,96... | collective-permute-start | bytes 12296 | tf_op jit(solution)/shard_map/ppermute | solution.py:374
  27.5 7.5 %collective-permute-start.11 = (f32[32,128]{1,0:T(8,128)S(1)}, f32[32,128]{1,0:T(8,128)S(1)}, u32[]{:S(2)}, u32[]{:S(2)}) collective-permute-start(f32[32,128]{1,0:T(8,128)S(1)} %get-tuple-element.67), channel_id=1, source_target_pairs={{1,2},{2,1},{3,4},{4,3},{5,6},{6,5},{7,0},{0,7},{9,10},{10,9},{11,... | collective-permute-start | bytes 49160 | tf_op jit(solution)/shard_map/ppermute | solution.py:374
  27.6 7.4 %collective-permute-start.12 = (f32[32,128]{1,0:T(8,128)S(1)}, f32[32,128]{1,0:T(8,128)S(1)}, u32[]{:S(2)}, u32[]{:S(2)}) collective-permute-start(f32[32,128]{1,0:T(8,128)S(1)} %get-tuple-element.68), channel_id=1, source_target_pairs={{0,1},{1,0},{2,3},{3,2},{4,5},{5,4},{6,7},{7,6},{8,9},{9,8},{10,11... | collective-permute-start | bytes 49160 | tf_op jit(solution)/shard_map/ppermute | solution.py:374
  28.0 4.5 %collective-permute-start.13 = (f32[8,128]{1,0:T(8,128)S(1)}, f32[8,128]{1,0:T(8,128)S(1)}, u32[]{:S(2)}, u32[]{:S(2)}) collective-permute-start(f32[8,128]{1,0:T(8,128)S(1)} %get-tuple-element.63.terms), channel_id=1, source_target_pairs={{0,64},{8,72},{16,80},{24,88},{32,96},{40,104},{48,112},{56,120},{... | collective-permute-start | bytes 12296 | tf_op jit(solution)/shard_map/ppermute | solution.py:374
  32.5 5.7 %collective-permute-start.14 = (f32[8,128]{1,0:T(8,128)S(1)}, f32[8,128]{1,0:T(8,128)S(1)}, u32[]{:S(2)}, u32[]{:S(2)}) collective-permute-start(f32[8,128]{1,0:T(8,128)S(1)} %add.30), channel_id=1, source_target_pairs={{64,128},{72,136},{80,144},{88,152},{96,160},{104,168},{112,176},{... | collective-permute-start | bytes 12296 | tf_op jit(solution)/shard_map/ppermute | solution.py:374
  38.3 10.0 %collective-permute-start.15 = (f32[72,128]{1,0:T(8,128)S(1)}, f32[72,128]{1,0:T(8,128)S(1)}, u32[]{:S(2)}, u32[]{:S(2)}) collective-permute-start(f32[72,128]{1,0:T(8,128)S(1)} %get-tuple-element.87), channel_id=1, source_target_pairs={{8,16},{16,8},{24,32},{32,24},{40,48},{48,40},{56,64},{64,56},{72,... | collective-permute-start | bytes 110600 | tf_op jit(solution)/shard_map/ppermute | solution.py:374
  38.7 6.9 %collective-permute-start.16 = (f32[64,128]{1,0:T(8,128)S(1)}, f32[64,128]{1,0:T(8,128)S(1)}, u32[]{:S(2)}, u32[]{:S(2)}) collective-permute-start(f32[64,128]{1,0:T(8,128)S(1)} %get-tuple-element.82), channel_id=1, source_target_pairs={{0,8},{8,0},{16,24},{24,16},{32,40},{40,32},{48,56},{56,48},{64,72... | collective-permute-start | bytes 98312 | tf_op jit(solution)/shard_map/ppermute | solution.py:374
  43.7 4.6 %collective-permute-start.17 = (f32[64,128]{1,0:T(8,128)S(1)}, f32[64,128]{1,0:T(8,128)S(1)}, u32[]{:S(2)}, u32[]{:S(2)}) collective-permute-start(f32[64,128]{1,0:T(8,128)S(1)} %get-tuple-element.83), channel_id=1, source_target_pairs={{1,2},{2,1},{3,4},{4,3},{5,6},{6,5},{7,0},{0,7},{9,10},{10,9},{11,... | collective-permute-start | bytes 98312 | tf_op jit(solution)/shard_map/ppermute | solution.py:374
  43.7 4.6 %collective-permute-start.18 = (f32[64,128]{1,0:T(8,128)S(1)}, f32[64,128]{1,0:T(8,128)S(1)}, u32[]{:S(2)}, u32[]{:S(2)}) collective-permute-start(f32[64,128]{1,0:T(8,128)S(1)} %get-tuple-element.84), channel_id=1, source_target_pairs={{0,1},{1,0},{2,3},{3,2},{4,5},{5,4},{6,7},{7,6},{8,9},{9,8},{10,11... | collective-permute-start | bytes 98312 | tf_op jit(solution)/shard_map/ppermute | solution.py:374

commit v6 on v5

--- a/solution.py
+++ b/solution.py
@@ -229,7 +229,6 @@
         ze[pl.ds(base, FACE), :] = source[layer(7 - z_up * 7), :]
         put_x(xo, base, source, x_up * 7)
         put_x(xe, base, source, 7 - x_up * 7)
-    zo[pl.ds(128, 16), :] = jnp.zeros((16, 128), F32)
     total = w[pl.ds(0, 8), :]
     for at in range(8, 512, 8):
         total = total + w[pl.ds(at, 8), :]
@@ -245,8 +244,8 @@
         terms[pl.ds(at, 1), :] = jnp.sum(top[:, at * 128 : (at + 1) * 128] * rhs, axis=0, keepdims=True)
     for at in range(2):
         terms[pl.ds(4 + at, 1), :] = jnp.sum(group[:, at * 128 : (at + 1) * 128] * rhs, axis=0, keepdims=True)
+    ze[pl.ds(128, 8), :] = terms[...]
     xe[pl.ds(128, 8), :] = terms[...]
-    ze[pl.ds(128, 8), :] = terms[...]
 
 
 def own_kernel(w, basis, eigen, terms, work, ylow, yhigh, inverse, same, plane, zx):
@@ -278,7 +277,6 @@
         message[pl.ds(FACE, FACE), :] = w[here, :] - c2[here, :] * r[here, :]
         message[pl.ds(128, 8), :] = x_face[rows8(FACE + up * 56), :]
         message[pl.ds(136, 8), :] = x_face[rows8(up * 56), :]
-    zo[pl.ds(LINK, 8), :] = jnp.zeros((8, 128), F32)
     for message, up in ((xo, place[1]), (xe, 1 - place[1])):
         message[pl.ds(0, FACE), :] = x_face[face(up), :]
         for k in range(8):
@@ -286,9 +284,8 @@
             message[pl.ds(FACE + k * 8, 8), :] = w[here, :] - c2[here, :] * r[here, :]
 
 
-def relay_kernel(zo, ze, terms, ro, re, same):
-    place = where_am_i()
-    same[...] = terms[...]
+def relay_kernel(zo, ze, ro, re):
+    place = where_am_i()
     z_low = place[0] == 0
     for message, up in ((ro, place[1]), (re, 1 - place[1])):
         edge = rows8(136 - up * 8)
@@ -299,9 +296,8 @@
         message[pl.ds(24, 8), :] = jnp.where(z_low, ze[line, :], zo[line, :])
 
 
-def second_own_kernel(w, c2, r, zo, ze, xo, xe, basis, terms, first, work, ylow, yhigh, same, field, plane):
-    place = where_am_i()
-    same[...] = terms[...]
+def second_own_kernel(w, c2, r, zo, ze, xo, xe, basis, first, work, ylow, yhigh, field, plane):
+    place = where_am_i()
     z_low, x_low = place[0] == 0, place[1] == 0
     first[...] = r[...]
     first[layer(7), :] += pick(z_low, ze, zo, 0, FACE)
@@ -338,24 +334,23 @@
     solve(work_in, ylow_in, yhigh_in, zl, zh, xl, xh, basis, inverse, work, ylow, yhigh)
     back_faces(work, basis, s_face, t_face)
     for message, up in ((co, place[0]), (ce, 1 - place[0])):
-        message[pl.ds(0, FACE), :] = s_face[face(up), :]
+        message[...] = s_face[face(up), :]
     for message, up in ((do, place[1]), (de, 1 - place[1])):
-        message[...] = t_face[face(up), :]
-
-
-def inner_kernel(first, work, ylow, yhigh, basis, grouped, own_part, own, group, out, base, plane):
+        message[pl.ds(0, FACE), :] = t_face[face(up), :]
+
+
+def inner_kernel(first, work, ylow, yhigh, basis, own_part, own, out, base, plane):
     back_inner(work, ylow, yhigh, basis, out, plane, first)
-    sums = own[...] * own_part[pl.ds(0, 1), :]
+    base[...] = own[...] * own_part[pl.ds(0, 1), :]
+
+
+def last_kernel(inner, base, zo, ze, xo, xe, terms, beside, coarse_map, group, top, out):
+    place = where_am_i()
+    z_low, x_low = place[0] == 0, place[1] == 0
+    total = terms[...] + beside[...]
+    sums = base[...]
     for at in range(2):
-        sums = sums + group[:, at * 128 : (at + 1) * 128] * grouped[pl.ds(4 + at, 1), :]
-    base[...] = sums
-
-
-def last_kernel(inner, base, zo, ze, xo, xe, terms, coarse_map, top, out):
-    place = where_am_i()
-    z_low, x_low = place[0] == 0, place[1] == 0
-    total = terms[...] + zo[pl.ds(FACE, 8), :]
-    sums = base[...]
+        sums = sums + group[:, at * 128 : (at + 1) * 128] * terms[pl.ds(4 + at, 1), :]
     for at in range(4):
         sums = sums + top[:, at * 128 : (at + 1) * 128] * total[at : at + 1]
     sol = jnp.sum(sums, axis=1, keepdims=True)
@@ -390,7 +385,7 @@
     held = [jax.ShapeDtypeStruct(a.shape, a.dtype) for a in (coarse_map, own, group, top)]
 
     zo, ze, xe, xo, w, c2, terms, own_part, coarse_map, own, group, top = call(
-        first_kernel, [144, 136, 136, 128, 512, 512, 8, 8] + held, (512,) * 3,
+        first_kernel, [128, 136, 136, 128, 512, 512, 8, 8] + held, (512,) * 3,
         residual, margin, diag, coarse_map, own, group, top,
         in_hbm=range(7), scratch=[pltpu.SemaphoreType.DMA((7,))], flops=300000,
     )
@@ -403,35 +398,32 @@
     terms = terms + axe[128:] + jnp.where(is_top, aze[128:] + across, 0.0)
     beside = move(terms, "coarse", swap(coarses, 4, 0))
     zo, ze, xo, xe, r, z_face, x_face = call(
-        pass_kernel, (LINK + 8, LINK, 136, 128, 512, 128, 128), (FACE,) * 4 + inner_rows + (128,),
+        pass_kernel, (LINK + 8, LINK, 128, 128, 512, 128, 128), (FACE,) * 4 + inner_rows + (128,),
         w, c2, azo, aze, axo, axe, basis, work, ylow, yhigh, inverse,
     )
     terms = terms + beside
-    zo, ze = move(zo, "dom", z_odd), move(ze, "dom", z_even)
-    xo = move(lax.dynamic_update_slice(xo, terms, (128, 0)), "coarse", x_odd)
-    xe = move(xe, "coarse", x_even)
-    grouped = terms + xo[128:]
-    terms = grouped + move(grouped, "dom", swap(doms, 4, 0))
-    ro, re, terms = call(relay_kernel, (RELAY, RELAY, 8), (), zo, ze, terms, flops=1000)
+    zo = move(lax.dynamic_update_slice(zo, terms, (LINK, 0)), "dom", z_odd)
+    ze, xe, xo = move(ze, "dom", z_even), move(xe, "coarse", x_even), move(xo, "coarse", x_odd)
+    terms = terms + jnp.where(is_top, zo[LINK:], 0.0)
+    wide = jnp.concatenate([terms, jnp.zeros((32, 128), F32)])
+    terms = terms + jnp.where(is_top, move(wide, "dom", swap(doms, 4, 0))[:8], 0.0)
+    ro, re = call(relay_kernel, (RELAY, RELAY), (), zo, ze, flops=1000)
     re, ro = move(re, "coarse", x_even), move(ro, "coarse", x_odd)
     beside = move(terms, "dom", swap(doms, 8, 0))
-    first, work, ylow, yhigh, terms = call(
-        second_own_kernel, (512,) + inner_rows + (8,), (512, 128), w, c2, r, zo, ze, xo, xe, basis, terms, flops=1000
+    first, work, ylow, yhigh = call(
+        second_own_kernel, (512,) + inner_rows, (512, 128), w, c2, r, zo, ze, xo, xe, basis, flops=1000
     )
-    terms = terms + beside
-    beside = move(terms, "dom", swap(doms, 8, 1))
     co, ce, do, de, work, ylow, yhigh = call(
-        second_pass_kernel, (FACE + 8, FACE, FACE, FACE) + inner_rows, (FACE,) * 4 + (128,) * 2,
+        second_pass_kernel, (FACE, FACE, FACE + 8, FACE) + inner_rows, (FACE,) * 4 + (128,) * 2,
         azo, aze, axo, axe, z_face, x_face, zo, ze, xo, xe, ro, re, basis, work, ylow, yhigh, inverse,
     )
-    terms = terms + beside
-    zo = move(lax.dynamic_update_slice(co, terms, (FACE, 0)), "dom", z_odd)
-    ze = move(ce, "dom", z_even)
-    xe, xo = move(de, "coarse", x_even), move(do, "coarse", x_odd)
-    inner, base = call(
-        inner_kernel, (512, 128), (128,), first, work, ylow, yhigh, basis, grouped, own_part, own, group, flops=1000
-    )
-    (out,) = call(last_kernel, (512,), (), inner, base, zo, ze, xo, xe, terms, coarse_map, top, flops=300000)
+    terms = terms + jnp.where(is_top, beside, 0.0)
+    xo = move(lax.dynamic_update_slice(do, terms, (FACE, 0)), "coarse", x_odd)
+    zo, ze, xe = move(co, "dom", z_odd), move(ce, "dom", z_even), move(de, "coarse", x_even)
+    terms = terms + xo[FACE:]
+    beside = move(terms, "dom", swap(doms, 8, 1))
+    inner, base = call(inner_kernel, (512, 128), (128,), first, work, ylow, yhigh, basis, own_part, own, flops=1000)
+    (out,) = call(last_kernel, (512,), (), inner, base, zo, ze, xo, xe, terms, beside, coarse_map, group, top, flops=300000)
     return out.reshape(shape)
 
 

time: 49.2 us -> 47.3 us (0.961)
  the two profiles are of different devices: /device:TPU:2 before, /device:TPU:4 now
where the time goes in v6:
time: 47.3 us; the launch traced here: 47.2 us
  starting transfers between devices  28 us (59%)
  waiting for transfers between devices  11.1 us (23%)
  Pallas kernels  7.68 us (16%)
    ppermute x19, starting transfers between devices, move(): return lax.ppermute(value, axis, pairs)  28 us
    ppermute x19, waiting for transfers between devices, move(): return lax.ppermute(value, axis, pairs)  11.1 us
    pallas_call x8, Pallas kernels, call(): pl.pallas_call(kernel, out_shape=outs, in_specs=specs, out_specs=[VMEM] *...  7.68 us
  transfers between devices with their start and end apart: 19, of which 9 were waited for; matrix products, arithmetic and copies ran while one was open for 1% of the time, Pallas kernels for 11%

profile of v6, /device:TPU:4, one launch (start us, length us, event | category | flops | bytes accessed | tf_op | source)
XLA Modules:
  0.0 47.2 jit_solution(3648594400437342905)
XLA Ops:
  0.0 0.0 copy-start
  0.0 1.5 %shard_map.91 = (f32[128,128]{1,0:T(8,128)S(1)}, f32[136,128]{1,0:T(8,128)S(1)}, f32[136,128]{1,0:T(8,128)S(1)}, f32[128,128]{1,0:T(8,128)S(1)}, f32[512,128]{1,...) custom-call(f32[512,128]{1,0:T(8,128)} %bitcast.18, ...), custom_call_target="tpu_custom_call" | custom-call | flops 300000 | bytes 1000000 | tf_op jit(solution)/shard_map/pallas_call | solution.py:43
  1.5 0.0 copy-start.1
  1.5 0.6 %collective-permute-start = (f32[128,128]{1,0:T(8,128)S(1)}, f32[128,128]{1,0:T(8,128)S(1)}, u32[]{:S(2)}, u32[]{:S(2)}) collective-permute-start(f32[128,128]{1,0:T(8,128)S(1)} %get-tuple-element.46), channel_id=1, source_target_pairs={{8,16},{16,8},{24,32},{32,24},{40,48},{48,40},{56,64},{64,56},{72,... | collective-permute-start | bytes 196616 | tf_op jit(solution)/shard_map/ppermute | solution.py:369
  2.1 2.5 %collective-permute-start.1 = (f32[136,128]{1,0:T(8,128)S(1)}, f32[136,128]{1,0:T(8,128)S(1)}, u32[]{:S(2)}, u32[]{:S(2)}) collective-permute-start(f32[136,128]{1,0:T(8,128)S(1)} %get-tuple-element.47), channel_id=1, source_target_pairs={{0,8},{8,0},{16,24},{24,16},{32,40},{40,32},{48,56},{56,48},{64,72... | collective-permute-start | bytes 208904 | tf_op jit(solution)/shard_map/ppermute | solution.py:369
  4.6 1.9 %collective-permute-start.2 = (f32[128,128]{1,0:T(8,128)S(1)}, f32[128,128]{1,0:T(8,128)S(1)}, u32[]{:S(2)}, u32[]{:S(2)}) collective-permute-start(f32[128,128]{1,0:T(8,128)S(1)} %get-tuple-element.48), channel_id=1, source_target_pairs={{1,2},{2,1},{3,4},{4,3},{5,6},{6,5},{7,0},{0,7},{9,10},{10,9},{11,... | collective-permute-start | bytes 196616 | tf_op jit(solution)/shard_map/ppermute | solution.py:369
  6.5 0.0 collective-permute-start.3
  6.5 0.4 collective-permute-start.4
  6.9 0.0 copy-done
  6.9 0.0 copy-done.1
  6.9 0.5 %shard_map.92 = (f32[840,128]{1,0:T(8,128)S(1)}, f32[160,128]{1,0:T(8,128)S(1)}, f32[160,128]{1,0:T(8,128)S(1)}, f32[1040,128]{1,0:T(8,128)S(1)}, f32[8,128]{1,0:T(8,128)S(1)}) custom-call(f32[512,128]{1,0:T(8,128)S(1)} %get-tuple-element.44.w, f32[300,1,128]{2,1,0:T(1,128)S(1)} %bitcast.12, f32[30,1,128]{2,1,0:T(1,128)S(1)} %bitcast.17, ...), custom_call_target="tpu_custom_call" | custom-call | flops 20000000 | bytes 1000000 | tf_op jit(solution)/shard_map/pallas_call | solution.py:43
  7.4 2.1 %collective-permute-done.4 = f32[8,128]{1,0:T(8,128)S(1)} collective-permute-done((f32[8,128]{1,0:T(8,128)S(1)}, f32[8,128]{1,0:T(8,128)S(1)}, u32[]{:S(2)}, u32[]{:S(2)}) %collective-permute-start.4) | collective-permute-done | bytes 4128 | tf_op jit(solution)/shard_map/ppermute | solution.py:369
  9.5 0.0 collective-permute-done.1.aze
  9.6 0.0 collective-permute-done.3.axe
  9.6 0.1 fusion.3
  9.6 2.7 %collective-permute-start.5 = (f32[8,128]{1,0:T(8,128)S(1)}, f32[8,128]{1,0:T(8,128)S(1)}, u32[]{:S(2)}, u32[]{:S(2)}) collective-permute-start(f32[8,128]{1,0:T(8,128)S(1)} %fusion.3), channel_id=1, source_target_pairs={{0,4},{1,5},{2,6},{3,7},{4,0},{5,1},{6,2},{7,3},{8,12},{9,13},{10,... | collective-permute-start | bytes 12296 | tf_op jit(solution)/shard_map/ppermute | solution.py:369
  12.3 0.0 collective-permute-done.azo
  12.4 0.0 collective-permute-done.2.axo
  12.4 2.1 %shard_map.93 = (f32[152,128]{1,0:T(8,128)S(1)}, f32[144,128]{1,0:T(8,128)S(1)}, f32[128,128]{1,0:T(8,128)S(1)}, f32[128,128]{1,0:T(8,128)S(1)}, f32[512,128]{1,...) custom-call(f32[512,128]{1,0:T(8,128)S(1)} %get-tuple-element.44.w, f32[512,128]{1,0:T(8,128)S(1)} %get-tuple-element.45.c2, ...), custom_call_target="tpu_custom_call" | custom-call | flops 15360000 | bytes 1000000 | tf_op jit(solution)/shard_map/pallas_call | solution.py:43
  14.5 0.3 collective-permute-done.5
  14.8 6.1 %collective-permute-start.6 = (f32[152,128]{1,0:T(8,128)S(1)}, f32[152,128]{1,0:T(8,128)S(1)}, u32[]{:S(2)}, u32[]{:S(2)}) collective-permute-start(f32[152,128]{1,0:T(8,128)S(1)} %get-tuple-element.83), channel_id=1, source_target_pairs={{8,16},{16,8},{24,32},{32,24},{40,48},{48,40},{56,64},{64,56},{72,... | collective-permute-start | bytes 233480 | tf_op jit(solution)/shard_map/ppermute | solution.py:369
  20.9 0.0 collective-permute-start.7
  20.9 2.4 %collective-permute-done.6.zo = f32[152,128]{1,0:T(8,128)S(1)} collective-permute-done((f32[152,128]{1,0:T(8,128)S(1)}, f32[152,128]{1,0:T(8,128)S(1)}, u32[]{:S(2)}, u32[]{:S(2)}) %collective-permute-start.6) | collective-permute-done | bytes 77856 | tf_op jit(solution)/shard_map/ppermute | solution.py:369
  23.2 0.1 fusion.1
  23.3 0.0 collective-permute-start.14
  23.3 0.1 collective-permute-start.8
  23.4 1.5 %collective-permute-start.9 = (f32[128,128]{1,0:T(8,128)S(1)}, f32[128,128]{1,0:T(8,128)S(1)}, u32[]{:S(2)}, u32[]{:S(2)}) collective-permute-start(f32[128,128]{1,0:T(8,128)S(1)} %get-tuple-element.60), channel_id=1, source_target_pairs={{0,1},{1,0},{2,3},{3,2},{4,5},{5,4},{6,7},{7,6},{8,9},{9,8},{10,11... | collective-permute-start | bytes 196616 | tf_op jit(solution)/shard_map/ppermute | solution.py:369
  24.9 0.3 collective-permute-done.7.ze
  25.2 1.3 %collective-permute-start.10 = (f32[32,128]{1,0:T(8,128)S(1)}, f32[32,128]{1,0:T(8,128)S(1)}, u32[]{:S(2)}, u32[]{:S(2)}) collective-permute-start(f32[32,128]{1,0:T(8,128)S(1)} %get-tuple-element.64), channel_id=1, source_target_pairs={{1,2},{2,1},{3,4},{4,3},{5,6},{6,5},{7,0},{0,7},{9,10},{10,9},{11,... | collective-permute-start | bytes 49160 | tf_op jit(solution)/shard_map/ppermute | solution.py:369
  26.5 0.2 collective-permute-start.11
  26.7 0.4 collective-permute-done.14
  27.1 0.1 fusion
  27.2 1.6 %collective-permute-start.15 = (f32[8,128]{1,0:T(8,128)S(1)}, f32[8,128]{1,0:T(8,128)S(1)}, u32[]{:S(2)}, u32[]{:S(2)}) collective-permute-start(f32[8,128]{1,0:T(8,128)S(1)} %fusion), channel_id=1, source_target_pairs={{0,64},{8,72},{16,80},{24,88},{32,96},{40,104},{48,112},{56,120},{... | collective-permute-start | bytes 12296 | tf_op jit(solution)/shard_map/ppermute | solution.py:369
  28.8 0.0 collective-permute-done.8.xo
  28.8 0.0 collective-permute-done.9.xe
  28.8 0.5 shard_map.94
  29.3 0.3 collective-permute-done.10.ro
  29.6 0.0 collective-permute-done.11.re
  29.6 1.8 %shard_map.96 = (f32[64,128]{1,0:T(8,128)S(1)}, f32[64,128]{1,0:T(8,128)S(1)}, f32[72,128]{1,0:T(8,128)S(1)}, f32[64,128]{1,0:T(8,128)S(1)}, f32[840,128]{1,0:T(...) custom-call(f32[128,128]{1,0:T(8,128)S(1)} %collective-permute-done.azo, ...), custom_call_target="tpu_custom_call" | custom-call | flops 15360000 | bytes 1000000 | tf_op jit(solution)/shard_map/pallas_call | solution.py:43
  31.4 0.3 collective-permute-done.15
  31.7 0.1 constant_dynamic-update-slice_fusion
  31.8 1.0 %collective-permute-start.16 = (f32[72,128]{1,0:T(8,128)S(1)}, f32[72,128]{1,0:T(8,128)S(1)}, u32[]{:S(2)}, u32[]{:S(2)}) collective-permute-start(f32[72,128]{1,0:T(8,128)S(1)} %constant_dynamic-update-slice_fusion), channel_id=1, source_target_pairs={{1,2},{2,1},{3,4},{4,3},{5,6},{6,5},{7,0},{0,7},{9,10},{10,9},{11,... | collective-permute-start | bytes 110600 | tf_op jit(solution)/shard_map/ppermute | solution.py:369
  32.8 2.0 %collective-permute-start.12 = (f32[64,128]{1,0:T(8,128)S(1)}, f32[64,128]{1,0:T(8,128)S(1)}, u32[]{:S(2)}, u32[]{:S(2)}) collective-permute-start(f32[64,128]{1,0:T(8,128)S(1)} %get-tuple-element.76), channel_id=1, source_target_pairs={{8,16},{16,8},{24,32},{32,24},{40,48},{48,40},{56,64},{64,56},{72,... | collective-permute-start | bytes 98312 | tf_op jit(solution)/shard_map/ppermute | solution.py:369
  34.8 5.7 %collective-permute-start.13 = (f32[64,128]{1,0:T(8,128)S(1)}, f32[64,128]{1,0:T(8,128)S(1)}, u32[]{:S(2)}, u32[]{:S(2)}) collective-permute-start(f32[64,128]{1,0:T(8,128)S(1)} %get-tuple-element.77), channel_id=1, source_target_pairs={{0,8},{8,0},{16,24},{24,16},{32,40},{40,32},{48,56},{56,48},{64,72... | collective-permute-start | bytes 98312 | tf_op jit(solution)/shard_map/ppermute | solution.py:369
  40.6 0.0 collective-permute-start.17
  40.6 0.0 collective-permute-done.16.xo
  40.6 0.1 slice_add_fusion.terms
  40.6 0.3 collective-permute-start.18
  40.9 0.4 shard_map.97
  41.3 0.0 collective-permute-done.12.zo
  41.3 1.1 %collective-permute-done.13.ze = f32[64,128]{1,0:T(8,128)S(1)} collective-permute-done((f32[64,128]{1,0:T(8,128)S(1)}, f32[64,128]{1,0:T(8,128)S(1)}, u32[]{:S(2)}, u32[]{:S(2)}) %collective-permute-start.13) | collective-permute-done | bytes 32800 | tf_op jit(solution)/shard_map/ppermute | solution.py:369
  42.4 0.0 collective-permute-done.17.xe
  42.4 3.9 %collective-permute-done.18.beside = f32[8,128]{1,0:T(8,128)S(1)} collective-permute-done((f32[8,128]{1,0:T(8,128)S(1)}, f32[8,128]{1,0:T(8,128)S(1)}, u32[]{:S(2)}, u32[]{:S(2)}) %collective-permute-start.18) | collective-permute-done | bytes 4128 | tf_op jit(solution)/shard_map/ppermute | solution.py:369
  46.4 0.8 %shard_map.98 = f32[512,128]{1,0:T(8,128)} custom-call(f32[512,128]{1,0:T(8,128)S(1)} %get-tuple-element.74.inner, f32[128,128]{1,0:T(8,128)S(1)} %get-tuple-element.75.base, f32[64,128]{1,0:T(8,128)S(1)} %collective-permute-done.12.zo, f32[64,128]{1,0:T(8,128)S(1)} %collective-permute-done.13.ze, f32[72,128]{1,0:T(8,128)S(1)} %collective-permute-done.16.xo, ...), custom_call_target="tpu_custom_call" | custom-call | flops 300000 | bytes 1000000 | tf_op jit(solution)/shard_map/pallas_call | solution.py:43
  (4 shorter events, 0.0 us)
Async XLA Ops:
  0.0 6.9 %copy-start = (f32[3,10,10,1,1,128]{5,4,3,2,1,0:T(1,128)S(1)}, f32[3,10,10,1,1,128]{5,4,3,2,1,0:T(1,128)}, u32[]{:S(2)}) copy-start(f32[3,10,10,1,1,128]{5,4,3,2,1,0:T(1,128)} %param.12) | copy-start | bytes 460804
  1.5 5.4 %copy-start.1 = (f32[3,10,1,1,128]{4,3,2,1,0:T(1,128)S(1)}, f32[3,10,1,1,128]{4,3,2,1,0:T(1,128)}, u32[]{:S(2)}) copy-start(f32[3,10,1,1,128]{4,3,2,1,0:T(1,128)} %param.13) | copy-start | bytes 46084
  1.5 10.9 %collective-permute-start = (f32[128,128]{1,0:T(8,128)S(1)}, f32[128,128]{1,0:T(8,128)S(1)}, u32[]{:S(2)}, u32[]{:S(2)}) collective-permute-start(f32[128,128]{1,0:T(8,128)S(1)} %get-tuple-element.46), channel_id=1, source_target_pairs={{8,16},{16,8},{24,32},{32,24},{40,48},{48,40},{56,64},{64,56},{72,... | collective-permute-start | bytes 196616 | tf_op jit(solution)/shard_map/ppermute | solution.py:369
  2.1 7.4 %collective-permute-start.1 = (f32[136,128]{1,0:T(8,128)S(1)}, f32[136,128]{1,0:T(8,128)S(1)}, u32[]{:S(2)}, u32[]{:S(2)}) collective-permute-start(f32[136,128]{1,0:T(8,128)S(1)} %get-tuple-element.47), channel_id=1, source_target_pairs={{0,8},{8,0},{16,24},{24,16},{32,40},{40,32},{48,56},{56,48},{64,72... | collective-permute-start | bytes 208904 | tf_op jit(solution)/shard_map/ppermute | solution.py:369
  4.6 7.7 %collective-permute-start.2 = (f32[128,128]{1,0:T(8,128)S(1)}, f32[128,128]{1,0:T(8,128)S(1)}, u32[]{:S(2)}, u32[]{:S(2)}) collective-permute-start(f32[128,128]{1,0:T(8,128)S(1)} %get-tuple-element.48), channel_id=1, source_target_pairs={{1,2},{2,1},{3,4},{4,3},{5,6},{6,5},{7,0},{0,7},{9,10},{10,9},{11,... | collective-permute-start | bytes 196616 | tf_op jit(solution)/shard_map/ppermute | solution.py:369
  6.5 3.0 %collective-permute-start.3 = (f32[136,128]{1,0:T(8,128)S(1)}, f32[136,128]{1,0:T(8,128)S(1)}, u32[]{:S(2)}, u32[]{:S(2)}) collective-permute-start(f32[136,128]{1,0:T(8,128)S(1)} %get-tuple-element.49), channel_id=1, source_target_pairs={{0,1},{1,0},{2,3},{3,2},{4,5},{5,4},{6,7},{7,6},{8,9},{9,8},{10,11... | collective-permute-start | bytes 208904 | tf_op jit(solution)/shard_map/ppermute | solution.py:369
  6.5 3.0 %collective-permute-start.4 = (f32[8,128]{1,0:T(8,128)S(1)}, f32[8,128]{1,0:T(8,128)S(1)}, u32[]{:S(2)}, u32[]{:S(2)}) collective-permute-start(f32[8,128]{1,0:T(8,128)S(1)} %get-tuple-element.50.terms), channel_id=1, source_target_pairs={{0,9},{1,8},{2,11},{3,10},{4,13},{5,12},{6,15},{7,14},{8,1},{9,0},... | collective-permute-start | bytes 12296 | tf_op jit(solution)/shard_map/ppermute | solution.py:369
  9.6 5.1 %collective-permute-start.5 = (f32[8,128]{1,0:T(8,128)S(1)}, f32[8,128]{1,0:T(8,128)S(1)}, u32[]{:S(2)}, u32[]{:S(2)}) collective-permute-start(f32[8,128]{1,0:T(8,128)S(1)} %fusion.3), channel_id=1, source_target_pairs={{0,4},{1,5},{2,6},{3,7},{4,0},{5,1},{6,2},{7,3},{8,12},{9,13},{10,... | collective-permute-start | bytes 12296 | tf_op jit(solution)/shard_map/ppermute | solution.py:369
  14.8 8.5 %collective-permute-start.6 = (f32[152,128]{1,0:T(8,128)S(1)}, f32[152,128]{1,0:T(8,128)S(1)}, u32[]{:S(2)}, u32[]{:S(2)}) collective-permute-start(f32[152,128]{1,0:T(8,128)S(1)} %get-tuple-element.83), channel_id=1, source_target_pairs={{8,16},{16,8},{24,32},{32,24},{40,48},{48,40},{56,64},{64,56},{72,... | collective-permute-start | bytes 233480 | tf_op jit(solution)/shard_map/ppermute | solution.py:369
  20.9 4.4 %collective-permute-start.7 = (f32[144,128]{1,0:T(8,128)S(1)}, f32[144,128]{1,0:T(8,128)S(1)}, u32[]{:S(2)}, u32[]{:S(2)}) collective-permute-start(f32[144,128]{1,0:T(8,128)S(1)} %get-tuple-element.58), channel_id=1, source_target_pairs={{0,8},{8,0},{16,24},{24,16},{32,40},{40,32},{48,56},{56,48},{64,72... | collective-permute-start | bytes 221192 | tf_op jit(solution)/shard_map/ppermute | solution.py:369
  23.3 3.8 %collective-permute-start.14 = (f32[40,128]{1,0:T(8,128)S(1)}, f32[40,128]{1,0:T(8,128)S(1)}, u32[]{:S(2)}, u32[]{:S(2)}) collective-permute-start(f32[40,128]{1,0:T(8,128)S(1)} %concatenate.3), channel_id=1, source_target_pairs={{0,32},{8,40},{16,48},{24,56},{32,0},{40,8},{48,16},{56,24},{64,96... | collective-permute-start | bytes 61448 | tf_op jit(solution)/shard_map/ppermute | solution.py:369
  23.3 5.5 %collective-permute-start.8 = (f32[128,128]{1,0:T(8,128)S(1)}, f32[128,128]{1,0:T(8,128)S(1)}, u32[]{:S(2)}, u32[]{:S(2)}) collective-permute-start(f32[128,128]{1,0:T(8,128)S(1)} %get-tuple-element.59), channel_id=1, source_target_pairs={{1,2},{2,1},{3,4},{4,3},{5,6},{6,5},{7,0},{0,7},{9,10},{10,9},{11,... | collective-permute-start | bytes 196616 | tf_op jit(solution)/shard_map/ppermute | solution.py:369
  23.4 5.4 %collective-permute-start.9 = (f32[128,128]{1,0:T(8,128)S(1)}, f32[128,128]{1,0:T(8,128)S(1)}, u32[]{:S(2)}, u32[]{:S(2)}) collective-permute-start(f32[128,128]{1,0:T(8,128)S(1)} %get-tuple-element.60), channel_id=1, source_target_pairs={{0,1},{1,0},{2,3},{3,2},{4,5},{5,4},{6,7},{7,6},{8,9},{9,8},{10,11... | collective-permute-start | bytes 196616 | tf_op jit(solution)/shard_map/ppermute | solution.py:369
  25.2 4.4 %collective-permute-start.10 = (f32[32,128]{1,0:T(8,128)S(1)}, f32[32,128]{1,0:T(8,128)S(1)}, u32[]{:S(2)}, u32[]{:S(2)}) collective-permute-start(f32[32,128]{1,0:T(8,128)S(1)} %get-tuple-element.64), channel_id=1, source_target_pairs={{1,2},{2,1},{3,4},{4,3},{5,6},{6,5},{7,0},{0,7},{9,10},{10,9},{11,... | collective-permute-start | bytes 49160 | tf_op jit(solution)/shard_map/ppermute | solution.py:369
  26.5 3.1 %collective-permute-start.11 = (f32[32,128]{1,0:T(8,128)S(1)}, f32[32,128]{1,0:T(8,128)S(1)}, u32[]{:S(2)}, u32[]{:S(2)}) collective-permute-start(f32[32,128]{1,0:T(8,128)S(1)} %get-tuple-element.65), channel_id=1, source_target_pairs={{0,1},{1,0},{2,3},{3,2},{4,5},{5,4},{6,7},{7,6},{8,9},{9,8},{10,11... | collective-permute-start | bytes 49160 | tf_op jit(solution)/shard_map/ppermute | solution.py:369
  27.2 4.5 %collective-permute-start.15 = (f32[8,128]{1,0:T(8,128)S(1)}, f32[8,128]{1,0:T(8,128)S(1)}, u32[]{:S(2)}, u32[]{:S(2)}) collective-permute-start(f32[8,128]{1,0:T(8,128)S(1)} %fusion), channel_id=1, source_target_pairs={{0,64},{8,72},{16,80},{24,88},{32,96},{40,104},{48,112},{56,120},{... | collective-permute-start | bytes 12296 | tf_op jit(solution)/shard_map/ppermute | solution.py:369
  31.8 8.8 %collective-permute-start.16 = (f32[72,128]{1,0:T(8,128)S(1)}, f32[72,128]{1,0:T(8,128)S(1)}, u32[]{:S(2)}, u32[]{:S(2)}) collective-permute-start(f32[72,128]{1,0:T(8,128)S(1)} %constant_dynamic-update-slice_fusion), channel_id=1, source_target_pairs={{1,2},{2,1},{3,4},{4,3},{5,6},{6,5},{7,0},{0,7},{9,10},{10,9},{11,... | collective-permute-start | bytes 110600 | tf_op jit(solution)/shard_map/ppermute | solution.py:369
  32.8 8.5 %collective-permute-start.12 = (f32[64,128]{1,0:T(8,128)S(1)}, f32[64,128]{1,0:T(8,128)S(1)}, u32[]{:S(2)}, u32[]{:S(2)}) collective-permute-start(f32[64,128]{1,0:T(8,128)S(1)} %get-tuple-element.76), channel_id=1, source_target_pairs={{8,16},{16,8},{24,32},{32,24},{40,48},{48,40},{56,64},{64,56},{72,... | collective-permute-start | bytes 98312 | tf_op jit(solution)/shard_map/ppermute | solution.py:369
  34.8 7.6 %collective-permute-start.13 = (f32[64,128]{1,0:T(8,128)S(1)}, f32[64,128]{1,0:T(8,128)S(1)}, u32[]{:S(2)}, u32[]{:S(2)}) collective-permute-start(f32[64,128]{1,0:T(8,128)S(1)} %get-tuple-element.77), channel_id=1, source_target_pairs={{0,8},{8,0},{16,24},{24,16},{32,40},{40,32},{48,56},{56,48},{64,72... | collective-permute-start | bytes 98312 | tf_op jit(solution)/shard_map/ppermute | solution.py:369
  40.6 1.9 %collective-permute-start.17 = (f32[64,128]{1,0:T(8,128)S(1)}, f32[64,128]{1,0:T(8,128)S(1)}, u32[]{:S(2)}, u32[]{:S(2)}) collective-permute-start(f32[64,128]{1,0:T(8,128)S(1)} %get-tuple-element.79), channel_id=1, source_target_pairs={{0,1},{1,0},{2,3},{3,2},{4,5},{5,4},{6,7},{7,6},{8,9},{9,8},{10,11... | collective-permute-start | bytes 98312 | tf_op jit(solution)/shard_map/ppermute | solution.py:369
  40.6 5.7 %collective-permute-start.18 = (f32[8,128]{1,0:T(8,128)S(1)}, f32[8,128]{1,0:T(8,128)S(1)}, u32[]{:S(2)}, u32[]{:S(2)}) collective-permute-start(f32[8,128]{1,0:T(8,128)S(1)} %slice_add_fusion.terms), channel_id=1, source_target_pairs={{64,128},{72,136},{80,144},{88,152},{96,160},{104,168},{112,176},{... | collective-permute-start | bytes 12296 | tf_op jit(solution)/shard_map/ppermute | solution.py:369

commit v7 on v6

--- a/solution.py
+++ b/solution.py
@@ -259,7 +259,7 @@
 
 
 def pass_kernel(
-    w, c2, azo, aze, axo, axe, basis, work_in, ylow_in, yhigh_in, inverse,
+    azo, terms, aze, axe, axo, w, c2, basis, work_in, ylow_in, yhigh_in, inverse,
     zo, ze, xo, xe, r, z_face, x_face, zl, zh, xl, xh, work, ylow, yhigh, plane
 ):
     place = where_am_i()
@@ -284,7 +284,7 @@
             message[pl.ds(FACE + k * 8, 8), :] = w[here, :] - c2[here, :] * r[here, :]
 
 
-def relay_kernel(zo, ze, ro, re):
+def relay_kernel(zo, ze, xo, xe, ro, re):
     place = where_am_i()
     z_low = place[0] == 0
     for message, up in ((ro, place[1]), (re, 1 - place[1])):
@@ -344,7 +344,7 @@
     base[...] = own[...] * own_part[pl.ds(0, 1), :]
 
 
-def last_kernel(inner, base, zo, ze, xo, xe, terms, beside, coarse_map, group, top, out):
+def last_kernel(inner, base, zo, ze, xo, terms, beside, xe, coarse_map, group, top, out):
     place = where_am_i()
     z_low, x_low = place[0] == 0, place[1] == 0
     total = terms[...] + beside[...]
@@ -399,7 +399,7 @@
     beside = move(terms, "coarse", swap(coarses, 4, 0))
     zo, ze, xo, xe, r, z_face, x_face = call(
         pass_kernel, (LINK + 8, LINK, 128, 128, 512, 128, 128), (FACE,) * 4 + inner_rows + (128,),
-        w, c2, azo, aze, axo, axe, basis, work, ylow, yhigh, inverse,
+        azo, terms, aze, axe, axo, w, c2, basis, work, ylow, yhigh, inverse,
     )
     terms = terms + beside
     zo = move(lax.dynamic_update_slice(zo, terms, (LINK, 0)), "dom", z_odd)
@@ -407,7 +407,7 @@
     terms = terms + jnp.where(is_top, zo[LINK:], 0.0)
     wide = jnp.concatenate([terms, jnp.zeros((32, 128), F32)])
     terms = terms + jnp.where(is_top, move(wide, "dom", swap(doms, 4, 0))[:8], 0.0)
-    ro, re = call(relay_kernel, (RELAY, RELAY), (), zo, ze, flops=1000)
+    ro, re = call(relay_kernel, (RELAY, RELAY), (), zo, ze, xo, xe, flops=1000)
     re, ro = move(re, "coarse", x_even), move(ro, "coarse", x_odd)
     beside = move(terms, "dom", swap(doms, 8, 0))
     first, work, ylow, yhigh = call(
@@ -423,7 +423,7 @@
     terms = terms + xo[FACE:]
     beside = move(terms, "dom", swap(doms, 8, 1))
     inner, base = call(inner_kernel, (512, 128), (128,), first, work, ylow, yhigh, basis, own_part, own, flops=1000)
-    (out,) = call(last_kernel, (512,), (), inner, base, zo, ze, xo, xe, terms, beside, coarse_map, group, top, flops=300000)
+    (out,) = call(last_kernel, (512,), (), inner, base, zo, ze, xo, terms, beside, xe, coarse_map, group, top, flops=300000)
     return out.reshape(shape)
 
 

time: 47.3 us -> 45.8 us (0.968)
  the two profiles are of different devices: /device:TPU:4 before, /device:TPU:1 now
where the time goes in v7:
time: 45.8 us; the launch traced here: 45.6 us
  starting transfers between devices  28.4 us (62%)
  waiting for transfers between devices  8.88 us (19%)
  Pallas kernels  7.76 us (17%)
    ppermute x19, starting transfers between devices, move(): return lax.ppermute(value, axis, pairs)  28.4 us
    ppermute x19, waiting for transfers between devices, move(): return lax.ppermute(value, axis, pairs)  8.88 us
    pallas_call x8, Pallas kernels, call(): pl.pallas_call(kernel, out_shape=outs, in_specs=specs, out_specs=[VMEM] *...  7.76 us
  transfers between devices with their start and end apart: 19, of which 5 were waited for; matrix products, arithmetic and copies ran while one was open for 1% of the time, Pallas kernels for 12%

profile of v7, /device:TPU:1, one launch (start us, length us, event | category | flops | bytes accessed | tf_op | source)
XLA Modules:
  0.0 45.6 jit_solution(7846045476225307657)
XLA Ops:
  0.0 0.0 copy-start
  0.0 1.5 %shard_map.91 = (f32[128,128]{1,0:T(8,128)S(1)}, f32[136,128]{1,0:T(8,128)S(1)}, f32[136,128]{1,0:T(8,128)S(1)}, f32[128,128]{1,0:T(8,128)S(1)}, f32[512,128]{1,...) custom-call(f32[512,128]{1,0:T(8,128)} %bitcast.18, ...), custom_call_target="tpu_custom_call" | custom-call | flops 300000 | bytes 1000000 | tf_op jit(solution)/shard_map/pallas_call | solution.py:43
  1.5 0.0 copy-start.1
  1.5 8.7 %collective-permute-start = (f32[128,128]{1,0:T(8,128)S(1)}, f32[128,128]{1,0:T(8,128)S(1)}, u32[]{:S(2)}, u32[]{:S(2)}) collective-permute-start(f32[128,128]{1,0:T(8,128)S(1)} %get-tuple-element.46), channel_id=1, source_target_pairs={{8,16},{16,8},{24,32},{32,24},{40,48},{48,40},{56,64},{64,56},{72,... | collective-permute-start | bytes 196616 | tf_op jit(solution)/shard_map/ppermute | solution.py:369
  10.2 0.0 collective-permute-start.3
  10.2 2.3 %collective-permute-start.2 = (f32[136,128]{1,0:T(8,128)S(1)}, f32[136,128]{1,0:T(8,128)S(1)}, u32[]{:S(2)}, u32[]{:S(2)}) collective-permute-start(f32[136,128]{1,0:T(8,128)S(1)} %get-tuple-element.50), channel_id=1, source_target_pairs={{0,8},{8,0},{16,24},{24,16},{32,40},{40,32},{48,56},{56,48},{64,72... | collective-permute-start | bytes 208904 | tf_op jit(solution)/shard_map/ppermute | solution.py:369
  12.5 0.0 collective-permute-start.1
  12.5 1.7 %collective-permute-start.4 = (f32[128,128]{1,0:T(8,128)S(1)}, f32[128,128]{1,0:T(8,128)S(1)}, u32[]{:S(2)}, u32[]{:S(2)}) collective-permute-start(f32[128,128]{1,0:T(8,128)S(1)} %get-tuple-element.51), channel_id=1, source_target_pairs={{1,2},{2,1},{3,4},{4,3},{5,6},{6,5},{7,0},{0,7},{9,10},{10,9},{11,... | collective-permute-start | bytes 196616 | tf_op jit(solution)/shard_map/ppermute | solution.py:369
  14.2 0.0 copy-done
  14.2 0.0 copy-done.1
  14.2 0.5 %shard_map.92 = (f32[840,128]{1,0:T(8,128)S(1)}, f32[160,128]{1,0:T(8,128)S(1)}, f32[160,128]{1,0:T(8,128)S(1)}, f32[1040,128]{1,0:T(8,128)S(1)}, f32[8,128]{1,0:T(8,128)S(1)}) custom-call(f32[512,128]{1,0:T(8,128)S(1)} %get-tuple-element.44.w, f32[300,1,128]{2,1,0:T(1,128)S(1)} %bitcast.12, f32[30,1,128]{2,1,0:T(1,128)S(1)} %bitcast.17, ...), custom_call_target="tpu_custom_call" | custom-call | flops 20000000 | bytes 1000000 | tf_op jit(solution)/shard_map/pallas_call | solution.py:43
  14.7 0.0 collective-permute-done.3
  14.7 0.0 collective-permute-done.2.aze
  14.8 0.0 collective-permute-done.1.axe
  14.8 0.1 fusion.3.terms
  14.8 2.9 %collective-permute-start.5 = (f32[8,128]{1,0:T(8,128)S(1)}, f32[8,128]{1,0:T(8,128)S(1)}, u32[]{:S(2)}, u32[]{:S(2)}) collective-permute-start(f32[8,128]{1,0:T(8,128)S(1)} %fusion.3.terms), channel_id=1, source_target_pairs={{0,4},{1,5},{2,6},{3,7},{4,0},{5,1},{6,2},{7,3},{8,12},{9,13},{10,... | collective-permute-start | bytes 12296 | tf_op jit(solution)/shard_map/ppermute | solution.py:369
  17.8 0.0 collective-permute-done.azo
  17.8 0.0 collective-permute-done.4.axo
  17.8 2.2 %shard_map.93 = (f32[152,128]{1,0:T(8,128)S(1)}, f32[144,128]{1,0:T(8,128)S(1)}, f32[128,128]{1,0:T(8,128)S(1)}, f32[128,128]{1,0:T(8,128)S(1)}, f32[512,128]{1,...) custom-call(f32[128,128]{1,0:T(8,128)S(1)} %collective-permute-done.azo, f32[8,128]{1,0:T(8,128)S(1)} %fusion.3.terms, ...), custom_call_target="tpu_custom_call" | custom-call | flops 15360000 | bytes 1000000 | tf_op jit(solution)/shard_map/pallas_call | solution.py:43
  20.0 0.0 collective-permute-done.5
  20.0 1.3 %collective-permute-start.6 = (f32[152,128]{1,0:T(8,128)S(1)}, f32[152,128]{1,0:T(8,128)S(1)}, u32[]{:S(2)}, u32[]{:S(2)}) collective-permute-start(f32[152,128]{1,0:T(8,128)S(1)} %get-tuple-element.83), channel_id=1, source_target_pairs={{8,16},{16,8},{24,32},{32,24},{40,48},{48,40},{56,64},{64,56},{72,... | collective-permute-start | bytes 233480 | tf_op jit(solution)/shard_map/ppermute | solution.py:369
  21.3 0.8 %collective-permute-start.7 = (f32[144,128]{1,0:T(8,128)S(1)}, f32[144,128]{1,0:T(8,128)S(1)}, u32[]{:S(2)}, u32[]{:S(2)}) collective-permute-start(f32[144,128]{1,0:T(8,128)S(1)} %get-tuple-element.58), channel_id=1, source_target_pairs={{0,8},{8,0},{16,24},{24,16},{32,40},{40,32},{48,56},{56,48},{64,72... | collective-permute-start | bytes 221192 | tf_op jit(solution)/shard_map/ppermute | solution.py:369
  22.1 1.7 %collective-permute-start.8 = (f32[128,128]{1,0:T(8,128)S(1)}, f32[128,128]{1,0:T(8,128)S(1)}, u32[]{:S(2)}, u32[]{:S(2)}) collective-permute-start(f32[128,128]{1,0:T(8,128)S(1)} %get-tuple-element.59), channel_id=1, source_target_pairs={{1,2},{2,1},{3,4},{4,3},{5,6},{6,5},{7,0},{0,7},{9,10},{10,9},{11,... | collective-permute-start | bytes 196616 | tf_op jit(solution)/shard_map/ppermute | solution.py:369
  23.8 0.1 collective-permute-start.9
  23.9 2.8 %collective-permute-done.6.zo = f32[152,128]{1,0:T(8,128)S(1)} collective-permute-done((f32[152,128]{1,0:T(8,128)S(1)}, f32[152,128]{1,0:T(8,128)S(1)}, u32[]{:S(2)}, u32[]{:S(2)}) %collective-permute-start.6) | collective-permute-done | bytes 77856 | tf_op jit(solution)/shard_map/ppermute | solution.py:369
  26.7 0.1 fusion.1
  26.7 0.0 collective-permute-start.14
  26.8 0.0 collective-permute-done.8.xo
  26.8 0.0 collective-permute-done.9.xe
  26.8 0.0 collective-permute-done.7.ze
  26.8 3.2 %collective-permute-start.10 = (f32[32,128]{1,0:T(8,128)S(1)}, f32[32,128]{1,0:T(8,128)S(1)}, u32[]{:S(2)}, u32[]{:S(2)}) collective-permute-start(f32[32,128]{1,0:T(8,128)S(1)} %get-tuple-element.64), channel_id=1, source_target_pairs={{1,2},{2,1},{3,4},{4,3},{5,6},{6,5},{7,0},{0,7},{9,10},{10,9},{11,... | collective-permute-start | bytes 49160 | tf_op jit(solution)/shard_map/ppermute | solution.py:369
  30.0 0.0 collective-permute-start.11
  30.1 0.0 collective-permute-done.14
  30.1 0.1 fusion
  30.1 0.0 collective-permute-start.15
  30.2 0.5 %shard_map.94 = (f32[512,128]{1,0:T(8,128)S(1)}, f32[840,128]{1,0:T(8,128)S(1)}, f32[160,128]{1,0:T(8,128)S(1)}, f32[160,128]{1,0:T(8,128)S(1)}) custom-call(f32[512,128]{1,0:T(8,128)S(1)} %get-tuple-element.44.w, f32[512,128]{1,0:T(8,128)S(1)} %get-tuple-element.45.c2, f32[512,128]{1,0:T(8,128)S(1)} %get-tuple-element.56.r, ...), custom_call_target="tpu_custom_call" | custom-call | flops 1000 | bytes 1000000 | tf_op jit(solution)/shard_map/pallas_call | solution.py:43
  30.6 0.8 %collective-permute-done.10.ro = f32[32,128]{1,0:T(8,128)S(1)} collective-permute-done((f32[32,128]{1,0:T(8,128)S(1)}, f32[32,128]{1,0:T(8,128)S(1)}, u32[]{:S(2)}, u32[]{:S(2)}) %collective-permute-start.10) | collective-permute-done | bytes 16416 | tf_op jit(solution)/shard_map/ppermute | solution.py:369
  31.5 0.0 collective-permute-done.11.re
  31.5 1.8 %shard_map.96 = (f32[64,128]{1,0:T(8,128)S(1)}, f32[64,128]{1,0:T(8,128)S(1)}, f32[72,128]{1,0:T(8,128)S(1)}, f32[64,128]{1,0:T(8,128)S(1)}, f32[840,128]{1,0:T(...) custom-call(f32[128,128]{1,0:T(8,128)S(1)} %collective-permute-done.azo, ...), custom_call_target="tpu_custom_call" | custom-call | flops 15360000 | bytes 1000000 | tf_op jit(solution)/shard_map/pallas_call | solution.py:43
  33.3 0.2 collective-permute-done.15
  33.5 0.1 constant_dynamic-update-slice_fusion
  33.6 4.7 %collective-permute-start.16 = (f32[72,128]{1,0:T(8,128)S(1)}, f32[72,128]{1,0:T(8,128)S(1)}, u32[]{:S(2)}, u32[]{:S(2)}) collective-permute-start(f32[72,128]{1,0:T(8,128)S(1)} %constant_dynamic-update-slice_fusion), channel_id=1, source_target_pairs={{1,2},{2,1},{3,4},{4,3},{5,6},{6,5},{7,0},{0,7},{9,10},{10,9},{11,... | collective-permute-start | bytes 110600 | tf_op jit(solution)/shard_map/ppermute | solution.py:369
  38.3 0.8 %collective-permute-start.12 = (f32[64,128]{1,0:T(8,128)S(1)}, f32[64,128]{1,0:T(8,128)S(1)}, u32[]{:S(2)}, u32[]{:S(2)}) collective-permute-start(f32[64,128]{1,0:T(8,128)S(1)} %get-tuple-element.76), channel_id=1, source_target_pairs={{8,16},{16,8},{24,32},{32,24},{40,48},{48,40},{56,64},{64,56},{72,... | collective-permute-start | bytes 98312 | tf_op jit(solution)/shard_map/ppermute | solution.py:369
  39.1 0.0 collective-permute-start.13
  39.1 0.1 collective-permute-start.18
  39.2 0.8 %collective-permute-done.16.xo = f32[72,128]{1,0:T(8,128)S(1)} collective-permute-done((f32[72,128]{1,0:T(8,128)S(1)}, f32[72,128]{1,0:T(8,128)S(1)}, u32[]{:S(2)}, u32[]{:S(2)}) %collective-permute-start.16) | collective-permute-done | bytes 36896 | tf_op jit(solution)/shard_map/ppermute | solution.py:369
  40.0 0.1 slice_add_fusion.terms
  40.0 0.0 collective-permute-start.17
  40.0 0.4 shard_map.97
  40.5 4.2 %collective-permute-done.12.zo = f32[64,128]{1,0:T(8,128)S(1)} collective-permute-done((f32[64,128]{1,0:T(8,128)S(1)}, f32[64,128]{1,0:T(8,128)S(1)}, u32[]{:S(2)}, u32[]{:S(2)}) %collective-permute-start.12) | collective-permute-done | bytes 32800 | tf_op jit(solution)/shard_map/ppermute | solution.py:369
  44.7 0.0 collective-permute-done.13.ze
  44.7 0.0 collective-permute-done.18.xe
  44.7 0.0 collective-permute-done.17.beside
  44.7 0.9 %shard_map.98 = f32[512,128]{1,0:T(8,128)} custom-call(f32[512,128]{1,0:T(8,128)S(1)} %get-tuple-element.74.inner, f32[128,128]{1,0:T(8,128)S(1)} %get-tuple-element.75.base, f32[64,128]{1,0:T(8,128)S(1)} %collective-permute-done.12.zo, f32[64,128]{1,0:T(8,128)S(1)} %collective-permute-done.13.ze, f32[72,128]{1,0:T(8,128)S(1)} %collective-permute-done.16.xo, ...), custom_call_target="tpu_custom_call" | custom-call | flops 300000 | bytes 1000000 | tf_op jit(solution)/shard_map/pallas_call | solution.py:43
  (4 shorter events, 0.0 us)
Async XLA Ops:
  0.0 14.2 %copy-start = (f32[3,10,10,1,1,128]{5,4,3,2,1,0:T(1,128)S(1)}, f32[3,10,10,1,1,128]{5,4,3,2,1,0:T(1,128)}, u32[]{:S(2)}) copy-start(f32[3,10,10,1,1,128]{5,4,3,2,1,0:T(1,128)} %param.12) | copy-start | bytes 460804
  1.5 12.7 %copy-start.1 = (f32[3,10,1,1,128]{4,3,2,1,0:T(1,128)S(1)}, f32[3,10,1,1,128]{4,3,2,1,0:T(1,128)}, u32[]{:S(2)}) copy-start(f32[3,10,1,1,128]{4,3,2,1,0:T(1,128)} %param.13) | copy-start | bytes 46084
  1.5 16.3 %collective-permute-start = (f32[128,128]{1,0:T(8,128)S(1)}, f32[128,128]{1,0:T(8,128)S(1)}, u32[]{:S(2)}, u32[]{:S(2)}) collective-permute-start(f32[128,128]{1,0:T(8,128)S(1)} %get-tuple-element.46), channel_id=1, source_target_pairs={{8,16},{16,8},{24,32},{32,24},{40,48},{48,40},{56,64},{64,56},{72,... | collective-permute-start | bytes 196616 | tf_op jit(solution)/shard_map/ppermute | solution.py:369
  10.2 4.5 %collective-permute-start.3 = (f32[8,128]{1,0:T(8,128)S(1)}, f32[8,128]{1,0:T(8,128)S(1)}, u32[]{:S(2)}, u32[]{:S(2)}) collective-permute-start(f32[8,128]{1,0:T(8,128)S(1)} %get-tuple-element.47.terms), channel_id=1, source_target_pairs={{0,9},{1,8},{2,11},{3,10},{4,13},{5,12},{6,15},{7,14},{8,1},{9,0},... | collective-permute-start | bytes 12296 | tf_op jit(solution)/shard_map/ppermute | solution.py:369
  10.2 4.6 %collective-permute-start.2 = (f32[136,128]{1,0:T(8,128)S(1)}, f32[136,128]{1,0:T(8,128)S(1)}, u32[]{:S(2)}, u32[]{:S(2)}) collective-permute-start(f32[136,128]{1,0:T(8,128)S(1)} %get-tuple-element.50), channel_id=1, source_target_pairs={{0,8},{8,0},{16,24},{24,16},{32,40},{40,32},{48,56},{56,48},{64,72... | collective-permute-start | bytes 208904 | tf_op jit(solution)/shard_map/ppermute | solution.py:369
  12.5 2.3 %collective-permute-start.1 = (f32[136,128]{1,0:T(8,128)S(1)}, f32[136,128]{1,0:T(8,128)S(1)}, u32[]{:S(2)}, u32[]{:S(2)}) collective-permute-start(f32[136,128]{1,0:T(8,128)S(1)} %get-tuple-element.49), channel_id=1, source_target_pairs={{0,1},{1,0},{2,3},{3,2},{4,5},{5,4},{6,7},{7,6},{8,9},{9,8},{10,11... | collective-permute-start | bytes 208904 | tf_op jit(solution)/shard_map/ppermute | solution.py:369
  12.5 5.3 %collective-permute-start.4 = (f32[128,128]{1,0:T(8,128)S(1)}, f32[128,128]{1,0:T(8,128)S(1)}, u32[]{:S(2)}, u32[]{:S(2)}) collective-permute-start(f32[128,128]{1,0:T(8,128)S(1)} %get-tuple-element.51), channel_id=1, source_target_pairs={{1,2},{2,1},{3,4},{4,3},{5,6},{6,5},{7,0},{0,7},{9,10},{10,9},{11,... | collective-permute-start | bytes 196616 | tf_op jit(solution)/shard_map/ppermute | solution.py:369
  14.8 5.1 %collective-permute-start.5 = (f32[8,128]{1,0:T(8,128)S(1)}, f32[8,128]{1,0:T(8,128)S(1)}, u32[]{:S(2)}, u32[]{:S(2)}) collective-permute-start(f32[8,128]{1,0:T(8,128)S(1)} %fusion.3.terms), channel_id=1, source_target_pairs={{0,4},{1,5},{2,6},{3,7},{4,0},{5,1},{6,2},{7,3},{8,12},{9,13},{10,... | collective-permute-start | bytes 12296 | tf_op jit(solution)/shard_map/ppermute | solution.py:369
  20.0 6.7 %collective-permute-start.6 = (f32[152,128]{1,0:T(8,128)S(1)}, f32[152,128]{1,0:T(8,128)S(1)}, u32[]{:S(2)}, u32[]{:S(2)}) collective-permute-start(f32[152,128]{1,0:T(8,128)S(1)} %get-tuple-element.83), channel_id=1, source_target_pairs={{8,16},{16,8},{24,32},{32,24},{40,48},{48,40},{56,64},{64,56},{72,... | collective-permute-start | bytes 233480 | tf_op jit(solution)/shard_map/ppermute | solution.py:369
  21.3 5.5 %collective-permute-start.7 = (f32[144,128]{1,0:T(8,128)S(1)}, f32[144,128]{1,0:T(8,128)S(1)}, u32[]{:S(2)}, u32[]{:S(2)}) collective-permute-start(f32[144,128]{1,0:T(8,128)S(1)} %get-tuple-element.58), channel_id=1, source_target_pairs={{0,8},{8,0},{16,24},{24,16},{32,40},{40,32},{48,56},{56,48},{64,72... | collective-permute-start | bytes 221192 | tf_op jit(solution)/shard_map/ppermute | solution.py:369
  22.1 4.7 %collective-permute-start.8 = (f32[128,128]{1,0:T(8,128)S(1)}, f32[128,128]{1,0:T(8,128)S(1)}, u32[]{:S(2)}, u32[]{:S(2)}) collective-permute-start(f32[128,128]{1,0:T(8,128)S(1)} %get-tuple-element.59), channel_id=1, source_target_pairs={{1,2},{2,1},{3,4},{4,3},{5,6},{6,5},{7,0},{0,7},{9,10},{10,9},{11,... | collective-permute-start | bytes 196616 | tf_op jit(solution)/shard_map/ppermute | solution.py:369
  23.8 3.0 %collective-permute-start.9 = (f32[128,128]{1,0:T(8,128)S(1)}, f32[128,128]{1,0:T(8,128)S(1)}, u32[]{:S(2)}, u32[]{:S(2)}) collective-permute-start(f32[128,128]{1,0:T(8,128)S(1)} %get-tuple-element.60), channel_id=1, source_target_pairs={{0,1},{1,0},{2,3},{3,2},{4,5},{5,4},{6,7},{7,6},{8,9},{9,8},{10,11... | collective-permute-start | bytes 196616 | tf_op jit(solution)/shard_map/ppermute | solution.py:369
  26.7 3.3 %collective-permute-start.14 = (f32[40,128]{1,0:T(8,128)S(1)}, f32[40,128]{1,0:T(8,128)S(1)}, u32[]{:S(2)}, u32[]{:S(2)}) collective-permute-start(f32[40,128]{1,0:T(8,128)S(1)} %concatenate.3), channel_id=1, source_target_pairs={{0,32},{8,40},{16,48},{24,56},{32,0},{40,8},{48,16},{56,24},{64,96... | collective-permute-start | bytes 61448 | tf_op jit(solution)/shard_map/ppermute | solution.py:369
  26.8 4.6 %collective-permute-start.10 = (f32[32,128]{1,0:T(8,128)S(1)}, f32[32,128]{1,0:T(8,128)S(1)}, u32[]{:S(2)}, u32[]{:S(2)}) collective-permute-start(f32[32,128]{1,0:T(8,128)S(1)} %get-tuple-element.64), channel_id=1, source_target_pairs={{1,2},{2,1},{3,4},{4,3},{5,6},{6,5},{7,0},{0,7},{9,10},{10,9},{11,... | collective-permute-start | bytes 49160 | tf_op jit(solution)/shard_map/ppermute | solution.py:369
  30.0 1.4 %collective-permute-start.11 = (f32[32,128]{1,0:T(8,128)S(1)}, f32[32,128]{1,0:T(8,128)S(1)}, u32[]{:S(2)}, u32[]{:S(2)}) collective-permute-start(f32[32,128]{1,0:T(8,128)S(1)} %get-tuple-element.65), channel_id=1, source_target_pairs={{0,1},{1,0},{2,3},{3,2},{4,5},{5,4},{6,7},{7,6},{8,9},{9,8},{10,11... | collective-permute-start | bytes 49160 | tf_op jit(solution)/shard_map/ppermute | solution.py:369
  30.1 3.4 %collective-permute-start.15 = (f32[8,128]{1,0:T(8,128)S(1)}, f32[8,128]{1,0:T(8,128)S(1)}, u32[]{:S(2)}, u32[]{:S(2)}) collective-permute-start(f32[8,128]{1,0:T(8,128)S(1)} %fusion), channel_id=1, source_target_pairs={{0,64},{8,72},{16,80},{24,88},{32,96},{40,104},{48,112},{56,120},{... | collective-permute-start | bytes 12296 | tf_op jit(solution)/shard_map/ppermute | solution.py:369
  33.6 6.4 %collective-permute-start.16 = (f32[72,128]{1,0:T(8,128)S(1)}, f32[72,128]{1,0:T(8,128)S(1)}, u32[]{:S(2)}, u32[]{:S(2)}) collective-permute-start(f32[72,128]{1,0:T(8,128)S(1)} %constant_dynamic-update-slice_fusion), channel_id=1, source_target_pairs={{1,2},{2,1},{3,4},{4,3},{5,6},{6,5},{7,0},{0,7},{9,10},{10,9},{11,... | collective-permute-start | bytes 110600 | tf_op jit(solution)/shard_map/ppermute | solution.py:369
  38.3 6.4 %collective-permute-start.12 = (f32[64,128]{1,0:T(8,128)S(1)}, f32[64,128]{1,0:T(8,128)S(1)}, u32[]{:S(2)}, u32[]{:S(2)}) collective-permute-start(f32[64,128]{1,0:T(8,128)S(1)} %get-tuple-element.76), channel_id=1, source_target_pairs={{8,16},{16,8},{24,32},{32,24},{40,48},{48,40},{56,64},{64,56},{72,... | collective-permute-start | bytes 98312 | tf_op jit(solution)/shard_map/ppermute | solution.py:369
  39.1 5.6 %collective-permute-start.13 = (f32[64,128]{1,0:T(8,128)S(1)}, f32[64,128]{1,0:T(8,128)S(1)}, u32[]{:S(2)}, u32[]{:S(2)}) collective-permute-start(f32[64,128]{1,0:T(8,128)S(1)} %get-tuple-element.77), channel_id=1, source_target_pairs={{0,8},{8,0},{16,24},{24,16},{32,40},{40,32},{48,56},{56,48},{64,72... | collective-permute-start | bytes 98312 | tf_op jit(solution)/shard_map/ppermute | solution.py:369
  39.1 5.6 %collective-permute-start.18 = (f32[64,128]{1,0:T(8,128)S(1)}, f32[64,128]{1,0:T(8,128)S(1)}, u32[]{:S(2)}, u32[]{:S(2)}) collective-permute-start(f32[64,128]{1,0:T(8,128)S(1)} %get-tuple-element.79), channel_id=1, source_target_pairs={{0,1},{1,0},{2,3},{3,2},{4,5},{5,4},{6,7},{7,6},{8,9},{9,8},{10,11... | collective-permute-start | bytes 98312 | tf_op jit(solution)/shard_map/ppermute | solution.py:369
  40.0 4.7 %collective-permute-start.17 = (f32[8,128]{1,0:T(8,128)S(1)}, f32[8,128]{1,0:T(8,128)S(1)}, u32[]{:S(2)}, u32[]{:S(2)}) collective-permute-start(f32[8,128]{1,0:T(8,128)S(1)} %slice_add_fusion.terms), channel_id=1, source_target_pairs={{64,128},{72,136},{80,144},{88,152},{96,160},{104,168},{112,176},{... | collective-permute-start | bytes 12296 | tf_op jit(solution)/shard_map/ppermute | solution.py:369

commit v8 on v7

--- a/solution.py
+++ b/solution.py
@@ -344,18 +344,26 @@
     base[...] = own[...] * own_part[pl.ds(0, 1), :]
 
 
-def last_kernel(inner, base, zo, ze, xo, terms, beside, xe, coarse_map, group, top, out):
+def correct(sums, coarse_map):
+    sol = jnp.sum(sums, axis=1, keepdims=True)
+    hit = lax.broadcasted_iota(jnp.int32, (128, 128), 0) == coarse_map[pl.ds(0, 1), :]
+    return jnp.sum(jnp.where(hit, sol, 0.0), axis=0, keepdims=True)
+
+
+def add_top(sums, top, total):
+    for at in range(4):
+        product = top[:, at * 128 : (at + 1) * 128] * total[pl.ds(at, 1), :]
+        sums = product if sums is None else sums + product
+    return sums
+
+
+def gather_kernel(inner, base, zo, ze, xo, xe, terms, coarse_map, group, top, out):
     place = where_am_i()
     z_low, x_low = place[0] == 0, place[1] == 0
-    total = terms[...] + beside[...]
     sums = base[...]
     for at in range(2):
         sums = sums + group[:, at * 128 : (at + 1) * 128] * terms[pl.ds(4 + at, 1), :]
-    for at in range(4):
-        sums = sums + top[:, at * 128 : (at + 1) * 128] * total[at : at + 1]
-    sol = jnp.sum(sums, axis=1, keepdims=True)
-    hit = lax.broadcasted_iota(jnp.int32, (128, 128), 0) == coarse_map[pl.ds(0, 1), :]
-    out[...] = inner[...] + jnp.sum(jnp.where(hit, sol, 0.0), axis=0, keepdims=True)
+    out[...] = inner[...] + correct(add_top(sums, top, terms), coarse_map)
     out[layer(7), :] += pick(z_low, ze, zo, 0, FACE)
     out[layer(0), :] += pick(z_low, zo, ze, 0, FACE)
     above = keep(place[3], pick(x_low, xe, xo, 0, FACE))
@@ -363,6 +371,10 @@
     for k in range(8):
         out[pl.ds(k * 64 + 56, 8), :] += above[k * 8 : k * 8 + 8]
         out[pl.ds(k * 64, 8), :] += below[k * 8 : k * 8 + 8]
+
+
+def last_kernel(gathered, beside, coarse_map, top, out):
+    out[...] = gathered[...] + correct(add_top(None, top, beside), coarse_map)
 
 
 def move(value, axis, pairs):
@@ -406,10 +418,10 @@
     ze, xe, xo = move(ze, "dom", z_even), move(xe, "coarse", x_even), move(xo, "coarse", x_odd)
     terms = terms + jnp.where(is_top, zo[LINK:], 0.0)
     wide = jnp.concatenate([terms, jnp.zeros((32, 128), F32)])
-    terms = terms + jnp.where(is_top, move(wide, "dom", swap(doms, 4, 0))[:8], 0.0)
+    terms = terms + jnp.where(is_top, move(wide, "dom", swap(doms, 8, 0))[:8], 0.0)
     ro, re = call(relay_kernel, (RELAY, RELAY), (), zo, ze, xo, xe, flops=1000)
     re, ro = move(re, "coarse", x_even), move(ro, "coarse", x_odd)
-    beside = move(terms, "dom", swap(doms, 8, 0))
+    beside = move(terms, "dom", swap(doms, 8, 1))
     first, work, ylow, yhigh = call(
         second_own_kernel, (512,) + inner_rows, (512, 128), w, c2, r, zo, ze, xo, xe, basis, flops=1000
     )
@@ -421,9 +433,10 @@
     xo = move(lax.dynamic_update_slice(do, terms, (FACE, 0)), "coarse", x_odd)
     zo, ze, xe = move(co, "dom", z_odd), move(ce, "dom", z_even), move(de, "coarse", x_even)
     terms = terms + xo[FACE:]
-    beside = move(terms, "dom", swap(doms, 8, 1))
+    beside = move(terms, "dom", swap(doms, 4, 0))
     inner, base = call(inner_kernel, (512, 128), (128,), first, work, ylow, yhigh, basis, own_part, own, flops=1000)
-    (out,) = call(last_kernel, (512,), (), inner, base, zo, ze, xo, terms, beside, xe, coarse_map, group, top, flops=300000)
+    (gathered,) = call(gather_kernel, (512,), (), inner, base, zo, ze, xo, xe, terms, coarse_map, group, top, flops=1000)
+    (out,) = call(last_kernel, (512,), (), gathered, beside, coarse_map, top, flops=1000)
     return out.reshape(shape)
 
 

time: 45.8 us -> 47.9 us (1.046)
  starting transfers between devices: 28.4 us -> 30.8 us
    ppermute x19, starting transfers between devices: 28.4 us -> 30.8 us  [move(): return lax.ppermute(value, axis, pairs)]
    pallas_call x8 -> x9, Pallas kernels: 7.76 us -> 7.88 us  [call(): pl.pallas_call(kernel, out_shape=outs, in_specs=specs, out_specs=[VMEM] *...]
where the time goes in v8:
time: 47.9 us; the launch traced here: 47.8 us
  starting transfers between devices  30.8 us (64%)
  waiting for transfers between devices  8.59 us (18%)
  Pallas kernels  7.88 us (16%)
    ppermute x19, starting transfers between devices, move(): return lax.ppermute(value, axis, pairs)  30.8 us
    ppermute x19, waiting for transfers between devices, move(): return lax.ppermute(value, axis, pairs)  8.59 us
    pallas_call x9, Pallas kernels, call(): pl.pallas_call(kernel, out_shape=outs, in_specs=specs, out_specs=[VMEM] *...  7.88 us
  transfers between devices with their start and end apart: 19, of which 5 were waited for; matrix products, arithmetic and copies ran while one was open for 1% of the time, Pallas kernels for 12%

profile of v8, /device:TPU:1, one launch (start us, length us, event | category | flops | bytes accessed | tf_op | source)
XLA Modules:
  0.0 47.8 jit_solution(2891954533307150024)
XLA Ops:
  0.0 0.0 copy-start
  0.0 1.5 %shard_map.91 = (f32[128,128]{1,0:T(8,128)S(1)}, f32[136,128]{1,0:T(8,128)S(1)}, f32[136,128]{1,0:T(8,128)S(1)}, f32[128,128]{1,0:T(8,128)S(1)}, f32[512,128]{1,...) custom-call(f32[512,128]{1,0:T(8,128)} %bitcast.18, ...), custom_call_target="tpu_custom_call" | custom-call | flops 300000 | bytes 1000000 | tf_op jit(solution)/shard_map/pallas_call | solution.py:43
  1.5 0.0 copy-start.1
  1.5 8.7 %collective-permute-start = (f32[128,128]{1,0:T(8,128)S(1)}, f32[128,128]{1,0:T(8,128)S(1)}, u32[]{:S(2)}, u32[]{:S(2)}) collective-permute-start(f32[128,128]{1,0:T(8,128)S(1)} %get-tuple-element.46), channel_id=1, source_target_pairs={{8,16},{16,8},{24,32},{32,24},{40,48},{48,40},{56,64},{64,56},{72,... | collective-permute-start | bytes 196616 | tf_op jit(solution)/shard_map/ppermute | solution.py:381
  10.2 0.0 collective-permute-start.3
  10.2 2.3 %collective-permute-start.2 = (f32[136,128]{1,0:T(8,128)S(1)}, f32[136,128]{1,0:T(8,128)S(1)}, u32[]{:S(2)}, u32[]{:S(2)}) collective-permute-start(f32[136,128]{1,0:T(8,128)S(1)} %get-tuple-element.50), channel_id=1, source_target_pairs={{0,8},{8,0},{16,24},{24,16},{32,40},{40,32},{48,56},{56,48},{64,72... | collective-permute-start | bytes 208904 | tf_op jit(solution)/shard_map/ppermute | solution.py:381
  12.5 0.0 collective-permute-start.1
  12.5 1.7 %collective-permute-start.4 = (f32[128,128]{1,0:T(8,128)S(1)}, f32[128,128]{1,0:T(8,128)S(1)}, u32[]{:S(2)}, u32[]{:S(2)}) collective-permute-start(f32[128,128]{1,0:T(8,128)S(1)} %get-tuple-element.51), channel_id=1, source_target_pairs={{1,2},{2,1},{3,4},{4,3},{5,6},{6,5},{7,0},{0,7},{9,10},{10,9},{11,... | collective-permute-start | bytes 196616 | tf_op jit(solution)/shard_map/ppermute | solution.py:381
  14.2 0.0 copy-done
  14.2 0.0 copy-done.1
  14.2 0.5 %shard_map.92 = (f32[840,128]{1,0:T(8,128)S(1)}, f32[160,128]{1,0:T(8,128)S(1)}, f32[160,128]{1,0:T(8,128)S(1)}, f32[1040,128]{1,0:T(8,128)S(1)}, f32[8,128]{1,0:T(8,128)S(1)}) custom-call(f32[512,128]{1,0:T(8,128)S(1)} %get-tuple-element.44.w, f32[300,1,128]{2,1,0:T(1,128)S(1)} %bitcast.12, f32[30,1,128]{2,1,0:T(1,128)S(1)} %bitcast.17, ...), custom_call_target="tpu_custom_call" | custom-call | flops 20000000 | bytes 1000000 | tf_op jit(solution)/shard_map/pallas_call | solution.py:43
  14.7 0.0 collective-permute-done.3
  14.7 0.0 collective-permute-done.2.aze
  14.8 0.0 collective-permute-done.1.axe
  14.8 0.1 fusion.3.terms
  14.8 2.9 %collective-permute-start.5 = (f32[8,128]{1,0:T(8,128)S(1)}, f32[8,128]{1,0:T(8,128)S(1)}, u32[]{:S(2)}, u32[]{:S(2)}) collective-permute-start(f32[8,128]{1,0:T(8,128)S(1)} %fusion.3.terms), channel_id=1, source_target_pairs={{0,4},{1,5},{2,6},{3,7},{4,0},{5,1},{6,2},{7,3},{8,12},{9,13},{10,... | collective-permute-start | bytes 12296 | tf_op jit(solution)/shard_map/ppermute | solution.py:381
  17.8 0.0 collective-permute-done.azo
  17.8 0.0 collective-permute-done.4.axo
  17.8 2.2 %shard_map.93 = (f32[152,128]{1,0:T(8,128)S(1)}, f32[144,128]{1,0:T(8,128)S(1)}, f32[128,128]{1,0:T(8,128)S(1)}, f32[128,128]{1,0:T(8,128)S(1)}, f32[512,128]{1,...) custom-call(f32[128,128]{1,0:T(8,128)S(1)} %collective-permute-done.azo, f32[8,128]{1,0:T(8,128)S(1)} %fusion.3.terms, ...), custom_call_target="tpu_custom_call" | custom-call | flops 15360000 | bytes 1000000 | tf_op jit(solution)/shard_map/pallas_call | solution.py:43
  20.0 0.0 collective-permute-done.5
  20.0 1.3 %collective-permute-start.6 = (f32[152,128]{1,0:T(8,128)S(1)}, f32[152,128]{1,0:T(8,128)S(1)}, u32[]{:S(2)}, u32[]{:S(2)}) collective-permute-start(f32[152,128]{1,0:T(8,128)S(1)} %get-tuple-element.83), channel_id=1, source_target_pairs={{8,16},{16,8},{24,32},{32,24},{40,48},{48,40},{56,64},{64,56},{72,... | collective-permute-start | bytes 233480 | tf_op jit(solution)/shard_map/ppermute | solution.py:381
  21.3 0.8 %collective-permute-start.7 = (f32[144,128]{1,0:T(8,128)S(1)}, f32[144,128]{1,0:T(8,128)S(1)}, u32[]{:S(2)}, u32[]{:S(2)}) collective-permute-start(f32[144,128]{1,0:T(8,128)S(1)} %get-tuple-element.58), channel_id=1, source_target_pairs={{0,8},{8,0},{16,24},{24,16},{32,40},{40,32},{48,56},{56,48},{64,72... | collective-permute-start | bytes 221192 | tf_op jit(solution)/shard_map/ppermute | solution.py:381
  22.1 1.7 %collective-permute-start.8 = (f32[128,128]{1,0:T(8,128)S(1)}, f32[128,128]{1,0:T(8,128)S(1)}, u32[]{:S(2)}, u32[]{:S(2)}) collective-permute-start(f32[128,128]{1,0:T(8,128)S(1)} %get-tuple-element.59), channel_id=1, source_target_pairs={{1,2},{2,1},{3,4},{4,3},{5,6},{6,5},{7,0},{0,7},{9,10},{10,9},{11,... | collective-permute-start | bytes 196616 | tf_op jit(solution)/shard_map/ppermute | solution.py:381
  23.8 0.1 collective-permute-start.9
  23.9 2.8 %collective-permute-done.6.zo = f32[152,128]{1,0:T(8,128)S(1)} collective-permute-done((f32[152,128]{1,0:T(8,128)S(1)}, f32[152,128]{1,0:T(8,128)S(1)}, u32[]{:S(2)}, u32[]{:S(2)}) %collective-permute-start.6) | collective-permute-done | bytes 77856 | tf_op jit(solution)/shard_map/ppermute | solution.py:381
  26.7 0.1 fusion.1
  26.7 0.0 collective-permute-start.14
  26.8 0.0 collective-permute-done.8.xo
  26.8 0.0 collective-permute-done.9.xe
  26.8 0.0 collective-permute-done.7.ze
  26.8 3.2 %collective-permute-start.10 = (f32[32,128]{1,0:T(8,128)S(1)}, f32[32,128]{1,0:T(8,128)S(1)}, u32[]{:S(2)}, u32[]{:S(2)}) collective-permute-start(f32[32,128]{1,0:T(8,128)S(1)} %get-tuple-element.64), channel_id=1, source_target_pairs={{1,2},{2,1},{3,4},{4,3},{5,6},{6,5},{7,0},{0,7},{9,10},{10,9},{11,... | collective-permute-start | bytes 49160 | tf_op jit(solution)/shard_map/ppermute | solution.py:381
  30.0 0.0 collective-permute-start.11
  30.1 0.2 collective-permute-done.14
  30.3 0.1 fusion
  30.4 1.8 %collective-permute-start.15 = (f32[8,128]{1,0:T(8,128)S(1)}, f32[8,128]{1,0:T(8,128)S(1)}, u32[]{:S(2)}, u32[]{:S(2)}) collective-permute-start(f32[8,128]{1,0:T(8,128)S(1)} %fusion), channel_id=1, source_target_pairs={{64,128},{72,136},{80,144},{88,152},{96,160},{104,168},{112,176},{... | collective-permute-start | bytes 12296 | tf_op jit(solution)/shard_map/ppermute | solution.py:381
  32.2 0.5 shard_map.94
  32.7 0.0 collective-permute-done.10.ro
  32.7 0.0 collective-permute-done.11.re
  32.7 1.8 %shard_map.96 = (f32[64,128]{1,0:T(8,128)S(1)}, f32[64,128]{1,0:T(8,128)S(1)}, f32[72,128]{1,0:T(8,128)S(1)}, f32[64,128]{1,0:T(8,128)S(1)}, f32[840,128]{1,0:T(...) custom-call(f32[128,128]{1,0:T(8,128)S(1)} %collective-permute-done.azo, ...), custom_call_target="tpu_custom_call" | custom-call | flops 15360000 | bytes 1000000 | tf_op jit(solution)/shard_map/pallas_call | solution.py:43
  34.5 0.4 collective-permute-done.15
  34.9 0.1 constant_dynamic-update-slice_fusion
  35.0 5.4 %collective-permute-start.16 = (f32[72,128]{1,0:T(8,128)S(1)}, f32[72,128]{1,0:T(8,128)S(1)}, u32[]{:S(2)}, u32[]{:S(2)}) collective-permute-start(f32[72,128]{1,0:T(8,128)S(1)} %constant_dynamic-update-slice_fusion), channel_id=1, source_target_pairs={{1,2},{2,1},{3,4},{4,3},{5,6},{6,5},{7,0},{0,7},{9,10},{10,9},{11,... | collective-permute-start | bytes 110600 | tf_op jit(solution)/shard_map/ppermute | solution.py:381
  40.4 0.8 %collective-permute-start.12 = (f32[64,128]{1,0:T(8,128)S(1)}, f32[64,128]{1,0:T(8,128)S(1)}, u32[]{:S(2)}, u32[]{:S(2)}) collective-permute-start(f32[64,128]{1,0:T(8,128)S(1)} %get-tuple-element.76), channel_id=1, source_target_pairs={{8,16},{16,8},{24,32},{32,24},{40,48},{48,40},{56,64},{64,56},{72,... | collective-permute-start | bytes 98312 | tf_op jit(solution)/shard_map/ppermute | solution.py:381
  41.2 0.0 collective-permute-start.13
  41.2 0.0 collective-permute-start.17
  41.2 0.9 %collective-permute-done.16.xo = f32[72,128]{1,0:T(8,128)S(1)} collective-permute-done((f32[72,128]{1,0:T(8,128)S(1)}, f32[72,128]{1,0:T(8,128)S(1)}, u32[]{:S(2)}, u32[]{:S(2)}) %collective-permute-start.16) | collective-permute-done | bytes 36896 | tf_op jit(solution)/shard_map/ppermute | solution.py:381
  42.1 0.1 slice_add_fusion.terms
  42.1 0.0 collective-permute-start.18
  42.1 0.4 shard_map.97
  42.6 4.2 %collective-permute-done.12.zo = f32[64,128]{1,0:T(8,128)S(1)} collective-permute-done((f32[64,128]{1,0:T(8,128)S(1)}, f32[64,128]{1,0:T(8,128)S(1)}, u32[]{:S(2)}, u32[]{:S(2)}) %collective-permute-start.12) | collective-permute-done | bytes 32800 | tf_op jit(solution)/shard_map/ppermute | solution.py:381
  46.8 0.0 collective-permute-done.13.ze
  46.8 0.0 collective-permute-done.17.xe
  46.8 0.1 shard_map.98.gathered
  47.0 0.0 collective-permute-done.18.beside
  47.0 0.8 %shard_map.99 = f32[512,128]{1,0:T(8,128)} custom-call(f32[512,128]{1,0:T(8,128)S(1)} %shard_map.98.gathered, f32[8,128]{1,0:T(8,128)S(1)} %collective-permute-done.18.beside, s32[1,128]{1,0:T(1,128)S(1)} %get-tuple-element.80.coarse_map, f32[128,512]{1,0:T(8,128)S(1)} %get-tuple-element.82.top), custom_call_target="tpu_custom_call" | custom-call | flops 1000 | bytes 1000000 | tf_op jit(solution)/shard_map/pallas_call | solution.py:43
  (4 shorter events, 0.0 us)
Async XLA Ops:
  0.0 14.2 %copy-start = (f32[3,10,10,1,1,128]{5,4,3,2,1,0:T(1,128)S(1)}, f32[3,10,10,1,1,128]{5,4,3,2,1,0:T(1,128)}, u32[]{:S(2)}) copy-start(f32[3,10,10,1,1,128]{5,4,3,2,1,0:T(1,128)} %param.12) | copy-start | bytes 460804
  1.5 12.7 %copy-start.1 = (f32[3,10,1,1,128]{4,3,2,1,0:T(1,128)S(1)}, f32[3,10,1,1,128]{4,3,2,1,0:T(1,128)}, u32[]{:S(2)}) copy-start(f32[3,10,1,1,128]{4,3,2,1,0:T(1,128)} %param.13) | copy-start | bytes 46084
  1.5 16.3 %collective-permute-start = (f32[128,128]{1,0:T(8,128)S(1)}, f32[128,128]{1,0:T(8,128)S(1)}, u32[]{:S(2)}, u32[]{:S(2)}) collective-permute-start(f32[128,128]{1,0:T(8,128)S(1)} %get-tuple-element.46), channel_id=1, source_target_pairs={{8,16},{16,8},{24,32},{32,24},{40,48},{48,40},{56,64},{64,56},{72,... | collective-permute-start | bytes 196616 | tf_op jit(solution)/shard_map/ppermute | solution.py:381
  10.2 4.5 %collective-permute-start.3 = (f32[8,128]{1,0:T(8,128)S(1)}, f32[8,128]{1,0:T(8,128)S(1)}, u32[]{:S(2)}, u32[]{:S(2)}) collective-permute-start(f32[8,128]{1,0:T(8,128)S(1)} %get-tuple-element.47.terms), channel_id=1, source_target_pairs={{0,9},{1,8},{2,11},{3,10},{4,13},{5,12},{6,15},{7,14},{8,1},{9,0},... | collective-permute-start | bytes 12296 | tf_op jit(solution)/shard_map/ppermute | solution.py:381
  10.2 4.6 %collective-permute-start.2 = (f32[136,128]{1,0:T(8,128)S(1)}, f32[136,128]{1,0:T(8,128)S(1)}, u32[]{:S(2)}, u32[]{:S(2)}) collective-permute-start(f32[136,128]{1,0:T(8,128)S(1)} %get-tuple-element.50), channel_id=1, source_target_pairs={{0,8},{8,0},{16,24},{24,16},{32,40},{40,32},{48,56},{56,48},{64,72... | collective-permute-start | bytes 208904 | tf_op jit(solution)/shard_map/ppermute | solution.py:381
  12.5 2.3 %collective-permute-start.1 = (f32[136,128]{1,0:T(8,128)S(1)}, f32[136,128]{1,0:T(8,128)S(1)}, u32[]{:S(2)}, u32[]{:S(2)}) collective-permute-start(f32[136,128]{1,0:T(8,128)S(1)} %get-tuple-element.49), channel_id=1, source_target_pairs={{0,1},{1,0},{2,3},{3,2},{4,5},{5,4},{6,7},{7,6},{8,9},{9,8},{10,11... | collective-permute-start | bytes 208904 | tf_op jit(solution)/shard_map/ppermute | solution.py:381
  12.5 5.3 %collective-permute-start.4 = (f32[128,128]{1,0:T(8,128)S(1)}, f32[128,128]{1,0:T(8,128)S(1)}, u32[]{:S(2)}, u32[]{:S(2)}) collective-permute-start(f32[128,128]{1,0:T(8,128)S(1)} %get-tuple-element.51), channel_id=1, source_target_pairs={{1,2},{2,1},{3,4},{4,3},{5,6},{6,5},{7,0},{0,7},{9,10},{10,9},{11,... | collective-permute-start | bytes 196616 | tf_op jit(solution)/shard_map/ppermute | solution.py:381
  14.8 5.1 %collective-permute-start.5 = (f32[8,128]{1,0:T(8,128)S(1)}, f32[8,128]{1,0:T(8,128)S(1)}, u32[]{:S(2)}, u32[]{:S(2)}) collective-permute-start(f32[8,128]{1,0:T(8,128)S(1)} %fusion.3.terms), channel_id=1, source_target_pairs={{0,4},{1,5},{2,6},{3,7},{4,0},{5,1},{6,2},{7,3},{8,12},{9,13},{10,... | collective-permute-start | bytes 12296 | tf_op jit(solution)/shard_map/ppermute | solution.py:381
  20.0 6.7 %collective-permute-start.6 = (f32[152,128]{1,0:T(8,128)S(1)}, f32[152,128]{1,0:T(8,128)S(1)}, u32[]{:S(2)}, u32[]{:S(2)}) collective-permute-start(f32[152,128]{1,0:T(8,128)S(1)} %get-tuple-element.83), channel_id=1, source_target_pairs={{8,16},{16,8},{24,32},{32,24},{40,48},{48,40},{56,64},{64,56},{72,... | collective-permute-start | bytes 233480 | tf_op jit(solution)/shard_map/ppermute | solution.py:381
  21.3 5.5 %collective-permute-start.7 = (f32[144,128]{1,0:T(8,128)S(1)}, f32[144,128]{1,0:T(8,128)S(1)}, u32[]{:S(2)}, u32[]{:S(2)}) collective-permute-start(f32[144,128]{1,0:T(8,128)S(1)} %get-tuple-element.58), channel_id=1, source_target_pairs={{0,8},{8,0},{16,24},{24,16},{32,40},{40,32},{48,56},{56,48},{64,72... | collective-permute-start | bytes 221192 | tf_op jit(solution)/shard_map/ppermute | solution.py:381
  22.1 4.7 %collective-permute-start.8 = (f32[128,128]{1,0:T(8,128)S(1)}, f32[128,128]{1,0:T(8,128)S(1)}, u32[]{:S(2)}, u32[]{:S(2)}) collective-permute-start(f32[128,128]{1,0:T(8,128)S(1)} %get-tuple-element.59), channel_id=1, source_target_pairs={{1,2},{2,1},{3,4},{4,3},{5,6},{6,5},{7,0},{0,7},{9,10},{10,9},{11,... | collective-permute-start | bytes 196616 | tf_op jit(solution)/shard_map/ppermute | solution.py:381
  23.8 3.0 %collective-permute-start.9 = (f32[128,128]{1,0:T(8,128)S(1)}, f32[128,128]{1,0:T(8,128)S(1)}, u32[]{:S(2)}, u32[]{:S(2)}) collective-permute-start(f32[128,128]{1,0:T(8,128)S(1)} %get-tuple-element.60), channel_id=1, source_target_pairs={{0,1},{1,0},{2,3},{3,2},{4,5},{5,4},{6,7},{7,6},{8,9},{9,8},{10,11... | collective-permute-start | bytes 196616 | tf_op jit(solution)/shard_map/ppermute | solution.py:381
  26.7 3.6 %collective-permute-start.14 = (f32[40,128]{1,0:T(8,128)S(1)}, f32[40,128]{1,0:T(8,128)S(1)}, u32[]{:S(2)}, u32[]{:S(2)}) collective-permute-start(f32[40,128]{1,0:T(8,128)S(1)} %concatenate.3), channel_id=1, source_target_pairs={{0,64},{8,72},{16,80},{24,88},{32,96},{40,104},{48,112},{56,120},{... | collective-permute-start | bytes 61448 | tf_op jit(solution)/shard_map/ppermute | solution.py:381
  26.8 5.8 %collective-permute-start.10 = (f32[32,128]{1,0:T(8,128)S(1)}, f32[32,128]{1,0:T(8,128)S(1)}, u32[]{:S(2)}, u32[]{:S(2)}) collective-permute-start(f32[32,128]{1,0:T(8,128)S(1)} %get-tuple-element.64), channel_id=1, source_target_pairs={{1,2},{2,1},{3,4},{4,3},{5,6},{6,5},{7,0},{0,7},{9,10},{10,9},{11,... | collective-permute-start | bytes 49160 | tf_op jit(solution)/shard_map/ppermute | solution.py:381
  30.0 2.6 %collective-permute-start.11 = (f32[32,128]{1,0:T(8,128)S(1)}, f32[32,128]{1,0:T(8,128)S(1)}, u32[]{:S(2)}, u32[]{:S(2)}) collective-permute-start(f32[32,128]{1,0:T(8,128)S(1)} %get-tuple-element.65), channel_id=1, source_target_pairs={{0,1},{1,0},{2,3},{3,2},{4,5},{5,4},{6,7},{7,6},{8,9},{9,8},{10,11... | collective-permute-start | bytes 49160 | tf_op jit(solution)/shard_map/ppermute | solution.py:381
  30.4 4.6 %collective-permute-start.15 = (f32[8,128]{1,0:T(8,128)S(1)}, f32[8,128]{1,0:T(8,128)S(1)}, u32[]{:S(2)}, u32[]{:S(2)}) collective-permute-start(f32[8,128]{1,0:T(8,128)S(1)} %fusion), channel_id=1, source_target_pairs={{64,128},{72,136},{80,144},{88,152},{96,160},{104,168},{112,176},{... | collective-permute-start | bytes 12296 | tf_op jit(solution)/shard_map/ppermute | solution.py:381
  35.0 7.1 %collective-permute-start.16 = (f32[72,128]{1,0:T(8,128)S(1)}, f32[72,128]{1,0:T(8,128)S(1)}, u32[]{:S(2)}, u32[]{:S(2)}) collective-permute-start(f32[72,128]{1,0:T(8,128)S(1)} %constant_dynamic-update-slice_fusion), channel_id=1, source_target_pairs={{1,2},{2,1},{3,4},{4,3},{5,6},{6,5},{7,0},{0,7},{9,10},{10,9},{11,... | collective-permute-start | bytes 110600 | tf_op jit(solution)/shard_map/ppermute | solution.py:381
  40.4 6.4 %collective-permute-start.12 = (f32[64,128]{1,0:T(8,128)S(1)}, f32[64,128]{1,0:T(8,128)S(1)}, u32[]{:S(2)}, u32[]{:S(2)}) collective-permute-start(f32[64,128]{1,0:T(8,128)S(1)} %get-tuple-element.76), channel_id=1, source_target_pairs={{8,16},{16,8},{24,32},{32,24},{40,48},{48,40},{56,64},{64,56},{72,... | collective-permute-start | bytes 98312 | tf_op jit(solution)/shard_map/ppermute | solution.py:381
  41.2 5.6 %collective-permute-start.13 = (f32[64,128]{1,0:T(8,128)S(1)}, f32[64,128]{1,0:T(8,128)S(1)}, u32[]{:S(2)}, u32[]{:S(2)}) collective-permute-start(f32[64,128]{1,0:T(8,128)S(1)} %get-tuple-element.77), channel_id=1, source_target_pairs={{0,8},{8,0},{16,24},{24,16},{32,40},{40,32},{48,56},{56,48},{64,72... | collective-permute-start | bytes 98312 | tf_op jit(solution)/shard_map/ppermute | solution.py:381
  41.2 5.6 %collective-permute-start.17 = (f32[64,128]{1,0:T(8,128)S(1)}, f32[64,128]{1,0:T(8,128)S(1)}, u32[]{:S(2)}, u32[]{:S(2)}) collective-permute-start(f32[64,128]{1,0:T(8,128)S(1)} %get-tuple-element.79), channel_id=1, source_target_pairs={{0,1},{1,0},{2,3},{3,2},{4,5},{5,4},{6,7},{7,6},{8,9},{9,8},{10,11... | collective-permute-start | bytes 98312 | tf_op jit(solution)/shard_map/ppermute | solution.py:381
  42.1 4.8 %collective-permute-start.18 = (f32[8,128]{1,0:T(8,128)S(1)}, f32[8,128]{1,0:T(8,128)S(1)}, u32[]{:S(2)}, u32[]{:S(2)}) collective-permute-start(f32[8,128]{1,0:T(8,128)S(1)} %slice_add_fusion.terms), channel_id=1, source_target_pairs={{0,32},{8,40},{16,48},{24,56},{32,0},{40,8},{48,16},{56,24},{64,96... | collective-permute-start | bytes 12296 | tf_op jit(solution)/shard_map/ppermute | solution.py:381

commit v9 on v8

--- a/solution.py
+++ b/solution.py
@@ -407,7 +407,7 @@
     work, ylow, yhigh, inverse, terms = call(
         own_kernel, inner_rows + (1040, 8), (128, 104), w, basis, eigen, terms, flops=20000000
     )
-    terms = terms + axe[128:] + jnp.where(is_top, aze[128:] + across, 0.0)
+    terms = terms + axe[128:] + jnp.where(is_top, across + aze[128:], 0.0)
     beside = move(terms, "coarse", swap(coarses, 4, 0))
     zo, ze, xo, xe, r, z_face, x_face = call(
         pass_kernel, (LINK + 8, LINK, 128, 128, 512, 128, 128), (FACE,) * 4 + inner_rows + (128,),
@@ -418,10 +418,10 @@
     ze, xe, xo = move(ze, "dom", z_even), move(xe, "coarse", x_even), move(xo, "coarse", x_odd)
     terms = terms + jnp.where(is_top, zo[LINK:], 0.0)
     wide = jnp.concatenate([terms, jnp.zeros((32, 128), F32)])
-    terms = terms + jnp.where(is_top, move(wide, "dom", swap(doms, 8, 0))[:8], 0.0)
+    terms = terms + jnp.where(is_top, move(wide, "dom", swap(doms, 4, 0))[:8], 0.0)
     ro, re = call(relay_kernel, (RELAY, RELAY), (), zo, ze, xo, xe, flops=1000)
     re, ro = move(re, "coarse", x_even), move(ro, "coarse", x_odd)
-    beside = move(terms, "dom", swap(doms, 8, 1))
+    beside = move(terms, "dom", swap(doms, 8, 0))
     first, work, ylow, yhigh = call(
         second_own_kernel, (512,) + inner_rows, (512, 128), w, c2, r, zo, ze, xo, xe, basis, flops=1000
     )
@@ -433,7 +433,7 @@
     xo = move(lax.dynamic_update_slice(do, terms, (FACE, 0)), "coarse", x_odd)
     zo, ze, xe = move(co, "dom", z_odd), move(ce, "dom", z_even), move(de, "coarse", x_even)
     terms = terms + xo[FACE:]
-    beside = move(terms, "dom", swap(doms, 4, 0))
+    beside = move(terms, "dom", swap(doms, 8, 1))
     inner, base = call(inner_kernel, (512, 128), (128,), first, work, ylow, yhigh, basis, own_part, own, flops=1000)
     (gathered,) = call(gather_kernel, (512,), (), inner, base, zo, ze, xo, xe, terms, coarse_map, group, top, flops=1000)
     (out,) = call(last_kernel, (512,), (), gathered, beside, coarse_map, top, flops=1000)

time: 47.9 us -> 45.8 us (0.956)
  starting transfers between devices: 30.8 us -> 28.4 us
    ppermute x19, starting transfers between devices: 30.8 us -> 28.4 us  [move(): return lax.ppermute(value, axis, pairs)]
where the time goes in v9:
time: 45.8 us; the launch traced here: 45.7 us
  starting transfers between devices  28.4 us (62%)
  waiting for transfers between devices  8.88 us (19%)
  Pallas kernels  7.87 us (17%)
    ppermute x19, starting transfers between devices, move(): return lax.ppermute(value, axis, pairs)  28.4 us
    ppermute x19, waiting for transfers between devices, move(): return lax.ppermute(value, axis, pairs)  8.88 us
    pallas_call x9, Pallas kernels, call(): pl.pallas_call(kernel, out_shape=outs, in_specs=specs, out_specs=[VMEM] *...  7.87 us
  transfers between devices with their start and end apart: 19, of which 5 were waited for; matrix products, arithmetic and copies ran while one was open for 1% of the time, Pallas kernels for 12%

profile of v9, /device:TPU:1, one launch (start us, length us, event | category | flops | bytes accessed | tf_op | source)
XLA Modules:
  0.0 45.7 jit_solution(16861078112682807067)
XLA Ops:
  0.0 0.0 copy-start
  0.0 1.5 %shard_map.91 = (f32[128,128]{1,0:T(8,128)S(1)}, f32[136,128]{1,0:T(8,128)S(1)}, f32[136,128]{1,0:T(8,128)S(1)}, f32[128,128]{1,0:T(8,128)S(1)}, f32[512,128]{1,...) custom-call(f32[512,128]{1,0:T(8,128)} %bitcast.18, ...), custom_call_target="tpu_custom_call" | custom-call | flops 300000 | bytes 1000000 | tf_op jit(solution)/shard_map/pallas_call | solution.py:43
  1.5 0.0 copy-start.1
  1.5 8.7 %collective-permute-start = (f32[128,128]{1,0:T(8,128)S(1)}, f32[128,128]{1,0:T(8,128)S(1)}, u32[]{:S(2)}, u32[]{:S(2)}) collective-permute-start(f32[128,128]{1,0:T(8,128)S(1)} %get-tuple-element.46), channel_id=1, source_target_pairs={{8,16},{16,8},{24,32},{32,24},{40,48},{48,40},{56,64},{64,56},{72,... | collective-permute-start | bytes 196616 | tf_op jit(solution)/shard_map/ppermute | solution.py:381
  10.2 0.0 collective-permute-start.2
  10.2 2.3 %collective-permute-start.3 = (f32[136,128]{1,0:T(8,128)S(1)}, f32[136,128]{1,0:T(8,128)S(1)}, u32[]{:S(2)}, u32[]{:S(2)}) collective-permute-start(f32[136,128]{1,0:T(8,128)S(1)} %get-tuple-element.50), channel_id=1, source_target_pairs={{0,8},{8,0},{16,24},{24,16},{32,40},{40,32},{48,56},{56,48},{64,72... | collective-permute-start | bytes 208904 | tf_op jit(solution)/shard_map/ppermute | solution.py:381
  12.5 0.0 collective-permute-start.1
  12.5 1.7 %collective-permute-start.4 = (f32[128,128]{1,0:T(8,128)S(1)}, f32[128,128]{1,0:T(8,128)S(1)}, u32[]{:S(2)}, u32[]{:S(2)}) collective-permute-start(f32[128,128]{1,0:T(8,128)S(1)} %get-tuple-element.51), channel_id=1, source_target_pairs={{1,2},{2,1},{3,4},{4,3},{5,6},{6,5},{7,0},{0,7},{9,10},{10,9},{11,... | collective-permute-start | bytes 196616 | tf_op jit(solution)/shard_map/ppermute | solution.py:381
  14.2 0.0 copy-done
  14.2 0.0 copy-done.1
  14.2 0.5 %shard_map.92 = (f32[840,128]{1,0:T(8,128)S(1)}, f32[160,128]{1,0:T(8,128)S(1)}, f32[160,128]{1,0:T(8,128)S(1)}, f32[1040,128]{1,0:T(8,128)S(1)}, f32[8,128]{1,0:T(8,128)S(1)}) custom-call(f32[512,128]{1,0:T(8,128)S(1)} %get-tuple-element.44.w, f32[300,1,128]{2,1,0:T(1,128)S(1)} %bitcast.12, f32[30,1,128]{2,1,0:T(1,128)S(1)} %bitcast.17, ...), custom_call_target="tpu_custom_call" | custom-call | flops 20000000 | bytes 1000000 | tf_op jit(solution)/shard_map/pallas_call | solution.py:43
  14.7 0.0 collective-permute-done.2
  14.7 0.0 collective-permute-done.3.aze
  14.8 0.0 collective-permute-done.1.axe
  14.8 0.1 fusion.3.terms
  14.8 2.9 %collective-permute-start.5 = (f32[8,128]{1,0:T(8,128)S(1)}, f32[8,128]{1,0:T(8,128)S(1)}, u32[]{:S(2)}, u32[]{:S(2)}) collective-permute-start(f32[8,128]{1,0:T(8,128)S(1)} %fusion.3.terms), channel_id=1, source_target_pairs={{0,4},{1,5},{2,6},{3,7},{4,0},{5,1},{6,2},{7,3},{8,12},{9,13},{10,... | collective-permute-start | bytes 12296 | tf_op jit(solution)/shard_map/ppermute | solution.py:381
  17.8 0.0 collective-permute-done.azo
  17.8 0.0 collective-permute-done.4.axo
  17.8 2.2 %shard_map.93 = (f32[152,128]{1,0:T(8,128)S(1)}, f32[144,128]{1,0:T(8,128)S(1)}, f32[128,128]{1,0:T(8,128)S(1)}, f32[128,128]{1,0:T(8,128)S(1)}, f32[512,128]{1,...) custom-call(f32[128,128]{1,0:T(8,128)S(1)} %collective-permute-done.azo, f32[8,128]{1,0:T(8,128)S(1)} %fusion.3.terms, ...), custom_call_target="tpu_custom_call" | custom-call | flops 15360000 | bytes 1000000 | tf_op jit(solution)/shard_map/pallas_call | solution.py:43
  20.0 0.0 collective-permute-done.5
  20.0 1.3 %collective-permute-start.6 = (f32[152,128]{1,0:T(8,128)S(1)}, f32[152,128]{1,0:T(8,128)S(1)}, u32[]{:S(2)}, u32[]{:S(2)}) collective-permute-start(f32[152,128]{1,0:T(8,128)S(1)} %get-tuple-element.83), channel_id=1, source_target_pairs={{8,16},{16,8},{24,32},{32,24},{40,48},{48,40},{56,64},{64,56},{72,... | collective-permute-start | bytes 233480 | tf_op jit(solution)/shard_map/ppermute | solution.py:381
  21.3 0.8 %collective-permute-start.7 = (f32[144,128]{1,0:T(8,128)S(1)}, f32[144,128]{1,0:T(8,128)S(1)}, u32[]{:S(2)}, u32[]{:S(2)}) collective-permute-start(f32[144,128]{1,0:T(8,128)S(1)} %get-tuple-element.58), channel_id=1, source_target_pairs={{0,8},{8,0},{16,24},{24,16},{32,40},{40,32},{48,56},{56,48},{64,72... | collective-permute-start | bytes 221192 | tf_op jit(solution)/shard_map/ppermute | solution.py:381
  22.1 1.7 %collective-permute-start.8 = (f32[128,128]{1,0:T(8,128)S(1)}, f32[128,128]{1,0:T(8,128)S(1)}, u32[]{:S(2)}, u32[]{:S(2)}) collective-permute-start(f32[128,128]{1,0:T(8,128)S(1)} %get-tuple-element.59), channel_id=1, source_target_pairs={{1,2},{2,1},{3,4},{4,3},{5,6},{6,5},{7,0},{0,7},{9,10},{10,9},{11,... | collective-permute-start | bytes 196616 | tf_op jit(solution)/shard_map/ppermute | solution.py:381
  23.8 0.1 collective-permute-start.9
  23.9 2.8 %collective-permute-done.6.zo = f32[152,128]{1,0:T(8,128)S(1)} collective-permute-done((f32[152,128]{1,0:T(8,128)S(1)}, f32[152,128]{1,0:T(8,128)S(1)}, u32[]{:S(2)}, u32[]{:S(2)}) %collective-permute-start.6) | collective-permute-done | bytes 77856 | tf_op jit(solution)/shard_map/ppermute | solution.py:381
  26.7 0.1 fusion.1
  26.7 0.0 collective-permute-start.14
  26.8 0.0 collective-permute-done.8.xo
  26.8 0.0 collective-permute-done.9.xe
  26.8 0.0 collective-permute-done.7.ze
  26.8 3.2 %collective-permute-start.10 = (f32[32,128]{1,0:T(8,128)S(1)}, f32[32,128]{1,0:T(8,128)S(1)}, u32[]{:S(2)}, u32[]{:S(2)}) collective-permute-start(f32[32,128]{1,0:T(8,128)S(1)} %get-tuple-element.64), channel_id=1, source_target_pairs={{1,2},{2,1},{3,4},{4,3},{5,6},{6,5},{7,0},{0,7},{9,10},{10,9},{11,... | collective-permute-start | bytes 49160 | tf_op jit(solution)/shard_map/ppermute | solution.py:381
  30.0 0.0 collective-permute-start.11
  30.1 0.0 collective-permute-done.14
  30.1 0.1 fusion
  30.1 0.0 collective-permute-start.15
  30.2 0.5 %shard_map.94 = (f32[512,128]{1,0:T(8,128)S(1)}, f32[840,128]{1,0:T(8,128)S(1)}, f32[160,128]{1,0:T(8,128)S(1)}, f32[160,128]{1,0:T(8,128)S(1)}) custom-call(f32[512,128]{1,0:T(8,128)S(1)} %get-tuple-element.44.w, f32[512,128]{1,0:T(8,128)S(1)} %get-tuple-element.45.c2, f32[512,128]{1,0:T(8,128)S(1)} %get-tuple-element.56.r, ...), custom_call_target="tpu_custom_call" | custom-call | flops 1000 | bytes 1000000 | tf_op jit(solution)/shard_map/pallas_call | solution.py:43
  30.6 0.8 %collective-permute-done.10.ro = f32[32,128]{1,0:T(8,128)S(1)} collective-permute-done((f32[32,128]{1,0:T(8,128)S(1)}, f32[32,128]{1,0:T(8,128)S(1)}, u32[]{:S(2)}, u32[]{:S(2)}) %collective-permute-start.10) | collective-permute-done | bytes 16416 | tf_op jit(solution)/shard_map/ppermute | solution.py:381
  31.5 0.0 collective-permute-done.11.re
  31.5 1.8 %shard_map.96 = (f32[64,128]{1,0:T(8,128)S(1)}, f32[64,128]{1,0:T(8,128)S(1)}, f32[72,128]{1,0:T(8,128)S(1)}, f32[64,128]{1,0:T(8,128)S(1)}, f32[840,128]{1,0:T(...) custom-call(f32[128,128]{1,0:T(8,128)S(1)} %collective-permute-done.azo, ...), custom_call_target="tpu_custom_call" | custom-call | flops 15360000 | bytes 1000000 | tf_op jit(solution)/shard_map/pallas_call | solution.py:43
  33.3 0.2 collective-permute-done.15
  33.5 0.1 constant_dynamic-update-slice_fusion
  33.6 4.7 %collective-permute-start.16 = (f32[72,128]{1,0:T(8,128)S(1)}, f32[72,128]{1,0:T(8,128)S(1)}, u32[]{:S(2)}, u32[]{:S(2)}) collective-permute-start(f32[72,128]{1,0:T(8,128)S(1)} %constant_dynamic-update-slice_fusion), channel_id=1, source_target_pairs={{1,2},{2,1},{3,4},{4,3},{5,6},{6,5},{7,0},{0,7},{9,10},{10,9},{11,... | collective-permute-start | bytes 110600 | tf_op jit(solution)/shard_map/ppermute | solution.py:381
  38.3 0.8 %collective-permute-start.12 = (f32[64,128]{1,0:T(8,128)S(1)}, f32[64,128]{1,0:T(8,128)S(1)}, u32[]{:S(2)}, u32[]{:S(2)}) collective-permute-start(f32[64,128]{1,0:T(8,128)S(1)} %get-tuple-element.76), channel_id=1, source_target_pairs={{8,16},{16,8},{24,32},{32,24},{40,48},{48,40},{56,64},{64,56},{72,... | collective-permute-start | bytes 98312 | tf_op jit(solution)/shard_map/ppermute | solution.py:381
  39.1 0.0 collective-permute-start.13
  39.1 0.1 collective-permute-start.17
  39.2 0.8 %collective-permute-done.16.xo = f32[72,128]{1,0:T(8,128)S(1)} collective-permute-done((f32[72,128]{1,0:T(8,128)S(1)}, f32[72,128]{1,0:T(8,128)S(1)}, u32[]{:S(2)}, u32[]{:S(2)}) %collective-permute-start.16) | collective-permute-done | bytes 36896 | tf_op jit(solution)/shard_map/ppermute | solution.py:381
  40.0 0.1 slice_add_fusion.terms
  40.0 0.0 collective-permute-start.18
  40.0 0.4 shard_map.97
  40.5 4.2 %collective-permute-done.12.zo = f32[64,128]{1,0:T(8,128)S(1)} collective-permute-done((f32[64,128]{1,0:T(8,128)S(1)}, f32[64,128]{1,0:T(8,128)S(1)}, u32[]{:S(2)}, u32[]{:S(2)}) %collective-permute-start.12) | collective-permute-done | bytes 32800 | tf_op jit(solution)/shard_map/ppermute | solution.py:381
  44.7 0.0 collective-permute-done.13.ze
  44.7 0.0 collective-permute-done.17.xe
  44.7 0.1 shard_map.98.gathered
  44.8 0.0 collective-permute-done.18.beside
  44.9 0.8 %shard_map.99 = f32[512,128]{1,0:T(8,128)} custom-call(f32[512,128]{1,0:T(8,128)S(1)} %shard_map.98.gathered, f32[8,128]{1,0:T(8,128)S(1)} %collective-permute-done.18.beside, s32[1,128]{1,0:T(1,128)S(1)} %get-tuple-element.80.coarse_map, f32[128,512]{1,0:T(8,128)S(1)} %get-tuple-element.82.top), custom_call_target="tpu_custom_call" | custom-call | flops 1000 | bytes 1000000 | tf_op jit(solution)/shard_map/pallas_call | solution.py:43
  (4 shorter events, 0.0 us)
Async XLA Ops:
  0.0 14.2 %copy-start = (f32[3,10,10,1,1,128]{5,4,3,2,1,0:T(1,128)S(1)}, f32[3,10,10,1,1,128]{5,4,3,2,1,0:T(1,128)}, u32[]{:S(2)}) copy-start(f32[3,10,10,1,1,128]{5,4,3,2,1,0:T(1,128)} %param.12) | copy-start | bytes 460804
  1.5 12.7 %copy-start.1 = (f32[3,10,1,1,128]{4,3,2,1,0:T(1,128)S(1)}, f32[3,10,1,1,128]{4,3,2,1,0:T(1,128)}, u32[]{:S(2)}) copy-start(f32[3,10,1,1,128]{4,3,2,1,0:T(1,128)} %param.13) | copy-start | bytes 46084
  1.5 16.3 %collective-permute-start = (f32[128,128]{1,0:T(8,128)S(1)}, f32[128,128]{1,0:T(8,128)S(1)}, u32[]{:S(2)}, u32[]{:S(2)}) collective-permute-start(f32[128,128]{1,0:T(8,128)S(1)} %get-tuple-element.46), channel_id=1, source_target_pairs={{8,16},{16,8},{24,32},{32,24},{40,48},{48,40},{56,64},{64,56},{72,... | collective-permute-start | bytes 196616 | tf_op jit(solution)/shard_map/ppermute | solution.py:381
  10.2 4.5 %collective-permute-start.2 = (f32[8,128]{1,0:T(8,128)S(1)}, f32[8,128]{1,0:T(8,128)S(1)}, u32[]{:S(2)}, u32[]{:S(2)}) collective-permute-start(f32[8,128]{1,0:T(8,128)S(1)} %get-tuple-element.47.terms), channel_id=1, source_target_pairs={{0,9},{1,8},{2,11},{3,10},{4,13},{5,12},{6,15},{7,14},{8,1},{9,0},... | collective-permute-start | bytes 12296 | tf_op jit(solution)/shard_map/ppermute | solution.py:381
  10.2 4.6 %collective-permute-start.3 = (f32[136,128]{1,0:T(8,128)S(1)}, f32[136,128]{1,0:T(8,128)S(1)}, u32[]{:S(2)}, u32[]{:S(2)}) collective-permute-start(f32[136,128]{1,0:T(8,128)S(1)} %get-tuple-element.50), channel_id=1, source_target_pairs={{0,8},{8,0},{16,24},{24,16},{32,40},{40,32},{48,56},{56,48},{64,72... | collective-permute-start | bytes 208904 | tf_op jit(solution)/shard_map/ppermute | solution.py:381
  12.5 2.3 %collective-permute-start.1 = (f32[136,128]{1,0:T(8,128)S(1)}, f32[136,128]{1,0:T(8,128)S(1)}, u32[]{:S(2)}, u32[]{:S(2)}) collective-permute-start(f32[136,128]{1,0:T(8,128)S(1)} %get-tuple-element.49), channel_id=1, source_target_pairs={{0,1},{1,0},{2,3},{3,2},{4,5},{5,4},{6,7},{7,6},{8,9},{9,8},{10,11... | collective-permute-start | bytes 208904 | tf_op jit(solution)/shard_map/ppermute | solution.py:381
  12.5 5.3 %collective-permute-start.4 = (f32[128,128]{1,0:T(8,128)S(1)}, f32[128,128]{1,0:T(8,128)S(1)}, u32[]{:S(2)}, u32[]{:S(2)}) collective-permute-start(f32[128,128]{1,0:T(8,128)S(1)} %get-tuple-element.51), channel_id=1, source_target_pairs={{1,2},{2,1},{3,4},{4,3},{5,6},{6,5},{7,0},{0,7},{9,10},{10,9},{11,... | collective-permute-start | bytes 196616 | tf_op jit(solution)/shard_map/ppermute | solution.py:381
  14.8 5.1 %collective-permute-start.5 = (f32[8,128]{1,0:T(8,128)S(1)}, f32[8,128]{1,0:T(8,128)S(1)}, u32[]{:S(2)}, u32[]{:S(2)}) collective-permute-start(f32[8,128]{1,0:T(8,128)S(1)} %fusion.3.terms), channel_id=1, source_target_pairs={{0,4},{1,5},{2,6},{3,7},{4,0},{5,1},{6,2},{7,3},{8,12},{9,13},{10,... | collective-permute-start | bytes 12296 | tf_op jit(solution)/shard_map/ppermute | solution.py:381
  20.0 6.7 %collective-permute-start.6 = (f32[152,128]{1,0:T(8,128)S(1)}, f32[152,128]{1,0:T(8,128)S(1)}, u32[]{:S(2)}, u32[]{:S(2)}) collective-permute-start(f32[152,128]{1,0:T(8,128)S(1)} %get-tuple-element.83), channel_id=1, source_target_pairs={{8,16},{16,8},{24,32},{32,24},{40,48},{48,40},{56,64},{64,56},{72,... | collective-permute-start | bytes 233480 | tf_op jit(solution)/shard_map/ppermute | solution.py:381
  21.3 5.5 %collective-permute-start.7 = (f32[144,128]{1,0:T(8,128)S(1)}, f32[144,128]{1,0:T(8,128)S(1)}, u32[]{:S(2)}, u32[]{:S(2)}) collective-permute-start(f32[144,128]{1,0:T(8,128)S(1)} %get-tuple-element.58), channel_id=1, source_target_pairs={{0,8},{8,0},{16,24},{24,16},{32,40},{40,32},{48,56},{56,48},{64,72... | collective-permute-start | bytes 221192 | tf_op jit(solution)/shard_map/ppermute | solution.py:381
  22.1 4.7 %collective-permute-start.8 = (f32[128,128]{1,0:T(8,128)S(1)}, f32[128,128]{1,0:T(8,128)S(1)}, u32[]{:S(2)}, u32[]{:S(2)}) collective-permute-start(f32[128,128]{1,0:T(8,128)S(1)} %get-tuple-element.59), channel_id=1, source_target_pairs={{1,2},{2,1},{3,4},{4,3},{5,6},{6,5},{7,0},{0,7},{9,10},{10,9},{11,... | collective-permute-start | bytes 196616 | tf_op jit(solution)/shard_map/ppermute | solution.py:381
  23.8 3.0 %collective-permute-start.9 = (f32[128,128]{1,0:T(8,128)S(1)}, f32[128,128]{1,0:T(8,128)S(1)}, u32[]{:S(2)}, u32[]{:S(2)}) collective-permute-start(f32[128,128]{1,0:T(8,128)S(1)} %get-tuple-element.60), channel_id=1, source_target_pairs={{0,1},{1,0},{2,3},{3,2},{4,5},{5,4},{6,7},{7,6},{8,9},{9,8},{10,11... | collective-permute-start | bytes 196616 | tf_op jit(solution)/shard_map/ppermute | solution.py:381
  26.7 3.3 %collective-permute-start.14 = (f32[40,128]{1,0:T(8,128)S(1)}, f32[40,128]{1,0:T(8,128)S(1)}, u32[]{:S(2)}, u32[]{:S(2)}) collective-permute-start(f32[40,128]{1,0:T(8,128)S(1)} %concatenate.3), channel_id=1, source_target_pairs={{0,32},{8,40},{16,48},{24,56},{32,0},{40,8},{48,16},{56,24},{64,96... | collective-permute-start | bytes 61448 | tf_op jit(solution)/shard_map/ppermute | solution.py:381
  26.8 4.6 %collective-permute-start.10 = (f32[32,128]{1,0:T(8,128)S(1)}, f32[32,128]{1,0:T(8,128)S(1)}, u32[]{:S(2)}, u32[]{:S(2)}) collective-permute-start(f32[32,128]{1,0:T(8,128)S(1)} %get-tuple-element.64), channel_id=1, source_target_pairs={{1,2},{2,1},{3,4},{4,3},{5,6},{6,5},{7,0},{0,7},{9,10},{10,9},{11,... | collective-permute-start | bytes 49160 | tf_op jit(solution)/shard_map/ppermute | solution.py:381
  30.0 1.4 %collective-permute-start.11 = (f32[32,128]{1,0:T(8,128)S(1)}, f32[32,128]{1,0:T(8,128)S(1)}, u32[]{:S(2)}, u32[]{:S(2)}) collective-permute-start(f32[32,128]{1,0:T(8,128)S(1)} %get-tuple-element.65), channel_id=1, source_target_pairs={{0,1},{1,0},{2,3},{3,2},{4,5},{5,4},{6,7},{7,6},{8,9},{9,8},{10,11... | collective-permute-start | bytes 49160 | tf_op jit(solution)/shard_map/ppermute | solution.py:381
  30.1 3.4 %collective-permute-start.15 = (f32[8,128]{1,0:T(8,128)S(1)}, f32[8,128]{1,0:T(8,128)S(1)}, u32[]{:S(2)}, u32[]{:S(2)}) collective-permute-start(f32[8,128]{1,0:T(8,128)S(1)} %fusion), channel_id=1, source_target_pairs={{0,64},{8,72},{16,80},{24,88},{32,96},{40,104},{48,112},{56,120},{... | collective-permute-start | bytes 12296 | tf_op jit(solution)/shard_map/ppermute | solution.py:381
  33.6 6.4 %collective-permute-start.16 = (f32[72,128]{1,0:T(8,128)S(1)}, f32[72,128]{1,0:T(8,128)S(1)}, u32[]{:S(2)}, u32[]{:S(2)}) collective-permute-start(f32[72,128]{1,0:T(8,128)S(1)} %constant_dynamic-update-slice_fusion), channel_id=1, source_target_pairs={{1,2},{2,1},{3,4},{4,3},{5,6},{6,5},{7,0},{0,7},{9,10},{10,9},{11,... | collective-permute-start | bytes 110600 | tf_op jit(solution)/shard_map/ppermute | solution.py:381
  38.3 6.4 %collective-permute-start.12 = (f32[64,128]{1,0:T(8,128)S(1)}, f32[64,128]{1,0:T(8,128)S(1)}, u32[]{:S(2)}, u32[]{:S(2)}) collective-permute-start(f32[64,128]{1,0:T(8,128)S(1)} %get-tuple-element.76), channel_id=1, source_target_pairs={{8,16},{16,8},{24,32},{32,24},{40,48},{48,40},{56,64},{64,56},{72,... | collective-permute-start | bytes 98312 | tf_op jit(solution)/shard_map/ppermute | solution.py:381
  39.1 5.6 %collective-permute-start.13 = (f32[64,128]{1,0:T(8,128)S(1)}, f32[64,128]{1,0:T(8,128)S(1)}, u32[]{:S(2)}, u32[]{:S(2)}) collective-permute-start(f32[64,128]{1,0:T(8,128)S(1)} %get-tuple-element.77), channel_id=1, source_target_pairs={{0,8},{8,0},{16,24},{24,16},{32,40},{40,32},{48,56},{56,48},{64,72... | collective-permute-start | bytes 98312 | tf_op jit(solution)/shard_map/ppermute | solution.py:381
  39.1 5.6 %collective-permute-start.17 = (f32[64,128]{1,0:T(8,128)S(1)}, f32[64,128]{1,0:T(8,128)S(1)}, u32[]{:S(2)}, u32[]{:S(2)}) collective-permute-start(f32[64,128]{1,0:T(8,128)S(1)} %get-tuple-element.79), channel_id=1, source_target_pairs={{0,1},{1,0},{2,3},{3,2},{4,5},{5,4},{6,7},{7,6},{8,9},{9,8},{10,11... | collective-permute-start | bytes 98312 | tf_op jit(solution)/shard_map/ppermute | solution.py:381
  40.0 4.8 %collective-permute-start.18 = (f32[8,128]{1,0:T(8,128)S(1)}, f32[8,128]{1,0:T(8,128)S(1)}, u32[]{:S(2)}, u32[]{:S(2)}) collective-permute-start(f32[8,128]{1,0:T(8,128)S(1)} %slice_add_fusion.terms), channel_id=1, source_target_pairs={{64,128},{72,136},{80,144},{88,152},{96,160},{104,168},{112,176},{... | collective-permute-start | bytes 12296 | tf_op jit(solution)/shard_map/ppermute | solution.py:381
